TPU v7x, 128 devices: a whole 4x4x4 slice. The times are simulated.
128 devices in a mesh: space: 32 (over x, z_hi, y), orb: 4 (over z_lo, core).
Axes of the slice: x: 4, y: 4, z: 4 (z_hi: 2, z_lo: 2; z = z_hi * 2 + z_lo), core: 2. Of those that a mesh axis runs over, the one named last changes fastest.
Arguments:
- orbitals: float32 [256, 16, 32, 512], P('space', None, None, 'orb'), may hold values from -75 to 75
- potential: float32 [256, 16, 32], P('space'), may hold values from -2 to 0
Outputs:
- whitened: float32 [256, 16, 32, 512], P('space', None, None, 'orb')
All inputs are finite; a program needn't handle non-finite values.
Results may differ from a plain program's by a relative error of at most 0.0003.
Values sent between devices are 32-bit elements; how exact they have to be, the bound alone decides.
No kernel may reach another device: no remote copies, remote signals or barrier semaphores. Data moves between devices by JAX's collectives and lax.ppermute only.
A program may use at most 192 MiB of HBM per device.

v0:
```python
import jax
import jax.numpy as jnp
from jax import lax
from jax.sharding import PartitionSpec as P

DEGREE = 4
NS_ITERS = 8


STENCIL_WEIGHTS = [-49.0 / 18.0, 3.0 / 2.0, -3.0 / 20.0, 1.0 / 90.0]
CENTER = 5.0
HALF_WIDTH = 4.0


def padded_2(cells, sides, width):
    for axis, dim in sides:
        count = lax.axis_size(axis)
        head = lax.slice_in_dim(cells, 0, width, axis=dim)
        tail = lax.slice_in_dim(cells, cells.shape[dim] - width, cells.shape[dim], axis=dim)
        cells = jnp.concatenate(
            [
                lax.ppermute(tail, axis, [(i, (i + 1) % count) for i in range(count)]),
                cells,
                lax.ppermute(head, axis, [((i + 1) % count, i) for i in range(count)]),
            ],
            axis=dim,
        )
    return cells


def slab_hamiltonian(field, potential):
    padded = padded_2(field, (("space", 0),), 3)
    planes = field.shape[0]
    laplace = 3.0 * STENCIL_WEIGHTS[0] * field
    for offset in range(1, 4):
        along_first = (
            padded[3 + offset : 3 + offset + planes] + padded[3 - offset : 3 - offset + planes]
        )
        along_second = jnp.roll(field, offset, 1) + jnp.roll(field, -offset, 1)
        along_third = jnp.roll(field, offset, 2) + jnp.roll(field, -offset, 2)
        laplace = laplace + STENCIL_WEIGHTS[offset] * (along_first + along_second + along_third)
    return -0.5 * laplace + potential[..., None] * field


def chebyshev(start, apply_operator):
    previous = start
    current = (apply_operator(start) - CENTER * start) / HALF_WIDTH
    for degree_step in range(2, DEGREE + 1):
        following = 2.0 * (apply_operator(current) - CENTER * current) / HALF_WIDTH - previous
        previous = current
        current = following
    return current


def whiten_factor(intersection):
    norm_scale = jnp.sqrt(jnp.sum(intersection * intersection) + 1e-06)
    identity = jnp.eye(intersection.shape[0], dtype=jnp.float32)
    scaled = intersection / norm_scale
    inverse = identity
    for step in range(NS_ITERS):
        factor = 1.5 * identity - 0.5 * jnp.dot(inverse, scaled, precision=lax.Precision.HIGHEST)
        scaled = jnp.dot(scaled, factor, precision=lax.Precision.HIGHEST)
        inverse = jnp.dot(factor, inverse, precision=lax.Precision.HIGHEST)
    return inverse / jnp.sqrt(norm_scale)


def body(orbitals, potential):
    local_orbs = orbitals.shape[-1]

    def slab_operator(field):
        return slab_hamiltonian(field, potential)

    filtered = chebyshev(orbitals, slab_operator)
    cell_rows = filtered.reshape(-1, local_orbs)
    total_cells = cell_rows.shape[0] * lax.axis_size("space")
    gathered = lax.all_gather(cell_rows, "orb", axis=1, tiled=True)
    partial_terms = jnp.dot(gathered.T, gathered, precision=lax.Precision.HIGHEST)
    intersection = lax.psum(partial_terms, "space") / total_cells
    root_inverse = whiten_factor(intersection)
    start = lax.axis_index("orb") * local_orbs
    own_columns = lax.dynamic_slice_in_dim(root_inverse, start, local_orbs, 1)
    whitened = jnp.dot(gathered, own_columns, precision=lax.Precision.HIGHEST)
    return whitened.reshape(filtered.shape)


def solution(mesh):
    return jax.shard_map(
        body,
        mesh=mesh,
        in_specs=(P("space", None, None, "orb"), P("space", None, None)),
        out_specs=P("space", None, None, "orb"),
        check_vma=False,
    )
```

profile of v0, /device:TPU:0, one launch (start us, length us, event | category | flops | bytes accessed | tf_op | source)
XLA Modules:
  0.0 686.0 jit_solution(7189807736035824030)
XLA Ops:
  10.0 7.0 %collective-permute-start = (f32[3,16,32,128]{3,2,1,0:T(8,128)S(1)}, f32[3,16,32,128]{3,2,1,0:T(8,128)S(1)}, u32[]{:S(2)}, u32[]{:S(2)}) collective-permute-start(f32[3,16,32,128]{3,2,1,0:T(8,128)S(1)} %get-tuple-element.101), channel_id=1, source_target_pairs={{4,0},{8,4},{12,8},{16,12},{20,16},{24,20},{28,24},{32,28},{36,32}... | collective-permute-start | bytes 2359304 | tf_op jit(solution)/shard_map/ppermute | solution.py:24
  17.9 1.8 fusion.135
  21.6 2.3 fusion.144
  27.6 6.8 collective-permute-done.1
  35.2 7.3 %broadcast_multiply_fusion = (f32[8,16,32,128]{3,2,1,0:T(8,128)S(1)}, f32[8,16,32,128]{3,2,1,0:T(8,128)S(1)}) fusion(f32[8,16,32,128]{3,2,1,0:T(8,128)S(1)} %copy-done, f32[8,16,32]{2,1,0:T(8,128)S(1)} %copy-done.1, f32[8,16,3,128]{3,2,1,0:T(4,128)S(1)} %get-tuple-element.110, f32[8,16,29,128]{3,2,1,0:T(8,128)S(1)} %get-tuple-element.112, ...), kind=kLoop, calls=%fused_computation.163 | loop fusion | flops 20971520 | bytes 44056576 | tf_op jit(solution)/shard_map/div | solution.py:47
  43.1 1.8 fusion.131
  45.0 2.4 fusion.127
  47.4 2.2 fusion.123
  50.3 7.0 %collective-permute-start.2 = (f32[3,16,32,128]{3,2,1,0:T(8,128)S(1)}, f32[3,16,32,128]{3,2,1,0:T(8,128)S(1)}, u32[]{:S(2)}, u32[]{:S(2)}) collective-permute-start(f32[3,16,32,128]{3,2,1,0:T(8,128)S(1)} %get-tuple-element.83), channel_id=1, source_target_pairs={{4,0},{8,4},{12,8},{16,12},{20,16},{24,20},{28,24},{32,28},{36,32}... | collective-permute-start | bytes 2359304 | tf_op jit(solution)/shard_map/ppermute | solution.py:24
  58.8 14.3 %collective-permute-done.2 = f32[3,16,32,128]{3,2,1,0:T(8,128)S(1)} collective-permute-done((f32[3,16,32,128]{3,2,1,0:T(8,128)S(1)}, f32[3,16,32,128]{3,2,1,0:T(8,128)S(1)}, u32[]{:S(2)}, u32[]{:S(2)}) %collective-permute-start.2) | collective-permute-done | bytes 786464 | tf_op jit(solution)/shard_map/ppermute | solution.py:24
  73.1 8.2 %collective-permute-done.3 = f32[3,16,32,128]{3,2,1,0:T(8,128)S(1)} collective-permute-done((f32[3,16,32,128]{3,2,1,0:T(8,128)S(1)}, f32[3,16,32,128]{3,2,1,0:T(8,128)S(1)}, u32[]{:S(2)}, u32[]{:S(2)}) %collective-permute-start.3) | collective-permute-done | bytes 786464 | tf_op jit(solution)/shard_map/ppermute | solution.py:22
  82.3 9.3 %fusion.51 = f32[8,16,32,128]{3,2,1,0:T(8,128)S(1)} fusion(f32[8,16,32,128]{3,2,1,0:T(8,128)S(1)} %copy-done, f32[8,16,32,128]{3,2,1,0:T(8,128)S(1)} %get-tuple-element.5, f32[3,16,32,128]{3,2,1,0:T(8,128)} %copy-done.6, f32[3,16,32,128]{3,2,1,0:T(8,128)} %copy-done.3, f32[8,15,32,128]{3,2,1,0:T(8,128)} %get-tuple-element.80, ...), kind=kLoop, calls=%fused_computation.83 | loop fusion | flops 24641536 | bytes 35143680 | tf_op jit(solution)/shard_map/sub | solution.py:49
  94.6 2.3 fusion.110
  104.4 13.2 %collective-permute-done.4 = f32[3,16,32,128]{3,2,1,0:T(8,128)S(1)} collective-permute-done((f32[3,16,32,128]{3,2,1,0:T(8,128)S(1)}, f32[3,16,32,128]{3,2,1,0:T(8,128)S(1)}, u32[]{:S(2)}, u32[]{:S(2)}) %collective-permute-start.4) | collective-permute-done | bytes 786464 | tf_op jit(solution)/shard_map/ppermute | solution.py:24
  117.6 6.0 collective-permute-done.5
  124.5 9.4 %fusion.31 = f32[8,16,32,128]{3,2,1,0:T(8,128)S(1)} fusion(f32[8,16,32,128]{3,2,1,0:T(8,128)S(1)} %fusion.51, f32[3,16,32,128]{3,2,1,0:T(8,128)} %copy-done.8, f32[3,16,32,128]{3,2,1,0:T(8,128)} %copy-done.5, f32[8,15,32,128]{3,2,1,0:T(8,128)S(1)} %get-tuple-element.54, f32[8,1,32,128]{3,2,1,0:T(8,128)} %get-tuple-element.56, ...), kind=kLoop, calls=%fused_computation.63 | loop fusion | flops 25165824 | bytes 33046528 | tf_op jit(solution)/shard_map/sub | solution.py:49
  135.6 2.3 fusion.97
  141.3 2.0 collective-permute-start.7
  145.3 11.8 %collective-permute-done.6 = f32[3,16,32,128]{3,2,1,0:T(8,128)S(1)} collective-permute-done((f32[3,16,32,128]{3,2,1,0:T(8,128)S(1)}, f32[3,16,32,128]{3,2,1,0:T(8,128)S(1)}, u32[]{:S(2)}, u32[]{:S(2)}) %collective-permute-start.6) | collective-permute-done | bytes 786464 | tf_op jit(solution)/shard_map/ppermute | solution.py:24
  157.0 6.8 collective-permute-done.7
  164.7 10.1 %fusion.11 = f32[8,16,32,128]{3,2,1,0:T(8,128)} fusion(f32[8,16,32,128]{3,2,1,0:T(8,128)S(1)} %fusion.51, f32[8,16,32,128]{3,2,1,0:T(8,128)S(1)} %fusion.31, f32[3,16,32,128]{3,2,1,0:T(8,128)} %copy-done.7, f32[3,16,32,128]{3,2,1,0:T(8,128)} %copy-done.4, f32[8,15,32,128]{3,2,1,0:T(8,128)S(1)} %get-tuple-element.28, f32[8,1,32,128]{3,2,1,0:T(8,128)} %get-tuple-element.30, ...), kind=kLoop, calls=%fused_computation.43 | loop fusion | flops 24641536 | bytes 33046528 | tf_op jit(solution)/shard_map/sub | solution.py:49
  174.8 74.3 %all-gather.2.cloned.1.call-done = f32[4096,512]{1,0:T(8,128)} async-done(((f32[4096,128]{1,0:T(8,128)}), f32[4096,512]{1,0:T(8,128)}) %all-gather.2.cloned.1.call-update) | async-done | bytes 8388624 | tf_op jit(solution)/shard_map/all_gather | solution.py:76
  249.2 18.4 %fusion.147 = f32[512,512]{1,0:T(8,128)} fusion(f32[4096,512]{1,0:T(8,128)} %all-gather.2.cloned.1.call-done), kind=kOutput, calls=%fused_computation.229 | convolution fusion | flops 12884901888 | bytes 9437184 | tf_op jit(solution)/shard_map/dot_general | solution.py:77
  267.6 355.0 %all-reduce.2.cloned.1.call-done = f32[512,512]{1,0:T(8,128)} async-done(((f32[512,512]{1,0:T(8,128)}), f32[512,512]{1,0:T(8,128)}) %all-reduce.2.cloned.1.call-update) | async-done | bytes 1048592 | tf_op jit(solution)/shard_map/psum | solution.py:78
  622.6 2.1 multiply_reduce_fusion
  625.4 2.3 select_subtract_fusion.7
  629.0 1.9 fusion.88
  630.9 1.8 select_subtract_fusion.6
  632.7 1.8 fusion.149
  634.6 1.8 fusion.148
  636.4 1.8 select_subtract_fusion.5
  638.3 2.1 fusion.151
  640.4 1.8 fusion.150
  642.2 1.9 select_subtract_fusion.4
  644.1 1.8 fusion.153
  645.9 1.8 fusion.152
  647.8 1.9 select_subtract_fusion.3
  649.6 1.8 fusion.155
  651.5 2.3 fusion.154
  653.8 1.9 select_subtract_fusion.2
  655.6 1.8 fusion.157
  657.5 1.8 fusion.156
  659.4 1.8 select_subtract_fusion.1
  661.2 1.8 fusion.159
  663.1 1.8 fusion.158
  665.0 2.0 select_subtract_fusion
  667.0 1.9 fusion.160
  668.9 10.1 %fusion.89 = f32[4096,128]{1,0:T(8,128)} fusion(f32[4096,512]{1,0:T(8,128)} %all-gather.2.cloned.1.call-done, f32[512,512]{1,0:T(8,128)S(1)} %fusion.160, s32[]{:T(128)S(6)} %select_n.3, f32[]{:T(128)S(6)} %sqrt.7), kind=kOutput, calls=%fused_computation.167 | convolution fusion | flops 3221291008 | bytes 10747912 | tf_op jit(solution)/shard_map/dot_general | solution.py:82
  (78 shorter events, 34.9 us)
Async XLA Ops:
  6.5 10.4 %copy-start = (f32[8,16,32,128]{3,2,1,0:T(8,128)S(1)}, f32[8,16,32,128]{3,2,1,0:T(8,128)}, u32[]{:S(2)}) copy-start(f32[8,16,32,128]{3,2,1,0:T(8,128)} %param.2) | copy-start | bytes 6291460
  6.5 242.6 %all-gather.2.cloned.1.call-start = ((), (), s32[]{:S(2)}) async-start(), calls=%async_computation | async-start | bytes 10485760 | tf_op jit(solution)/shard_map/all_gather | solution.py:76
  8.2 26.2 %collective-permute-start.1 = (f32[3,16,32,128]{3,2,1,0:T(8,128)S(1)}, f32[3,16,32,128]{3,2,1,0:T(8,128)S(1)}, u32[]{:S(2)}, u32[]{:S(2)}) collective-permute-start(f32[3,16,32,128]{3,2,1,0:T(8,128)S(1)} %get-tuple-element.102), channel_id=1, source_target_pairs={{0,4},{4,8},{8,12},{12,16},{16,20},{20,24},{24,28},{28,32},{32,36}... | collective-permute-start | bytes 2359304 | tf_op jit(solution)/shard_map/ppermute | solution.py:22
  10.0 25.1 %collective-permute-start = (f32[3,16,32,128]{3,2,1,0:T(8,128)S(1)}, f32[3,16,32,128]{3,2,1,0:T(8,128)S(1)}, u32[]{:S(2)}, u32[]{:S(2)}) collective-permute-start(f32[3,16,32,128]{3,2,1,0:T(8,128)S(1)} %get-tuple-element.101), channel_id=1, source_target_pairs={{4,0},{8,4},{12,8},{16,12},{20,16},{24,20},{28,24},{32,28},{36,32}... | collective-permute-start | bytes 2359304 | tf_op jit(solution)/shard_map/ppermute | solution.py:24
  23.9 3.1 copy-start.1
  50.3 22.9 %collective-permute-start.2 = (f32[3,16,32,128]{3,2,1,0:T(8,128)S(1)}, f32[3,16,32,128]{3,2,1,0:T(8,128)S(1)}, u32[]{:S(2)}, u32[]{:S(2)}) collective-permute-start(f32[3,16,32,128]{3,2,1,0:T(8,128)S(1)} %get-tuple-element.83), channel_id=1, source_target_pairs={{4,0},{8,4},{12,8},{16,12},{20,16},{24,20},{28,24},{32,28},{36,32}... | collective-permute-start | bytes 2359304 | tf_op jit(solution)/shard_map/ppermute | solution.py:24
  57.2 24.1 %collective-permute-start.3 = (f32[3,16,32,128]{3,2,1,0:T(8,128)S(1)}, f32[3,16,32,128]{3,2,1,0:T(8,128)S(1)}, u32[]{:S(2)}, u32[]{:S(2)}) collective-permute-start(f32[3,16,32,128]{3,2,1,0:T(8,128)S(1)} %get-tuple-element.84), channel_id=1, source_target_pairs={{0,4},{4,8},{8,12},{12,16},{16,20},{20,24},{24,28},{28,32},{32,36}... | collective-permute-start | bytes 2359304 | tf_op jit(solution)/shard_map/ppermute | solution.py:22
  73.1 8.2 %copy-start.3 = (f32[3,16,32,128]{3,2,1,0:T(8,128)}, f32[3,16,32,128]{3,2,1,0:T(8,128)S(1)}, u32[]{:S(2)}) copy-start(f32[3,16,32,128]{3,2,1,0:T(8,128)S(1)} %collective-permute-done.2) | copy-start | bytes 2359300
  81.3 1.0 copy-start.6
  100.4 17.2 %collective-permute-start.4 = (f32[3,16,32,128]{3,2,1,0:T(8,128)S(1)}, f32[3,16,32,128]{3,2,1,0:T(8,128)S(1)}, u32[]{:S(2)}, u32[]{:S(2)}) collective-permute-start(f32[3,16,32,128]{3,2,1,0:T(8,128)S(1)} %get-tuple-element.57), channel_id=1, source_target_pairs={{4,0},{8,4},{12,8},{16,12},{20,16},{24,20},{28,24},{32,28},{36,32}... | collective-permute-start | bytes 2359304 | tf_op jit(solution)/shard_map/ppermute | solution.py:24
  100.7 22.9 %collective-permute-start.5 = (f32[3,16,32,128]{3,2,1,0:T(8,128)S(1)}, f32[3,16,32,128]{3,2,1,0:T(8,128)S(1)}, u32[]{:S(2)}, u32[]{:S(2)}) collective-permute-start(f32[3,16,32,128]{3,2,1,0:T(8,128)S(1)} %get-tuple-element.58), channel_id=1, source_target_pairs={{0,4},{4,8},{8,12},{12,16},{16,20},{20,24},{24,28},{28,32},{32,36}... | collective-permute-start | bytes 2359304 | tf_op jit(solution)/shard_map/ppermute | solution.py:22
  117.6 6.0 copy-start.5
  123.6 0.9 copy-start.8
  140.7 16.3 %collective-permute-start.6 = (f32[3,16,32,128]{3,2,1,0:T(8,128)S(1)}, f32[3,16,32,128]{3,2,1,0:T(8,128)S(1)}, u32[]{:S(2)}, u32[]{:S(2)}) collective-permute-start(f32[3,16,32,128]{3,2,1,0:T(8,128)S(1)} %get-tuple-element.31), channel_id=1, source_target_pairs={{4,0},{8,4},{12,8},{16,12},{20,16},{24,20},{28,24},{32,28},{36,32}... | collective-permute-start | bytes 2359304 | tf_op jit(solution)/shard_map/ppermute | solution.py:24
  141.3 22.5 %collective-permute-start.7 = (f32[3,16,32,128]{3,2,1,0:T(8,128)S(1)}, f32[3,16,32,128]{3,2,1,0:T(8,128)S(1)}, u32[]{:S(2)}, u32[]{:S(2)}) collective-permute-start(f32[3,16,32,128]{3,2,1,0:T(8,128)S(1)} %get-tuple-element.32), channel_id=1, source_target_pairs={{0,4},{4,8},{8,12},{12,16},{16,20},{20,24},{24,28},{28,32},{32,36}... | collective-permute-start | bytes 2359304 | tf_op jit(solution)/shard_map/ppermute | solution.py:22
  157.0 6.8 copy-start.4
  163.8 0.9 copy-start.7
  174.8 447.8 %all-reduce.2.cloned.1.call-start = ((), (), s32[]{:S(2)}) async-start(), calls=%async_computation.1 | async-start | bytes 2097152 | tf_op jit(solution)/shard_map/psum | solution.py:78
  627.7 1.2 copy-start.2
Sparse Core Ops, SparseCore 0:
  174.9 74.2 all-gather.1
  267.8 354.8 all-reduce.1
where the time goes:
time: 692 us; the launch traced here: 686 us
  waiting for transfers between devices  496 us (72%)
  matrix products  71.5 us (10%)
  local copies, waits for them, and re-layouts  44.4 us (6%)
  other arithmetic  38.2 us (6%)
  starting transfers between devices  20.6 us (3%)
  between operations  14.9 us (2%)
    psum x1, waiting for transfers between devices, body(): intersection = lax.psum(partial_terms, 'space') / total_cells  355 us
    all_gather x1, waiting for transfers between devices, body(): gathered = lax.all_gather(cell_rows, 'orb', axis=1, tiled=True)  74.3 us
    ppermute x4, waiting for transfers between devices, padded_2(): lax.ppermute(head, axis, [((i + 1) % count, i) for i in range(count)])  39.3 us
    sub x3, other arithmetic, chebyshev(): 2.0 * (apply_operator(current) - CENTER * current) / HALF_WIDTH - previous  28.8 us
    ppermute x4, waiting for transfers between devices, padded_2(): lax.ppermute(tail, axis, [(i, (i + 1) % count) for i in range(count)])  27.8 us
    slice x24, local copies, waits for them, and re-layouts, slab_hamiltonian(): along_second = jnp.roll(field, offset, 1) + jnp.roll(field, -offset, 1)  25.3 us
    dot_general x1, matrix products, body(): jnp.dot(gathered.T, gathered, precision=lax.Precision.HIGHEST)  18.4 us
    dot_general x8, matrix products, whiten_factor(): jnp.dot(inverse, scaled, precision=lax.Precision.HIGHEST)  15.5 us
  transfers between devices with their start and end apart: 10, of which 9 were waited for; matrix products, arithmetic and copies ran while one was open for 2% of the time, Pallas kernels for 0%

commit v1 on v0

v1 whole, which is shorter than its diff:
```python
import numpy as np
import jax
import jax.numpy as jnp
from jax import lax
from jax.experimental import pallas as pl
from jax.experimental.pallas import tpu as pltpu
from jax.sharding import Mesh, PartitionSpec as P

DEGREE = 4
NS_ITERS = 8
NY, NZ = 16, 32
PLANE = NY * NZ
NX = 256
NORB = 512
SLAB = 8
SPACE = ("x", "zh", "y")
ORB = ("zl", "c")
EVERY = SPACE + ORB
F32 = jnp.float32
BF16 = jnp.bfloat16
VMEM = 56 * 1024 * 1024

STENCIL = (270.0, -27.0, 2.0)
UNIT = -0.5 / 180.0 / 4.0
DIAGONAL = (1.5 * 49.0 / 18.0 - 5.0) / 4.0


def plane_stencil():
    def ring(n):
        m = np.zeros((n, n), np.float32)
        for k, w in enumerate(STENCIL, 1):
            for i in range(n):
                m[i, (i + k) % n] += w
                m[i, (i - k) % n] += w
        return m

    return np.kron(ring(NY), np.eye(NZ, dtype=np.float32)) + np.kron(
        np.eye(NY, dtype=np.float32), ring(NZ)
    )


def low_rows(shape):
    return lax.broadcasted_iota(jnp.int32, shape, len(shape) - 2) < 4


def swap_halves(a):
    return pltpu.roll(a, 4, a.ndim - 2)


def split(a):
    hi = a.astype(BF16)
    return hi, (a - hi.astype(F32)).astype(BF16)


def dot(a, b):
    return jnp.dot(a, b, preferred_element_type=F32)


def dot3(a, b):
    return dot(a[0], b[0]) + (dot(a[0], b[1]) + dot(a[1], b[0]))


def spread_kernel(v_ref, pot_ref, out_ref):
    step = pl.program_id(0)

    @pl.when(step < 4)
    def _():
        a = v_ref[0].T.reshape(16, 8, PLANE)
        b = v_ref[1].T.reshape(16, 8, PLANE)
        low = low_rows(a.shape)
        out_ref[:, 0] = jnp.where(low, a, swap_halves(b))
        out_ref[:, 1] = jnp.where(low, swap_halves(a), b)

    @pl.when(step == 4)
    def _():
        out_ref[...] = jnp.broadcast_to(pot_ref[...], out_ref.shape)


def spread(field, potential):
    out = pl.pallas_call(
        spread_kernel,
        grid=(5,),
        in_specs=[
            pl.BlockSpec((2, PLANE, 128), lambda i: (jnp.minimum(i, 3), 0, 0)),
            pl.BlockSpec((SLAB, PLANE), lambda i: (0, 0)),
        ],
        out_specs=pl.BlockSpec((16, 2, 8, PLANE), lambda i: (0, 0, i, 0)),
        out_shape=jax.ShapeDtypeStruct((16, 2, 40, PLANE), F32),
        compiler_params=pltpu.CompilerParams(vmem_limit_bytes=VMEM),
        name="spread",
    )(field, potential)
    return out.reshape(32 * 40, PLANE)


ROWS = 4 * NX
EDGE = 16
CHUNK = 256


def filter_kernel(in_ref, ring_ref, out_ref, one_ref, two_ref, diag_ref):
    def fill(s, _):
        base = pl.multiple_of(s * 32, 32)
        one_ref[pl.ds(EDGE + base, 32), :] = in_ref[s, 0:32, :]
        pot = in_ref[s, 32:40, :]
        low = low_rows((8, PLANE))
        for t in range(4):
            row = jnp.where(low, pot[2 * t : 2 * t + 1], pot[2 * t + 1 : 2 * t + 2])
            diag_ref[pl.ds(base + 8 * t, 8), :] = 0.25 * row + DIAGONAL
        return 0

    lax.fori_loop(0, 32, fill, 0)
    ring = ring_ref[...]

    def close(ref):
        ref[0:EDGE, :] = ref[ROWS : ROWS + EDGE, :]
        ref[ROWS + EDGE :, :] = ref[EDGE : 2 * EDGE, :]

    def apply(cur_ref, base):
        wide = cur_ref[pl.ds(base, CHUNK + 2 * EDGE), :]
        cur = wide[EDGE : EDGE + CHUNK]
        hi, lo = split(cur)
        both = dot(jnp.concatenate([hi, lo], axis=0), ring)
        near = both[:CHUNK] + both[CHUNK:]
        half = pltpu.roll(wide, 4, 0)

        def at(a, shift):
            return a[EDGE + shift : EDGE + shift + CHUNK]

        along = (
            STENCIL[0] * (at(half, 0) + at(half, 8))
            + STENCIL[1] * (at(wide, 8) + at(wide, -8))
            + STENCIL[2] * (at(half, -8) + at(half, 16))
        )
        return UNIT * (near + along) + diag_ref[pl.ds(base, CHUNK), :] * cur, cur

    def sweep(body):
        def run(i, _):
            body(pl.multiple_of(i * CHUNK, CHUNK))
            return 0

        lax.fori_loop(0, ROWS // CHUNK, run, 0)

    close(one_ref)

    def first(base):
        value, _ = apply(one_ref, base)
        two_ref[pl.ds(EDGE + base, CHUNK), :] = value

    sweep(first)
    previous, current = one_ref, two_ref
    for degree_step in range(2, DEGREE + 1):
        close(current)
        last = degree_step == DEGREE

        def following(base, previous=previous, current=current, last=last):
            value, _ = apply(current, base)
            value = 2.0 * value - previous[pl.ds(EDGE + base, CHUNK), :]
            if last:
                out_ref[pl.ds(base, CHUNK), :] = value
            else:
                previous[pl.ds(EDGE + base, CHUNK), :] = value

        sweep(following)
        previous, current = current, previous


def chebyshev(spread_cells, ring):
    return pl.pallas_call(
        filter_kernel,
        out_shape=jax.ShapeDtypeStruct((ROWS, PLANE), F32),
        scratch_shapes=[
            pltpu.VMEM((ROWS + 2 * EDGE, PLANE), F32),
            pltpu.VMEM((ROWS + 2 * EDGE, PLANE), F32),
            pltpu.VMEM((ROWS, PLANE), F32),
        ],
        compiler_params=pltpu.CompilerParams(vmem_limit_bytes=VMEM),
        name="chebyshev",
    )(spread_cells.reshape(32, 40, PLANE), ring)


def gram_kernel(in_ref, hi_ref, lo_ref, gram_ref, cells_ref):
    for q in range(4):
        a = in_ref[:, 0, q]
        b = in_ref[:, 1, q]
        low = low_rows(a.shape)
        rows = pl.ds(128 * q, 128)
        cells_ref[rows, :PLANE] = jnp.where(low, a, swap_halves(b)).reshape(128, PLANE)
        cells_ref[rows, PLANE:] = jnp.where(low, swap_halves(a), b).reshape(128, PLANE)
    by_orbital = cells_ref[...]
    left = split(by_orbital)
    right = split(by_orbital.T)
    hi_ref[...] = right[0]
    lo_ref[...] = right[1]
    gram = dot3(left, right)
    for k in range(4):
        gram_ref[k] = gram[:, 128 * k : 128 * (k + 1)]


def gram(cells):
    return pl.pallas_call(
        gram_kernel,
        out_shape=(
            jax.ShapeDtypeStruct((2 * PLANE, NORB), BF16),
            jax.ShapeDtypeStruct((2 * PLANE, NORB), BF16),
            jax.ShapeDtypeStruct((4, NORB, 128), F32),
        ),
        scratch_shapes=[pltpu.VMEM((NORB, 2 * PLANE), F32)],
        compiler_params=pltpu.CompilerParams(vmem_limit_bytes=VMEM),
        name="gram",
    )(cells.reshape(16, 2, 4, 8, PLANE))


def whiten_kernel(gram_ref, hi_ref, lo_ref, out_ref):
    total = jnp.concatenate([gram_ref[k] for k in range(4)], axis=1)
    total = total * (1.0 / (NX * PLANE))
    square = jnp.sum(jnp.sum(total * total, axis=0, keepdims=True), axis=1, keepdims=True)
    norm_scale = jnp.sqrt(square + 1e-06)
    row = lax.broadcasted_iota(jnp.int32, (NORB, NORB), 0)
    col = lax.broadcasted_iota(jnp.int32, (NORB, NORB), 1)
    three_halves = jnp.where(row == col, 1.5, 0.0).astype(F32)
    scaled = total / norm_scale
    inverse = None
    for step in range(NS_ITERS):
        factor = three_halves - 0.5 * scaled
        parts = split(factor)
        inverse = factor if inverse is None else dot3(parts, split(inverse))
        if step < NS_ITERS - 1:
            scaled = dot3(split(dot3(split(scaled), parts)), parts)
    root = split(inverse / jnp.sqrt(norm_scale))
    white = dot3((hi_ref[...], lo_ref[...]), root)
    for k in range(4):
        out_ref[k] = white[:, 128 * k : 128 * (k + 1)]


def whiten(total, hi, lo):
    return pl.pallas_call(
        whiten_kernel,
        out_shape=jax.ShapeDtypeStruct((4, 2 * PLANE, 128), F32),
        compiler_params=pltpu.CompilerParams(vmem_limit_bytes=VMEM),
        name="whiten",
    )(total, hi, lo)


def exchange(a, axes):
    return lax.all_to_all(a, axes, 0, 0, tiled=True)


def body(orbitals, potential):
    ring = jnp.asarray(plane_stencil(), BF16)
    sent = spread(orbitals.reshape(SLAB, PLANE, 128), potential.reshape(SLAB, PLANE))
    filtered = chebyshev(exchange(sent, SPACE), ring)
    hi, lo, partial_terms = gram(exchange(filtered, EVERY))
    terms = exchange(partial_terms.reshape(4 * NORB, 128), EVERY)
    own = jnp.sum(terms.reshape(128, -1, 128), axis=0)
    total = exchange(jnp.tile(own, (128, 1)), EVERY).reshape(4, NORB, 128)
    whitened = exchange(whiten(total, hi, lo).reshape(8 * PLANE, 128), ORB)
    return whitened.reshape(orbitals.shape)


def solution(mesh):
    fine = Mesh(mesh.devices.reshape(4, 2, 4, 2, 2), EVERY)
    return jax.shard_map(
        body,
        mesh=fine,
        in_specs=(P(SPACE, None, None, ORB), P(SPACE, None, None)),
        out_specs=P(SPACE, None, None, ORB),
        check_vma=False,
    )
```

time: 692 us -> 208 us (0.30)
  waiting for transfers between devices: 496 us -> 0 us
  blocking collectives: 0 us -> 158 us
  matrix products: 71.5 us -> 0 us
  Pallas kernels: 0 us -> 45.1 us
  local copies, waits for them, and re-layouts: 44.4 us -> 2.92 us
  other arithmetic: 38.2 us -> 0.14 us
  starting transfers between devices: 20.6 us -> 0 us
  between operations: 14.9 us -> 0.02 us
    psum x1 -> x0, waiting for transfers between devices: 355 us -> none  [body(): intersection = lax.psum(partial_terms, 'space') / total_cells]
    all_to_all x0 -> x5, blocking collectives: none -> 158 us  [exchange(): return lax.all_to_all(a, axes, 0, 0, tiled=True)]
    all_gather x1 -> x0, waiting for transfers between devices: 74.3 us -> none  [body(): gathered = lax.all_gather(cell_rows, 'orb', axis=1, tiled=True)]
    dot_general x25 -> x0, matrix products: 71.5 us -> none  [the longest x1 18.4 us: body(): jnp.dot(gathered.T, gathered, precision=lax.Precision.HIGHEST)]
    ppermute x8 -> x0, waiting for transfers between devices: 67 us -> none  [the longest x4 39.3 us: padded_2(): lax.ppermute(head, axis, [((i + 1) % count, i) for i in range(count)])]
    pallas_call x0 -> x4, Pallas kernels: none -> 45.1 us  [the longest x1 22.6 us: whiten(): pl.pallas_call(whiten_kernel, out_shape=jax.ShapeDtypeStruct((4, 2 * PLAN...]
    slice x52 -> x0, local copies, waits for them, and re-layouts: 40.8 us -> none  [the longest x24 25.3 us: slab_hamiltonian(): along_second = jnp.roll(field, offset, 1) + jnp.roll(field, -offset, 1)]
    sub x3 -> x0, other arithmetic: 28.8 us -> none  [chebyshev(): 2.0 * (apply_operator(current) - CENTER * current) / HALF_WIDTH - previous]
  transfers between devices with their start and end apart: 10 -> 0, of which waited for: 9 -> 0; matrix products, arithmetic and copies ran while one was open for 2% -> 0% of each run, Pallas kernels for 0% -> 0%
where the time goes in v1:
time: 208 us; the launch traced here: 207 us
  blocking collectives  158 us (76%)
  Pallas kernels  45.1 us (22%)
  local copies, waits for them, and re-layouts  2.92 us (1%)
    all_to_all x5, blocking collectives, exchange(): return lax.all_to_all(a, axes, 0, 0, tiled=True)  158 us
    pallas_call x1, Pallas kernels, whiten(): pl.pallas_call(whiten_kernel, out_shape=jax.ShapeDtypeStruct((4, 2 * PLAN...  22.6 us
    pallas_call x1, Pallas kernels, chebyshev(): pl.pallas_call(filter_kernel, out_shape=jax.ShapeDtypeStruct((ROWS, PLANE...  13.2 us
    pallas_call x1, Pallas kernels, gram(): pl.pallas_call(gram_kernel, out_shape=(jax.ShapeDtypeStruct((2 * PLANE, N...  4.72 us
    pallas_call x1, Pallas kernels, spread(): pl.pallas_call(spread_kernel, grid=(5,), in_specs=[pl.BlockSpec((2, PLANE...  4.67 us

profile of v1, /device:TPU:0, one launch (start us, length us, event | category | flops | bytes accessed | tf_op | source)
XLA Modules:
  0.0 206.6 jit_solution(3832260987063523729)
XLA Ops:
  0.0 1.5 reshape.44.pot_ref
  1.5 4.7 %spread.1 = f32[16,2,40,512]{3,2,1,0:T(8,128)} custom-call(f32[8,512,128]{2,1,0:T(8,128)} %bitcast.12, f32[8,512]{1,0:T(8,128)} %reshape.44.pot_ref), custom_call_target="tpu_custom_call" | custom-call | tf_op jit(solution)/shard_map/spread/pallas_call | solution.py:80
  6.2 46.7 %all_to_all.39.in_ref = f32[32,40,512]{2,1,0:T(8,128)} all-to-all(f32[32,40,512]{2,1,0:T(8,128)} %bitcast.7), channel_id=1, replica_groups=mesh['x'=4,'zh'=2,'y'=4,'zl'=2,'c'=2] {'x','zh','y'}, dimensions={0} | all-to-all | bytes 5242880 | tf_op jit(solution)/shard_map/all_to_all | solution.py:245
  52.9 13.2 %chebyshev.1 = f32[1024,512]{1,0:T(8,128)} custom-call(f32[32,40,512]{2,1,0:T(8,128)} %all_to_all.39.in_ref, bf16[512,512]{1,0:T(8,128)(2,1)} %constant.4.clone.ring_ref), custom_call_target="tpu_custom_call" | custom-call | tf_op jit(solution)/shard_map/chebyshev/pallas_call | solution.py:168
  66.0 35.6 %all_to_all.40 = f32[128,8,512]{2,1,0:T(8,128)} all-to-all(f32[128,8,512]{2,1,0:T(8,128)} %bitcast.9), channel_id=1, replica_groups=mesh['x'=4,'zh'=2,'y'=4,'zl'=2,'c'=2] {'x','zh','y','zl','c'}, dimensions={0} | all-to-all | bytes 4194304 | tf_op jit(solution)/shard_map/all_to_all | solution.py:245
  101.6 4.7 %gram.1 = (bf16[1024,512]{1,0:T(8,128)(2,1)}, bf16[1024,512]{1,0:T(8,128)(2,1)}, f32[4,512,128]{2,1,0:T(8,128)}) custom-call(f32[16,2,4,8,512]{4,3,2,1,0:T(8,128)} %bitcast.8), custom_call_target="tpu_custom_call" | custom-call | tf_op jit(solution)/shard_map/gram/pallas_call | solution.py:200
  106.3 23.5 %all_to_all.41 = f32[128,16,128]{2,1,0:T(8,128)S(1)} all-to-all(f32[128,16,128]{2,1,0:T(8,128)} %bitcast.13), channel_id=1, replica_groups=mesh['x'=4,'zh'=2,'y'=4,'zl'=2,'c'=2] {'x','zh','y','zl','c'}, dimensions={0} | all-to-all | bytes 2097152 | tf_op jit(solution)/shard_map/all_to_all | solution.py:245
  129.9 0.1 reduce_sum.9
  130.0 0.1 tile.2
  130.1 23.3 %all_to_all.42 = f32[128,16,128]{2,1,0:T(8,128)} all-to-all(f32[128,16,128]{2,1,0:T(8,128)S(1)} %tile.2), channel_id=1, replica_groups=mesh['x'=4,'zh'=2,'y'=4,'zl'=2,'c'=2] {'x','zh','y','zl','c'}, dimensions={0} | all-to-all | bytes 2097152 | tf_op jit(solution)/shard_map/all_to_all | solution.py:245
  153.4 22.6 %whiten.1 = f32[4,1024,128]{2,1,0:T(8,128)} custom-call(f32[4,512,128]{2,1,0:T(8,128)} %bitcast.11, bf16[1024,512]{1,0:T(8,128)(2,1)} %get-tuple-element.9.hi_ref, bf16[1024,512]{1,0:T(8,128)(2,1)} %get-tuple-element.10.lo_ref), custom_call_target="tpu_custom_call" | custom-call | tf_op jit(solution)/shard_map/whiten/pallas_call | solution.py:236
  176.0 29.3 %all_to_all.43 = f32[4,1024,128]{2,1,0:T(8,128)S(1)} all-to-all(f32[4,1024,128]{2,1,0:T(8,128)} %whiten.1), channel_id=1, replica_groups=mesh['x'=4,'zh'=2,'y'=4,'zl'=2,'c'=2] {'zl','c'}, dimensions={0} | all-to-all | bytes 4194304 | tf_op jit(solution)/shard_map/all_to_all | solution.py:245
  205.3 1.3 copy.5

commit v2 on v1

--- a/solution.py
+++ b/solution.py
@@ -18,10 +18,11 @@
 EVERY = SPACE + ORB
 F32 = jnp.float32
 BF16 = jnp.bfloat16
-VMEM = 56 * 1024 * 1024
-
-STENCIL = (270.0, -27.0, 2.0)
-UNIT = -0.5 / 180.0 / 4.0
+VMEM = 30 * 1024 * 1024
+VMEM_SMALL = 24 * 1024 * 1024
+
+STENCIL = (135.0, -13.5, 1.0)
+UNIT = -0.5 / 90.0 / 4.0
 DIAGONAL = (1.5 * 49.0 / 18.0 - 5.0) / 4.0
 
 
@@ -95,6 +96,7 @@
 ROWS = 4 * NX
 EDGE = 16
 CHUNK = 256
+UNROLL = False
 
 
 def filter_kernel(in_ref, ring_ref, out_ref, one_ref, two_ref, diag_ref):
@@ -105,7 +107,7 @@
         low = low_rows((8, PLANE))
         for t in range(4):
             row = jnp.where(low, pot[2 * t : 2 * t + 1], pot[2 * t + 1 : 2 * t + 2])
-            diag_ref[pl.ds(base + 8 * t, 8), :] = 0.25 * row + DIAGONAL
+            diag_ref[pl.ds(base + 8 * t, 8), :] = 0.5 * row + 2.0 * DIAGONAL
         return 0
 
     lax.fori_loop(0, 32, fill, 0)
@@ -115,12 +117,10 @@
         ref[0:EDGE, :] = ref[ROWS : ROWS + EDGE, :]
         ref[ROWS + EDGE :, :] = ref[EDGE : 2 * EDGE, :]
 
-    def apply(cur_ref, base):
+    def twice(cur_ref, base):
         wide = cur_ref[pl.ds(base, CHUNK + 2 * EDGE), :]
         cur = wide[EDGE : EDGE + CHUNK]
-        hi, lo = split(cur)
-        both = dot(jnp.concatenate([hi, lo], axis=0), ring)
-        near = both[:CHUNK] + both[CHUNK:]
+        near = dot(jnp.concatenate(split(cur), axis=1), ring)
         half = pltpu.roll(wide, 4, 0)
 
         def at(a, shift):
@@ -129,11 +129,16 @@
         along = (
             STENCIL[0] * (at(half, 0) + at(half, 8))
             + STENCIL[1] * (at(wide, 8) + at(wide, -8))
-            + STENCIL[2] * (at(half, -8) + at(half, 16))
+            + (at(half, -8) + at(half, 16))
         )
-        return UNIT * (near + along) + diag_ref[pl.ds(base, CHUNK), :] * cur, cur
+        return (2.0 * UNIT) * (near + along) + diag_ref[pl.ds(base, CHUNK), :] * cur
 
     def sweep(body):
+        if UNROLL:
+            for i in range(ROWS // CHUNK):
+                body(i * CHUNK)
+            return
+
         def run(i, _):
             body(pl.multiple_of(i * CHUNK, CHUNK))
             return 0
@@ -143,8 +148,7 @@
     close(one_ref)
 
     def first(base):
-        value, _ = apply(one_ref, base)
-        two_ref[pl.ds(EDGE + base, CHUNK), :] = value
+        two_ref[pl.ds(EDGE + base, CHUNK), :] = 0.5 * twice(one_ref, base)
 
     sweep(first)
     previous, current = one_ref, two_ref
@@ -153,8 +157,7 @@
         last = degree_step == DEGREE
 
         def following(base, previous=previous, current=current, last=last):
-            value, _ = apply(current, base)
-            value = 2.0 * value - previous[pl.ds(EDGE + base, CHUNK), :]
+            value = twice(current, base) - previous[pl.ds(EDGE + base, CHUNK), :]
             if last:
                 out_ref[pl.ds(base, CHUNK), :] = value
             else:
@@ -178,7 +181,11 @@
     )(spread_cells.reshape(32, 40, PLANE), ring)
 
 
-def gram_kernel(in_ref, hi_ref, lo_ref, gram_ref, cells_ref):
+BLOCKS = tuple((i, j) for i in range(4) for j in range(i, 4))
+PART = 384
+
+
+def gram_kernel(in_ref, near_ref, far_ref, gram_ref, cells_ref):
     for q in range(4):
         a = in_ref[:, 0, q]
         b = in_ref[:, 1, q]
@@ -187,22 +194,26 @@
         cells_ref[rows, :PLANE] = jnp.where(low, a, swap_halves(b)).reshape(128, PLANE)
         cells_ref[rows, PLANE:] = jnp.where(low, swap_halves(a), b).reshape(128, PLANE)
     by_orbital = cells_ref[...]
-    left = split(by_orbital)
-    right = split(by_orbital.T)
-    hi_ref[...] = right[0]
-    lo_ref[...] = right[1]
-    gram = dot3(left, right)
-    for k in range(4):
-        gram_ref[k] = gram[:, 128 * k : 128 * (k + 1)]
+    by_cell = by_orbital.T
+    near_ref[...] = by_cell[:PART]
+    far_ref[...] = by_cell[PART:]
+    left, right = split(by_orbital), split(by_cell)
+    top = dot3([p[:256] for p in left], right)
+    low_block = dot3([p[256:] for p in left], [p[:, 256:] for p in right])
+    for k, (i, j) in enumerate(BLOCKS):
+        part, i, j = (top, i, j) if i < 2 else (low_block, i - 2, j - 2)
+        gram_ref[128 * k : 128 * (k + 1), :] = part[
+            128 * i : 128 * (i + 1), 128 * j : 128 * (j + 1)
+        ]
 
 
 def gram(cells):
     return pl.pallas_call(
         gram_kernel,
         out_shape=(
-            jax.ShapeDtypeStruct((2 * PLANE, NORB), BF16),
-            jax.ShapeDtypeStruct((2 * PLANE, NORB), BF16),
-            jax.ShapeDtypeStruct((4, NORB, 128), F32),
+            jax.ShapeDtypeStruct((PART, NORB), F32),
+            jax.ShapeDtypeStruct((2 * PLANE - PART, NORB), F32),
+            jax.ShapeDtypeStruct((128 * len(BLOCKS), 128), F32),
         ),
         scratch_shapes=[pltpu.VMEM((NORB, 2 * PLANE), F32)],
         compiler_params=pltpu.CompilerParams(vmem_limit_bytes=VMEM),
@@ -210,50 +221,126 @@
     )(cells.reshape(16, 2, 4, 8, PLANE))
 
 
-def whiten_kernel(gram_ref, hi_ref, lo_ref, out_ref):
-    total = jnp.concatenate([gram_ref[k] for k in range(4)], axis=1)
-    total = total * (1.0 / (NX * PLANE))
+def product(a, b):
+    top = dot3([p[:256] for p in a], b)
+    low_block = dot3([p[256:] for p in a], [p[:, 256:] for p in b])
+    return jnp.concatenate(
+        [top, jnp.concatenate([top[:, 256:].T, low_block], axis=1)], axis=0
+    )
+
+
+def root_kernel(gram_ref, out_ref):
+    blocks = {}
+    for k, (i, j) in enumerate(BLOCKS):
+        block = gram_ref[128 * k : 128 * (k + 1), :] * (1.0 / (NX * PLANE))
+        blocks[i, j] = block
+        if i != j:
+            blocks[j, i] = block.T
+    total = jnp.concatenate(
+        [jnp.concatenate([blocks[i, j] for j in range(4)], axis=1) for i in range(4)], axis=0
+    )
     square = jnp.sum(jnp.sum(total * total, axis=0, keepdims=True), axis=1, keepdims=True)
     norm_scale = jnp.sqrt(square + 1e-06)
     row = lax.broadcasted_iota(jnp.int32, (NORB, NORB), 0)
     col = lax.broadcasted_iota(jnp.int32, (NORB, NORB), 1)
-    three_halves = jnp.where(row == col, 1.5, 0.0).astype(F32)
-    scaled = total / norm_scale
+    diagonal = row == col
+    m = total / norm_scale
     inverse = None
-    for step in range(NS_ITERS):
-        factor = three_halves - 0.5 * scaled
-        parts = split(factor)
-        inverse = factor if inverse is None else dot3(parts, split(inverse))
-        if step < NS_ITERS - 1:
-            scaled = dot3(split(dot3(split(scaled), parts)), parts)
+    for pair in range(NS_ITERS // 2):
+        parts = split(m)
+        m2 = product(parts, parts)
+        tail = product(split(m2), split(0.0625 * m2 - 0.5625 * m))
+        factor = (jnp.where(diagonal, 2.25, 0.0) - 2.4375 * m) + (1.6875 * m2 + tail)
+        factors = split(factor)
+        inverse = factor if inverse is None else product(split(inverse), factors)
+        if pair < NS_ITERS // 2 - 1:
+            m = product(parts, split(product(factors, factors)))
     root = split(inverse / jnp.sqrt(norm_scale))
-    white = dot3((hi_ref[...], lo_ref[...]), root)
-    for k in range(4):
-        out_ref[k] = white[:, 128 * k : 128 * (k + 1)]
-
-
-def whiten(total, hi, lo):
+    for h in range(2):
+        for k in range(4):
+            out_ref[h, k] = root[h][:, 128 * k : 128 * (k + 1)]
+
+
+def inverse_root(total):
+    return pl.pallas_call(
+        root_kernel,
+        out_shape=jax.ShapeDtypeStruct((2, 4, NORB, 128), BF16),
+        compiler_params=pltpu.CompilerParams(vmem_limit_bytes=VMEM),
+        name="inverse_root",
+    )(total)
+
+
+def whiten_kernel(place_ref, *refs):
+    chunks, root_ref, out_ref = refs[:4], refs[4], refs[5]
+    root = (root_ref[0, 0], root_ref[1, 0])
+    for part in range(2):
+
+        @pl.when(pl.program_id(0) == part)
+        def _():
+            near, far = chunks[2 * part : 2 * part + 2]
+            out_ref[0, 0, :PART] = dot3(split(near[...]), root)
+            out_ref[0, 0, PART:] = dot3(split(far[...]), root)
+
+
+def whiten(place, chunks, root, whole):
+    def slot(i, p):
+        return (jnp.where(i == 0, p[0], 1 - p[0]), p[2] if whole else 0, 0, 0)
+
+    def all_of(a):
+        return pl.BlockSpec(a.shape, lambda i, p: (0, 0))
+
     return pl.pallas_call(
         whiten_kernel,
-        out_shape=jax.ShapeDtypeStruct((4, 2 * PLANE, 128), F32),
-        compiler_params=pltpu.CompilerParams(vmem_limit_bytes=VMEM),
+        grid_spec=pltpu.PrefetchScalarGridSpec(
+            num_scalar_prefetch=1,
+            grid=(2,),
+            in_specs=[all_of(a) for a in chunks]
+            + [pl.BlockSpec((2, 1, NORB, 128), lambda i, p: (0, p[1], 0, 0))],
+            out_specs=pl.BlockSpec((1, 1, 2 * PLANE, 128), slot),
+        ),
+        out_shape=jax.ShapeDtypeStruct((2, 2 if whole else 1, 2 * PLANE, 128), F32),
+        compiler_params=pltpu.CompilerParams(vmem_limit_bytes=VMEM_SMALL),
         name="whiten",
-    )(total, hi, lo)
+    )(place, *chunks, root)
 
 
 def exchange(a, axes):
     return lax.all_to_all(a, axes, 0, 0, tiled=True)
 
 
+def swap(a, axis):
+    return lax.ppermute(a, axis, [(0, 1), (1, 0)])
+
+
 def body(orbitals, potential):
-    ring = jnp.asarray(plane_stencil(), BF16)
+    zl, c = lax.axis_index("zl"), lax.axis_index("c")
+    ring = jnp.asarray(np.tile(plane_stencil(), (2, 1)), BF16)
     sent = spread(orbitals.reshape(SLAB, PLANE, 128), potential.reshape(SLAB, PLANE))
     filtered = chebyshev(exchange(sent, SPACE), ring)
-    hi, lo, partial_terms = gram(exchange(filtered, EVERY))
-    terms = exchange(partial_terms.reshape(4 * NORB, 128), EVERY)
-    own = jnp.sum(terms.reshape(128, -1, 128), axis=0)
-    total = exchange(jnp.tile(own, (128, 1)), EVERY).reshape(4, NORB, 128)
-    whitened = exchange(whiten(total, hi, lo).reshape(8 * PLANE, 128), ORB)
+    near, far, terms = gram(exchange(filtered, EVERY))
+
+    other_near = swap(near, "zl")
+    halves = terms.reshape(2, -1, 128)
+    own = lax.dynamic_index_in_dim(halves, c, 0, False)
+    own = own + swap(lax.dynamic_index_in_dim(halves, 1 - c, 0, False), "c")
+    share = exchange(own, ("x", "y"))
+    share = jnp.sum(share.reshape(16, -1, 128), axis=0)
+    share, other_near = lax.optimization_barrier((share, other_near))
+    share = share + swap(share, "zl")
+    share = share + swap(share, "zh")
+    share, far = lax.optimization_barrier((share, far))
+    other_far = swap(far, "zl")
+    own = exchange(jnp.tile(share, (16, 1)), ("x", "y"))
+    sibling = swap(own, "c")
+    total = jnp.where(
+        c == 0, jnp.concatenate([own, sibling]), jnp.concatenate([sibling, own])
+    )
+    root = inverse_root(total)
+
+    chunks = (near, far, other_near, other_far)
+    theirs = whiten(jnp.stack([zl, 2 * zl + 1 - c, c]), chunks, root, False)
+    ours = whiten(jnp.stack([zl, 2 * zl + c, c]), chunks, root, True)
+    whitened = lax.dynamic_update_slice(ours, swap(theirs, "c"), (0, 1 - c, 0, 0))
     return whitened.reshape(orbitals.shape)
 
 

time: 208 us -> 170 us (0.82)
  blocking collectives: 158 us -> 71.4 us
  waiting for transfers between devices: 0 us -> 43.5 us
  starting transfers between devices: 0 us -> 8.36 us
  Pallas kernels: 45.1 us -> 37.2 us
  local copies, waits for them, and re-layouts: 2.92 us -> 6.84 us
    all_to_all x5 -> x3, blocking collectives: 158 us -> 71.4 us  [exchange(): return lax.all_to_all(a, axes, 0, 0, tiled=True)]
    all_to_all x0 -> x1, waiting for transfers between devices: none -> 30 us  [exchange(): return lax.all_to_all(a, axes, 0, 0, tiled=True)]
    ppermute x0 -> x7, waiting for transfers between devices: none -> 13.5 us  [swap(): return lax.ppermute(a, axis, [(0, 1), (1, 0)])]
    all_to_all x0 -> x1, starting transfers between devices: none -> 4.65 us  [exchange(): return lax.all_to_all(a, axes, 0, 0, tiled=True)]
    ppermute x0 -> x7, starting transfers between devices: none -> 3.71 us  [swap(): return lax.ppermute(a, axis, [(0, 1), (1, 0)])]
    pallas_call x1, Pallas kernels: 13.2 us -> 9.6 us  [chebyshev(): pl.pallas_call(filter_kernel, out_shape=jax.ShapeDtypeStruct((ROWS, PLANE...]
    pallas_call x1, Pallas kernels: 4.67 us -> 1.13 us  [spread(): pl.pallas_call(spread_kernel, grid=(5,), in_specs=[pl.BlockSpec((2, PLANE...]
    unnamed x1 -> x8, local copies, waits for them, and re-layouts: 1.32 us -> 3.6 us
  transfers between devices with their start and end apart: 0 -> 8, of which waited for: 0 -> 6; matrix products, arithmetic and copies ran while one was open for 0% -> 1% of each run, Pallas kernels for 0% -> 12%
where the time goes in v2:
time: 170 us; the launch traced here: 169 us
  blocking collectives  71.4 us (42%)
  waiting for transfers between devices  43.5 us (26%)
  Pallas kernels  37.2 us (22%)
  starting transfers between devices  8.36 us (5%)
  local copies, waits for them, and re-layouts  6.84 us (4%)
    all_to_all x3, blocking collectives, exchange(): return lax.all_to_all(a, axes, 0, 0, tiled=True)  71.4 us
    all_to_all x1, waiting for transfers between devices, exchange(): return lax.all_to_all(a, axes, 0, 0, tiled=True)  30 us
    pallas_call x1, Pallas kernels, inverse_root(): pl.pallas_call(root_kernel, out_shape=jax.ShapeDtypeStruct((2, 4, NORB, 1...  14.5 us
    ppermute x7, waiting for transfers between devices, swap(): return lax.ppermute(a, axis, [(0, 1), (1, 0)])  13.5 us
    pallas_call x2, Pallas kernels, whiten(): pl.pallas_call(whiten_kernel, grid_spec=pltpu.PrefetchScalarGridSpec(num_...  10.2 us
    pallas_call x1, Pallas kernels, chebyshev(): pl.pallas_call(filter_kernel, out_shape=jax.ShapeDtypeStruct((ROWS, PLANE...  9.6 us
    all_to_all x1, starting transfers between devices, exchange(): return lax.all_to_all(a, axes, 0, 0, tiled=True)  4.65 us
    ppermute x7, starting transfers between devices, swap(): return lax.ppermute(a, axis, [(0, 1), (1, 0)])  3.71 us
  transfers between devices with their start and end apart: 8, of which 6 were waited for; matrix products, arithmetic and copies ran while one was open for 1% of the time, Pallas kernels for 12%

profile of v2, /device:TPU:0, one launch (start us, length us, event | category | flops | bytes accessed | tf_op | source)
XLA Modules:
  0.0 168.7 jit_solution(8532458218593318896)
XLA Ops:
  0.0 0.9 reshape.36.pot_ref
  0.9 0.0 copy-start.1
  0.9 1.6 copy-done.1
  2.5 1.1 spread.1
  3.7 0.0 copy-start.2
  3.7 46.5 %all_to_all.36.in_ref = f32[32,40,512]{2,1,0:T(8,128)S(1)} all-to-all(f32[32,40,512]{2,1,0:T(8,128)S(1)} %bitcast.16), channel_id=1, replica_groups=mesh['x'=4,'zh'=2,'y'=4,'zl'=2,'c'=2] {'x','zh','y'}, dimensions={0} | all-to-all | bytes 5242880 | tf_op jit(solution)/shard_map/all_to_all | solution.py:308
  50.1 0.0 copy-done.2
  50.2 9.6 %chebyshev.1 = f32[1024,512]{1,0:T(8,128)S(1)} custom-call(f32[32,40,512]{2,1,0:T(8,128)S(1)} %all_to_all.36.in_ref, bf16[1024,512]{1,0:T(8,128)(2,1)S(1)} %copy-done.2), custom_call_target="tpu_custom_call" | custom-call | tf_op jit(solution)/shard_map/chebyshev/pallas_call | solution.py:171
  59.8 0.0 copy-start
  59.8 1.3 copy-done
  61.1 4.7 %all-to-all-start.1 = ((f32[128,8,512]{2,1,0:T(8,128)}), f32[128,8,512]{2,1,0:T(8,128)S(1)}, u32[]{:S(2)}, u32[]{:S(2)}) async-start(f32[128,8,512]{2,1,0:T(8,128)} %bitcast.18), calls=%async_computation.1 | async-start | bytes 4194304 | tf_op jit(solution)/shard_map/all_to_all | solution.py:308
  65.7 30.0 %all-to-all-done.1 = f32[128,8,512]{2,1,0:T(8,128)S(1)} async-done(((f32[128,8,512]{2,1,0:T(8,128)}), f32[128,8,512]{2,1,0:T(8,128)S(1)}, u32[]{:S(2)}, u32[]{:S(2)}) %all-to-all-start.1) | async-done | bytes 2097184 | tf_op jit(solution)/shard_map/all_to_all | solution.py:308
  95.8 1.7 %gram.1 = (f32[384,512]{1,0:T(8,128)}, f32[640,512]{1,0:T(8,128)S(1)}, f32[1280,128]{1,0:T(8,128)S(1)}) custom-call(f32[16,2,4,8,512]{4,3,2,1,0:T(8,128)S(1)} %bitcast.17), custom_call_target="tpu_custom_call" | custom-call | tf_op jit(solution)/shard_map/gram/pallas_call | solution.py:211
  97.5 0.0 copy-start.3
  97.5 0.1 collective-permute-start
  97.6 0.7 copy-done.3
  98.3 0.8 collective-permute-start.1
  99.1 0.1 collective-permute-done
  99.2 1.0 bitcast_add_fusion
  100.2 13.1 %all_to_all.37 = f32[16,40,128]{2,1,0:T(8,128)S(1)} all-to-all(f32[16,40,128]{2,1,0:T(8,128)S(1)} %bitcast.22), channel_id=1, replica_groups=mesh['x'=4,'zh'=2,'y'=4,'zl'=2,'c'=2] {'x','y'}, dimensions={0} | all-to-all | bytes 655360 | tf_op jit(solution)/shard_map/all_to_all | solution.py:308
  113.3 4.4 %collective-permute-done.1.refs_2_ = f32[384,512]{1,0:T(8,128)S(1)} collective-permute-done((f32[384,512]{1,0:T(8,128)}, f32[384,512]{1,0:T(8,128)S(1)}, u32[]{:S(2)}, u32[]{:S(2)}) %collective-permute-start.1) | collective-permute-done | bytes 786464 | tf_op jit(solution)/shard_map/ppermute | solution.py:312
  117.8 0.8 collective-permute-start.2
  118.5 3.0 %collective-permute-done.2 = f32[40,128]{1,0:T(8,128)S(1)} collective-permute-done((f32[40,128]{1,0:T(8,128)S(1)}, f32[40,128]{1,0:T(8,128)S(1)}, u32[]{:S(2)}, u32[]{:S(2)}) %collective-permute-start.2) | collective-permute-done | bytes 20512 | tf_op jit(solution)/shard_map/ppermute | solution.py:312
  121.5 1.1 collective-permute-start.3
  122.7 4.4 %collective-permute-done.3 = f32[40,128]{1,0:T(8,128)S(1)} collective-permute-done((f32[40,128]{1,0:T(8,128)S(1)}, f32[40,128]{1,0:T(8,128)S(1)}, u32[]{:S(2)}, u32[]{:S(2)}) %collective-permute-start.3) | collective-permute-done | bytes 20512 | tf_op jit(solution)/shard_map/ppermute | solution.py:312
  127.0 0.8 collective-permute-start.4
  127.8 11.9 %all_to_all.38 = f32[16,40,128]{2,1,0:T(8,128)S(1)} all-to-all(f32[16,40,128]{2,1,0:T(8,128)S(1)} %tile.2), channel_id=1, replica_groups=mesh['x'=4,'zh'=2,'y'=4,'zl'=2,'c'=2] {'x','y'}, dimensions={0} | all-to-all | bytes 655360 | tf_op jit(solution)/shard_map/all_to_all | solution.py:308
  139.7 0.0 collective-permute-start.5
  139.7 0.1 add_add_fusion.1.place_ref
  139.8 1.6 collective-permute-done.5
  141.4 14.5 %inverse_root.1.refs_4_ = bf16[2,4,512,128]{3,2,1,0:T(8,128)(2,1)S(1)} custom-call(f32[1280,128]{1,0:T(8,128)S(1)} %maximum_select_fusion.gram_ref), custom_call_target="tpu_custom_call" | custom-call | tf_op jit(solution)/shard_map/inverse_root/pallas_call | solution.py:265
  155.9 0.0 collective-permute-done.4.refs_3_
  155.9 5.2 %whiten.3 = f32[2,1,1024,128]{3,2,1,0:T(8,128)} custom-call(s32[3]{0:T(128)S(1)} %add_add_fusion.1.place_ref, f32[384,512]{1,0:T(8,128)} %get-tuple-element.12.refs_0_, f32[640,512]{1,0:T(8,128)S(1)} %get-tuple-element.16.refs_1_, f32[384,512]{1,0:T(8,128)S(1)} %collective-permute-done.1.refs_2_, f32[640,512]{1,0:T(8,128)} %collective-permute-done.4.refs_3_, ...), custom_call_target="tpu_custom_call" | custom-call | tf_op jit(solution)/shard_map/whiten/pallas_call | solution.py:292
  161.2 0.1 collective-permute-start.6
  161.3 0.1 add_add_fusion.place_ref
  161.4 5.0 %whiten.2 = f32[2,2,1024,128]{3,2,1,0:T(8,128)} custom-call(s32[3]{0:T(128)S(1)} %add_add_fusion.place_ref, f32[384,512]{1,0:T(8,128)} %get-tuple-element.12.refs_0_, f32[640,512]{1,0:T(8,128)S(1)} %get-tuple-element.16.refs_1_, f32[384,512]{1,0:T(8,128)S(1)} %collective-permute-done.1.refs_2_, f32[640,512]{1,0:T(8,128)} %collective-permute-done.4.refs_3_, ...), custom_call_target="tpu_custom_call" | custom-call | tf_op jit(solution)/shard_map/whiten/pallas_call | solution.py:292
  166.4 0.0 collective-permute-done.6
  166.4 2.3 %constant_dynamic-update-slice_fusion = f32[2,2,1024,128]{3,2,1,0:T(8,128)} fusion(f32[2,2,1024,128]{3,2,1,0:T(8,128)} %whiten.2, f32[2,1,1024,128]{3,2,1,0:T(8,128)} %collective-permute-done.6, s32[]{:T(128)S(6)} %select_n.17), kind=kLoop, calls=%fused_computation.3 | loop fusion | bytes 2097156 | tf_op jit(solution)/shard_map/dynamic_update_slice | solution.py:343
  (6 shorter events, 0.1 us)
Async XLA Ops:
  0.9 1.6 copy-start.1
  3.7 46.5 %copy-start.2 = (bf16[1024,512]{1,0:T(8,128)(2,1)S(1)}, bf16[1024,512]{1,0:T(8,128)(2,1)}, u32[]{:S(2)}) copy-start(bf16[1024,512]{1,0:T(8,128)(2,1)} %constant.24.clone.ring_ref) | copy-start | bytes 3145732
  59.8 1.3 copy-start
  61.1 34.7 %all-to-all-start.1 = ((f32[128,8,512]{2,1,0:T(8,128)}), f32[128,8,512]{2,1,0:T(8,128)S(1)}, u32[]{:S(2)}, u32[]{:S(2)}) async-start(f32[128,8,512]{2,1,0:T(8,128)} %bitcast.18), calls=%async_computation.1 | async-start | bytes 4194304 | tf_op jit(solution)/shard_map/all_to_all | solution.py:308
  97.5 0.8 copy-start.3
  97.5 1.7 %collective-permute-start = (f32[640,128]{1,0:T(8,128)S(1)}, f32[640,128]{1,0:T(8,128)S(1)}, u32[]{:S(2)}, u32[]{:S(2)}) collective-permute-start(f32[640,128]{1,0:T(8,128)S(1)} %dynamic-slice_bitcast_fusion), channel_id=1, source_target_pairs={{0,1},{1,0},{2,3},{3,2},{4,5},{5,4},{6,7},{7,6},{8,9},{9,8},{10,11... | collective-permute-start | bytes 983048 | tf_op jit(solution)/shard_map/ppermute | solution.py:312
  98.3 19.5 %collective-permute-start.1 = (f32[384,512]{1,0:T(8,128)}, f32[384,512]{1,0:T(8,128)S(1)}, u32[]{:S(2)}, u32[]{:S(2)}) collective-permute-start(f32[384,512]{1,0:T(8,128)} %get-tuple-element.12.refs_0_), channel_id=1, source_target_pairs={{0,2},{2,0},{1,3},{3,1},{4,6},{6,4},{5,7},{7,5},{8,10},{10,8},{9,1... | collective-permute-start | bytes 2359304 | tf_op jit(solution)/shard_map/ppermute | solution.py:312
  117.8 3.8 %collective-permute-start.2 = (f32[40,128]{1,0:T(8,128)S(1)}, f32[40,128]{1,0:T(8,128)S(1)}, u32[]{:S(2)}, u32[]{:S(2)}) collective-permute-start(f32[40,128]{1,0:T(8,128)S(1)} %reduce_sum.9), channel_id=1, source_target_pairs={{0,2},{2,0},{1,3},{3,1},{4,6},{6,4},{5,7},{7,5},{8,10},{10,8},{9,1... | collective-permute-start | bytes 61448 | tf_op jit(solution)/shard_map/ppermute | solution.py:312
  121.5 5.5 %collective-permute-start.3 = (f32[40,128]{1,0:T(8,128)S(1)}, f32[40,128]{1,0:T(8,128)S(1)}, u32[]{:S(2)}, u32[]{:S(2)}) collective-permute-start(f32[40,128]{1,0:T(8,128)S(1)} %add.28), channel_id=1, source_target_pairs={{0,16},{16,0},{1,17},{17,1},{2,18},{18,2},{3,19},{19,3},{4,20},{20... | collective-permute-start | bytes 61448 | tf_op jit(solution)/shard_map/ppermute | solution.py:312
  127.0 28.9 %collective-permute-start.4 = (f32[640,512]{1,0:T(8,128)S(1)}, f32[640,512]{1,0:T(8,128)}, u32[]{:S(2)}, u32[]{:S(2)}) collective-permute-start(f32[640,512]{1,0:T(8,128)S(1)} %get-tuple-element.16.refs_1_), channel_id=1, source_target_pairs={{0,2},{2,0},{1,3},{3,1},{4,6},{6,4},{5,7},{7,5},{8,10},{10,8},{9,1... | collective-permute-start | bytes 3932168 | tf_op jit(solution)/shard_map/ppermute | solution.py:312
  139.7 1.6 collective-permute-start.5
  161.2 5.2 %collective-permute-start.6 = (f32[2,1,1024,128]{3,2,1,0:T(8,128)}, f32[2,1,1024,128]{3,2,1,0:T(8,128)}, u32[]{:S(2)}, u32[]{:S(2)}) collective-permute-start(f32[2,1,1024,128]{3,2,1,0:T(8,128)} %whiten.3), channel_id=1, source_target_pairs={{0,1},{1,0},{2,3},{3,2},{4,5},{5,4},{6,7},{7,6},{8,9},{9,8},{10,11... | collective-permute-start | bytes 3145736 | tf_op jit(solution)/shard_map/ppermute | solution.py:312

commit v3 on v2

v3 whole, which is shorter than its diff:
```python
import functools

import numpy as np
import jax
import jax.numpy as jnp
from jax import lax
from jax.experimental import pallas as pl
from jax.experimental.pallas import tpu as pltpu
from jax.sharding import Mesh, PartitionSpec as P

DEGREE = 4
NS_ITERS = 8
NY, NZ = 16, 32
PLANE = NY * NZ
NX = 256
NORB = 512
SLAB = 8
SPACE = ("x", "zh", "y")
ORB = ("zl", "c")
EVERY = SPACE + ORB
F32 = jnp.float32
BF16 = jnp.bfloat16
VMEM = 30 * 1024 * 1024
VMEM_SMALL = 24 * 1024 * 1024

STENCIL = (135.0, -13.5, 1.0)
UNIT = -0.5 / 90.0 / 4.0
DIAGONAL = (1.5 * 49.0 / 18.0 - 5.0) / 4.0


def plane_stencil():
    def ring(n):
        m = np.zeros((n, n), np.float32)
        for k, w in enumerate(STENCIL, 1):
            for i in range(n):
                m[i, (i + k) % n] += w
                m[i, (i - k) % n] += w
        return m

    return np.kron(ring(NY), np.eye(NZ, dtype=np.float32)) + np.kron(
        np.eye(NY, dtype=np.float32), ring(NZ)
    )


def low_rows(shape):
    return lax.broadcasted_iota(jnp.int32, shape, len(shape) - 2) < 4


def swap_halves(a):
    return pltpu.roll(a, 4, a.ndim - 2)


def split(a):
    hi = a.astype(BF16)
    return hi, (a - hi.astype(F32)).astype(BF16)


def dot(a, b):
    return jnp.dot(a, b, preferred_element_type=F32)


def dot_wide(a, b):
    wide = jnp.concatenate(b, axis=1)
    high, low = dot(a[0], wide), dot(a[1], wide)
    n = b[0].shape[1]
    return high[:, :n] + (high[:, n:] + low[:, :n])


def dot3(a, b):
    return dot(a[0], b[0]) + (dot(a[0], b[1]) + dot(a[1], b[0]))


def spread_kernel(v_ref, pot_ref, out_ref):
    step = pl.program_id(0)

    @pl.when(step < 4)
    def _():
        a = v_ref[0].T.reshape(16, 8, PLANE)
        b = v_ref[1].T.reshape(16, 8, PLANE)
        low = low_rows(a.shape)
        out_ref[:, 0] = jnp.where(low, a, swap_halves(b))
        out_ref[:, 1] = jnp.where(low, swap_halves(a), b)

    @pl.when(step == 4)
    def _():
        pot = jnp.concatenate([pot_ref[:, y, :] for y in range(NY)], axis=1)
        out_ref[...] = jnp.broadcast_to(pot, out_ref.shape)


def spread(field, potential):
    out = pl.pallas_call(
        spread_kernel,
        grid=(5,),
        in_specs=[
            pl.BlockSpec((2, PLANE, 128), lambda i: (jnp.minimum(i, 3), 0, 0)),
            pl.BlockSpec((SLAB, NY, NZ), lambda i: (0, 0, 0)),
        ],
        out_specs=pl.BlockSpec((16, 2, 8, PLANE), lambda i: (0, 0, i, 0)),
        out_shape=jax.ShapeDtypeStruct((16, 2, 40, PLANE), F32),
        compiler_params=pltpu.CompilerParams(vmem_limit_bytes=VMEM),
        name="spread",
    )(field, potential)
    return out.reshape(32 * 40, PLANE)


ROWS = 4 * NX
EDGE = 16
CHUNK = 256


def filter_kernel(in_ref, ring_ref, out_ref, one_ref, two_ref, diag_ref, sems):
    def fill(s, _):
        base = pl.multiple_of(s * 32, 32)
        one_ref[pl.ds(EDGE + base, 32), :] = in_ref[s, 0:32, :]
        pot = in_ref[s, 32:40, :]
        low = low_rows((8, PLANE))
        for t in range(4):
            row = jnp.where(low, pot[2 * t : 2 * t + 1], pot[2 * t + 1 : 2 * t + 2])
            diag_ref[pl.ds(base + 8 * t, 8), :] = 0.5 * row + 2.0 * DIAGONAL
        return 0

    lax.fori_loop(0, 32, fill, 0)
    ring = ring_ref[...]

    def close(ref):
        ref[0:EDGE, :] = ref[ROWS : ROWS + EDGE, :]
        ref[ROWS + EDGE :, :] = ref[EDGE : 2 * EDGE, :]

    def twice(cur_ref, base):
        wide = cur_ref[pl.ds(base, CHUNK + 2 * EDGE), :]
        cur = wide[EDGE : EDGE + CHUNK]
        near = dot(jnp.concatenate(split(cur), axis=1), ring)
        half = pltpu.roll(wide, 4, 0)

        def at(a, shift):
            return a[EDGE + shift : EDGE + shift + CHUNK]

        along = (
            STENCIL[0] * (at(half, 0) + at(half, 8))
            + STENCIL[1] * (at(wide, 8) + at(wide, -8))
            + (at(half, -8) + at(half, 16))
        )
        return (2.0 * UNIT) * (near + along) + diag_ref[pl.ds(base, CHUNK), :] * cur

    def sweep(body):
        for i in range(ROWS // CHUNK):
            body(i * CHUNK)

    def copy(ref, base):
        return pltpu.make_async_copy(
            ref.at[pl.ds(EDGE + base, CHUNK)],
            out_ref.at[pl.ds(base, CHUNK)],
            sems.at[base // CHUNK],
        )

    close(one_ref)

    def first(base):
        two_ref[pl.ds(EDGE + base, CHUNK), :] = 0.5 * twice(one_ref, base)

    sweep(first)
    previous, current = one_ref, two_ref
    for degree_step in range(2, DEGREE + 1):
        close(current)
        last = degree_step == DEGREE

        def following(base, previous=previous, current=current, last=last):
            rows = pl.ds(EDGE + base, CHUNK)
            previous[rows, :] = twice(current, base) - previous[rows, :]
            if last:
                copy(previous, base).start()

        sweep(following)
        previous, current = current, previous
    sweep(lambda base: copy(current, base).wait())


def chebyshev(spread_cells, ring):
    return pl.pallas_call(
        filter_kernel,
        out_shape=jax.ShapeDtypeStruct((ROWS, PLANE), F32),
        scratch_shapes=[
            pltpu.VMEM((ROWS + 2 * EDGE, PLANE), F32),
            pltpu.VMEM((ROWS + 2 * EDGE, PLANE), F32),
            pltpu.VMEM((ROWS, PLANE), F32),
            pltpu.SemaphoreType.DMA((ROWS // CHUNK,)),
        ],
        out_specs=pl.BlockSpec(memory_space=pltpu.HBM),
        compiler_params=pltpu.CompilerParams(vmem_limit_bytes=VMEM),
        name="chebyshev",
    )(spread_cells.reshape(32, 40, PLANE), ring)


BLOCKS = tuple((i, j) for i in range(4) for j in range(i, 4))
PART = 320


def gram_kernel(place_ref, in_ref, near_ref, far_ref, mine_ref, other_ref, cells_ref, sums_ref):
    for q in range(4):
        a = in_ref[:, 0, q]
        b = in_ref[:, 1, q]
        low = low_rows(a.shape)
        rows = pl.ds(128 * q, 128)
        cells_ref[rows, :PLANE] = jnp.where(low, a, swap_halves(b)).reshape(128, PLANE)
        cells_ref[rows, PLANE:] = jnp.where(low, swap_halves(a), b).reshape(128, PLANE)
    by_orbital = cells_ref[...]
    by_cell = by_orbital.T
    near_ref[...] = by_cell[:PART]
    far_ref[...] = by_cell[PART:]
    left, right = by_orbital.astype(BF16), split(by_cell)
    square, cross = dot(left, right[0]), dot(left, right[1])

    def block(a, i, j):
        return a[128 * i : 128 * (i + 1), 128 * j : 128 * (j + 1)]

    for k, (i, j) in enumerate(BLOCKS):
        rows = pl.ds(128 * (k % 5), 128)
        sums_ref[k // 5, rows, :] = block(square, i, j) + (
            block(cross, i, j) + block(cross, j, i).T
        )
    mine_ref[...] = sums_ref[place_ref[1]]
    other_ref[...] = sums_ref[1 - place_ref[1]]


SCALARS = pl.BlockSpec(memory_space=pltpu.SMEM)
VECTORS = pl.BlockSpec(memory_space=pltpu.VMEM)
ANYWHERE = pl.BlockSpec(memory_space=pl.ANY)


def gram(place, cells):
    return pl.pallas_call(
        gram_kernel,
        out_shape=(
            jax.ShapeDtypeStruct((PART, NORB), F32),
            jax.ShapeDtypeStruct((2 * PLANE - PART, NORB), F32),
            jax.ShapeDtypeStruct((640, 128), F32),
            jax.ShapeDtypeStruct((640, 128), F32),
        ),
        in_specs=[SCALARS, VECTORS],
        scratch_shapes=[pltpu.VMEM((NORB, 2 * PLANE), F32), pltpu.VMEM((2, 640, 128), F32)],
        compiler_params=pltpu.CompilerParams(vmem_limit_bytes=VMEM),
        name="gram",
    )(place, cells.reshape(16, 2, 4, 8, PLANE))


def product(a, b):
    top = dot3([p[:256] for p in a], b)
    low_block = dot_wide([p[256:] for p in a], [p[:, 256:] for p in b])
    return jnp.concatenate(
        [top, jnp.concatenate([top[:, 256:].T, low_block], axis=1)], axis=0
    )


def squared(a):
    cross = dot(a[0], a[1])
    return dot(a[0], a[0]) + (cross + cross.T)


def root_kernel(place_ref, mine_ref, other_ref, out_ref):
    zl, c = place_ref[0], place_ref[1]
    blocks = {}
    for k, (i, j) in enumerate(BLOCKS):
        rows = pl.ds(128 * (k % 5), 128)
        mine, other = mine_ref[rows, :], other_ref[rows, :]
        block = jnp.where(c == k // 5, mine, other) * (1.0 / (NX * PLANE))
        blocks[i, j] = block
        if i != j:
            blocks[j, i] = block.T
    total = jnp.concatenate(
        [jnp.concatenate([blocks[i, j] for j in range(4)], axis=1) for i in range(4)], axis=0
    )
    square = jnp.sum(jnp.sum(total * total, axis=0, keepdims=True), axis=1, keepdims=True)
    norm_scale = jnp.sqrt(square + 1e-06)
    row = lax.broadcasted_iota(jnp.int32, (NORB, NORB), 0)
    col = lax.broadcasted_iota(jnp.int32, (NORB, NORB), 1)
    diagonal = row == col
    m = total / norm_scale
    inverse = None
    for pair in range(NS_ITERS // 2):
        parts = split(m)
        m2 = squared(parts)
        tail = product(split(m2), split(0.0625 * m2 - 0.5625 * m))
        factor = (jnp.where(diagonal, 2.25, 0.0) - 2.4375 * m) + (1.6875 * m2 + tail)
        factors = split(factor)
        if inverse is None:
            chip = jnp.where(zl == 0, factor[:, :256], factor[:, 256:])
            first, second = chip[:, :128], chip[:, 128:]
            inverse = jnp.concatenate(
                [jnp.where(c == 0, first, second), jnp.where(c == 0, second, first)], axis=1
            )
        else:
            inverse = dot_wide(factors, split(inverse))
        if pair < NS_ITERS // 2 - 1:
            m = product(parts, split(squared(factors)))
    root = split(inverse / jnp.sqrt(norm_scale))
    out_ref[0] = root[0]
    out_ref[1] = root[1]


def inverse_root(place, mine, other):
    return pl.pallas_call(
        root_kernel,
        in_specs=[SCALARS, VECTORS, VECTORS],
        out_shape=jax.ShapeDtypeStruct((2, NORB, 256), BF16),
        compiler_params=pltpu.CompilerParams(vmem_limit_bytes=VMEM),
        name="inverse_root",
    )(place, mine, other)


def whiten_kernel(near_ref, far_ref, root_ref, ours_ref, theirs_ref):
    root = (root_ref[0], root_ref[1])
    for ref, rows in ((near_ref, pl.ds(0, PART)), (far_ref, pl.ds(PART, 2 * PLANE - PART))):
        white = dot_wide(split(ref[...]), root)
        ours_ref[rows, :] = white[:, :128]
        theirs_ref[rows, :] = white[:, 128:]


def whiten(near, far, root):
    return pl.pallas_call(
        whiten_kernel,
        out_shape=(jax.ShapeDtypeStruct((2 * PLANE, 128), F32),) * 2,
        compiler_params=pltpu.CompilerParams(vmem_limit_bytes=VMEM_SMALL),
        name="whiten",
    )(near, far, root)


WHOLE = jax.ShapeDtypeStruct((2, 2, 2 * PLANE, 128), F32)


def place_kernel(slots, place_ref, *refs):
    parts, whole_ref, sems = refs[: len(slots)], refs[-2], refs[-1]
    copies = []
    for k, (zl_flip, c_flip) in enumerate(slots):
        zl = 1 - place_ref[0] if zl_flip else place_ref[0]
        c = 1 - place_ref[1] if c_flip else place_ref[1]
        copies.append(pltpu.make_async_copy(parts[k], whole_ref.at[zl, c], sems.at[k]))
    for copy in copies:
        copy.start()
    for copy in copies:
        copy.wait()


def put(place, slots, parts, whole=None):
    aliased = () if whole is None else (whole,)
    return pl.pallas_call(
        functools.partial(place_kernel, slots),
        in_specs=[SCALARS] + [ANYWHERE] * (len(parts) + len(aliased)),
        out_specs=ANYWHERE,
        out_shape=WHOLE,
        scratch_shapes=[pltpu.SemaphoreType.DMA((len(parts),))],
        input_output_aliases={1 + len(parts): 0} if aliased else {},
        compiler_params=pltpu.CompilerParams(vmem_limit_bytes=VMEM_SMALL),
        name="put",
    )(place, *parts, *aliased)


def exchange(a, axes):
    return lax.all_to_all(a, axes, 0, 0, tiled=True)


def swap(a, axis):
    return lax.ppermute(a, axis, [(0, 1), (1, 0)])


def body(orbitals, potential):
    place = jnp.stack([lax.axis_index("zl"), lax.axis_index("c")])
    ring = jnp.asarray(np.tile(plane_stencil(), (2, 1)), BF16)
    sent = spread(orbitals.reshape(SLAB, PLANE, 128), potential)
    sent, place = lax.optimization_barrier((sent, place))
    filtered = chebyshev(exchange(sent, SPACE), ring)
    near, far, mine, other = gram(place, exchange(filtered, EVERY))

    other_near = swap(near, "zl")
    share = exchange(mine + swap(other, "c"), ("x", "y"))
    share = jnp.sum(share.reshape(16, -1, 128), axis=0)
    share, other_near = lax.optimization_barrier((share, other_near))
    share = share + swap(share, "zl")
    share = share + swap(share, "zh")
    share, far = lax.optimization_barrier((share, far))
    other_far = swap(far, "zl")
    total = exchange(jnp.tile(share, (16, 1)), ("x", "y"))
    root = inverse_root(place, total, swap(total, "c"))

    ours, theirs = whiten(near, far, root)
    first = swap(theirs, "c")
    other_ours, other_theirs = whiten(other_near, other_far, root)
    second = swap(other_theirs, "c")
    slots = ((False, False), (True, False), (False, True))
    whole = put(place, slots, (ours, other_ours, first))
    whitened = put(place, ((True, True),), (second,), whole)
    return whitened.reshape(orbitals.shape)


def solution(mesh):
    fine = Mesh(mesh.devices.reshape(4, 2, 4, 2, 2), EVERY)
    return jax.shard_map(
        body,
        mesh=fine,
        in_specs=(P(SPACE, None, None, ORB), P(SPACE, None, None)),
        out_specs=P(SPACE, None, None, ORB),
        check_vma=False,
    )
```

time: 170 us -> 156 us (0.918)
  blocking collectives: 71.4 us -> 105 us
  waiting for transfers between devices: 43.5 us -> 11.4 us
  Pallas kernels: 37.2 us -> 29.8 us
  local copies, waits for them, and re-layouts: 6.84 us -> 2.46 us
  starting transfers between devices: 8.36 us -> 5.33 us
    all_to_all x3 -> x4, blocking collectives: 71.4 us -> 105 us  [exchange(): return lax.all_to_all(a, axes, 0, 0, tiled=True)]
    all_to_all x1 -> x0, waiting for transfers between devices: 30 us -> none  [exchange(): return lax.all_to_all(a, axes, 0, 0, tiled=True)]
    pallas_call x3 -> x5, Pallas kernels: 24.8 us -> 18.4 us  [the longest x1 13.4 us: inverse_root(): pl.pallas_call(root_kernel, in_specs=[SCALARS, VECTORS, VECTORS], out_sha...]
    all_to_all x1 -> x0, starting transfers between devices: 4.65 us -> none  [exchange(): return lax.all_to_all(a, axes, 0, 0, tiled=True)]
    dynamic_update_slice x1 -> x0, local copies, waits for them, and re-layouts: 2.26 us -> none  [body(): lax.dynamic_update_slice(ours, swap(theirs, 'c'), (0, 1 - c, 0, 0))]
    ppermute x7 -> x8, waiting for transfers between devices: 13.5 us -> 11.4 us  [swap(): return lax.ppermute(a, axis, [(0, 1), (1, 0)])]
    ppermute x7 -> x8, starting transfers between devices: 3.71 us -> 5.33 us  [swap(): return lax.ppermute(a, axis, [(0, 1), (1, 0)])]
    unnamed x8 -> x6, local copies, waits for them, and re-layouts: 3.6 us -> 2.44 us
  transfers between devices with their start and end apart: 8 -> 8, of which waited for: 6 -> 6; matrix products, arithmetic and copies ran while one was open for 1% -> 0% of each run, Pallas kernels for 12% -> 11%
where the time goes in v3:
time: 156 us; the launch traced here: 154 us
  blocking collectives  105 us (67%)
  Pallas kernels  29.8 us (19%)
  waiting for transfers between devices  11.4 us (7%)
  starting transfers between devices  5.33 us (3%)
  local copies, waits for them, and re-layouts  2.46 us (2%)
    all_to_all x4, blocking collectives, exchange(): return lax.all_to_all(a, axes, 0, 0, tiled=True)  105 us
    pallas_call x1, Pallas kernels, inverse_root(): pl.pallas_call(root_kernel, in_specs=[SCALARS, VECTORS, VECTORS], out_sha...  13.4 us
    ppermute x8, waiting for transfers between devices, swap(): return lax.ppermute(a, axis, [(0, 1), (1, 0)])  11.4 us
    pallas_call x1, Pallas kernels, chebyshev(): pl.pallas_call(filter_kernel, out_shape=jax.ShapeDtypeStruct((ROWS, PLANE...  7.95 us
    ppermute x8, starting transfers between devices, swap(): return lax.ppermute(a, axis, [(0, 1), (1, 0)])  5.33 us
  transfers between devices with their start and end apart: 8, of which 6 were waited for; matrix products, arithmetic and copies ran while one was open for 0% of the time, Pallas kernels for 11%

profile of v3, /device:TPU:0, one launch (start us, length us, event | category | flops | bytes accessed | tf_op | source)
XLA Modules:
  0.0 154.2 jit_solution(11255631060798949045)
XLA Ops:
  0.0 0.1 pad_add_fusion.place_ref
  0.1 0.0 copy-start
  0.1 1.6 %copy-done = f32[8,16,32,128]{3,2,1,0:T(8,128)S(1)} copy-done((f32[8,16,32,128]{3,2,1,0:T(8,128)S(1)}, f32[8,16,32,128]{3,2,1,0:T(8,128)}, u32[]{:S(2)}) %copy-start) | copy-done | bytes 2097176
  1.7 0.0 copy-start.2
  1.7 0.8 copy-done.2
  2.5 1.2 spread.1
  3.7 0.0 copy-start.1
  3.7 46.5 %all_to_all.35.in_ref = f32[32,40,512]{2,1,0:T(8,128)S(1)} all-to-all(f32[32,40,512]{2,1,0:T(8,128)S(1)} %bitcast.10), channel_id=1, replica_groups=mesh['x'=4,'zh'=2,'y'=4,'zl'=2,'c'=2] {'x','zh','y'}, dimensions={0} | all-to-all | bytes 5242880 | tf_op jit(solution)/shard_map/all_to_all | solution.py:358
  50.2 0.0 copy-done.1
  50.2 7.9 %chebyshev.1 = f32[1024,512]{1,0:T(8,128)S(1)} custom-call(f32[32,40,512]{2,1,0:T(8,128)S(1)} %all_to_all.35.in_ref, bf16[1024,512]{1,0:T(8,128)(2,1)S(1)} %copy-done.1), custom_call_target="tpu_custom_call" | custom-call | tf_op jit(solution)/shard_map/chebyshev/pallas_call | solution.py:179
  58.2 34.0 %all_to_all.36 = f32[128,8,512]{2,1,0:T(8,128)S(1)} all-to-all(f32[128,8,512]{2,1,0:T(8,128)S(1)} %bitcast.12), channel_id=1, replica_groups=mesh['x'=4,'zh'=2,'y'=4,'zl'=2,'c'=2] {'x','zh','y','zl','c'}, dimensions={0} | all-to-all | bytes 4194304 | tf_op jit(solution)/shard_map/all_to_all | solution.py:358
  92.2 2.2 %gram.1 = (f32[320,512]{1,0:T(8,128)S(1)}, f32[704,512]{1,0:T(8,128)S(1)}, f32[640,128]{1,0:T(8,128)S(1)}, f32[640,128]{1,0:T(8,128)S(1)}) custom-call(s32[2]{0:T(128)S(1)} %pad_add_fusion.place_ref, f32[16,2,4,8,512]{4,3,2,1,0:T(8,128)S(1)} %bitcast.11), custom_call_target="tpu_custom_call" | custom-call | tf_op jit(solution)/shard_map/gram/pallas_call | solution.py:231
  94.4 0.9 collective-permute-start.1
  95.3 0.0 collective-permute-start
  95.3 1.6 %collective-permute-done = f32[640,128]{1,0:T(8,128)S(1)} collective-permute-done((f32[640,128]{1,0:T(8,128)S(1)}, f32[640,128]{1,0:T(8,128)S(1)}, u32[]{:S(2)}, u32[]{:S(2)}) %collective-permute-start) | collective-permute-done | bytes 327712 | tf_op jit(solution)/shard_map/ppermute | solution.py:362
  97.0 12.5 %all_to_all.37 = f32[16,40,128]{2,1,0:T(8,128)S(1)} all-to-all(f32[16,40,128]{2,1,0:T(8,128)S(1)} %bitcast.16), channel_id=1, replica_groups=mesh['x'=4,'zh'=2,'y'=4,'zl'=2,'c'=2] {'x','y'}, dimensions={0} | all-to-all | bytes 655360 | tf_op jit(solution)/shard_map/all_to_all | solution.py:358
  109.5 0.8 collective-permute-done.1.near_ref
  110.3 1.4 collective-permute-start.2
  111.7 2.4 %collective-permute-done.2 = f32[40,128]{1,0:T(8,128)S(1)} collective-permute-done((f32[40,128]{1,0:T(8,128)S(1)}, f32[40,128]{1,0:T(8,128)S(1)}, u32[]{:S(2)}, u32[]{:S(2)}) %collective-permute-start.2) | collective-permute-done | bytes 20512 | tf_op jit(solution)/shard_map/ppermute | solution.py:362
  114.1 0.8 collective-permute-start.3
  115.0 4.7 %collective-permute-done.3 = f32[40,128]{1,0:T(8,128)S(1)} collective-permute-done((f32[40,128]{1,0:T(8,128)S(1)}, f32[40,128]{1,0:T(8,128)S(1)}, u32[]{:S(2)}, u32[]{:S(2)}) %collective-permute-start.3) | collective-permute-done | bytes 20512 | tf_op jit(solution)/shard_map/ppermute | solution.py:362
  119.6 1.5 collective-permute-start.4
  121.2 11.8 %all_to_all.38 = f32[16,40,128]{2,1,0:T(8,128)S(1)} all-to-all(f32[16,40,128]{2,1,0:T(8,128)S(1)} %tile.2), channel_id=1, replica_groups=mesh['x'=4,'zh'=2,'y'=4,'zl'=2,'c'=2] {'x','y'}, dimensions={0} | all-to-all | bytes 655360 | tf_op jit(solution)/shard_map/all_to_all | solution.py:358
  133.0 0.0 collective-permute-start.5
  133.0 1.6 %collective-permute-done.5.other_ref = f32[640,128]{1,0:T(8,128)S(1)} collective-permute-done((f32[640,128]{1,0:T(8,128)S(1)}, f32[640,128]{1,0:T(8,128)S(1)}, u32[]{:S(2)}, u32[]{:S(2)}) %collective-permute-start.5) | collective-permute-done | bytes 327712 | tf_op jit(solution)/shard_map/ppermute | solution.py:362
  134.6 13.4 %inverse_root.1.root_ref = bf16[2,512,256]{2,1,0:T(8,128)(2,1)S(1)} custom-call(s32[2]{0:T(128)S(1)} %pad_add_fusion.place_ref, f32[640,128]{1,0:T(8,128)S(1)} %bitcast.15, f32[640,128]{1,0:T(8,128)S(1)} %collective-permute-done.5.other_ref), custom_call_target="tpu_custom_call" | custom-call | tf_op jit(solution)/shard_map/inverse_root/pallas_call | solution.py:301
  148.0 1.0 whiten.3
  149.0 0.2 collective-permute-start.7
  149.2 0.0 collective-permute-done.4.far_ref
  149.2 1.0 whiten.2
  150.2 0.5 collective-permute-start.6
  150.7 0.3 collective-permute-done.7.refs_2_
  151.0 1.7 %put.2.refs_1_ = f32[2,2,1024,128]{3,2,1,0:T(8,128)} custom-call(s32[2]{0:T(128)S(1)} %pad_add_fusion.place_ref, f32[1024,128]{1,0:T(8,128)S(1)} %get-tuple-element.30.refs_0_, f32[1024,128]{1,0:T(8,128)S(1)} %get-tuple-element.31.refs_1_, f32[1024,128]{1,0:T(8,128)S(1)} %collective-permute-done.7.refs_2_), custom_call_target="tpu_custom_call" | custom-call | tf_op jit(solution)/shard_map/put/pallas_call | solution.py:345
  152.7 0.0 collective-permute-done.6.refs_0_
  152.7 1.4 put.3
  (5 shorter events, 0.1 us)
Async XLA Ops:
  0.1 1.6 %copy-start = (f32[8,16,32,128]{3,2,1,0:T(8,128)S(1)}, f32[8,16,32,128]{3,2,1,0:T(8,128)}, u32[]{:S(2)}) copy-start(f32[8,16,32,128]{3,2,1,0:T(8,128)} %param.3) | copy-start | bytes 6291460
  1.7 0.8 copy-start.2
  3.7 46.5 %copy-start.1 = (bf16[1024,512]{1,0:T(8,128)(2,1)S(1)}, bf16[1024,512]{1,0:T(8,128)(2,1)}, u32[]{:S(2)}) copy-start(bf16[1024,512]{1,0:T(8,128)(2,1)} %constant.10.clone.ring_ref) | copy-start | bytes 3145732
  94.4 15.9 %collective-permute-start.1 = (f32[320,512]{1,0:T(8,128)S(1)}, f32[320,512]{1,0:T(8,128)S(1)}, u32[]{:S(2)}, u32[]{:S(2)}) collective-permute-start(f32[320,512]{1,0:T(8,128)S(1)} %get-tuple-element.23.near_ref), channel_id=1, source_target_pairs={{0,2},{2,0},{1,3},{3,1},{4,6},{6,4},{5,7},{7,5},{8,10},{10,8},{9,1... | collective-permute-start | bytes 1966088 | tf_op jit(solution)/shard_map/ppermute | solution.py:362
  95.3 1.6 %collective-permute-start = (f32[640,128]{1,0:T(8,128)S(1)}, f32[640,128]{1,0:T(8,128)S(1)}, u32[]{:S(2)}, u32[]{:S(2)}) collective-permute-start(f32[640,128]{1,0:T(8,128)S(1)} %get-tuple-element.22), channel_id=1, source_target_pairs={{0,1},{1,0},{2,3},{3,2},{4,5},{5,4},{6,7},{7,6},{8,9},{9,8},{10,11... | collective-permute-start | bytes 983048 | tf_op jit(solution)/shard_map/ppermute | solution.py:362
  110.3 3.8 %collective-permute-start.2 = (f32[40,128]{1,0:T(8,128)S(1)}, f32[40,128]{1,0:T(8,128)S(1)}, u32[]{:S(2)}, u32[]{:S(2)}) collective-permute-start(f32[40,128]{1,0:T(8,128)S(1)} %reduce_sum.9), channel_id=1, source_target_pairs={{0,2},{2,0},{1,3},{3,1},{4,6},{6,4},{5,7},{7,5},{8,10},{10,8},{9,1... | collective-permute-start | bytes 61448 | tf_op jit(solution)/shard_map/ppermute | solution.py:362
  114.1 5.5 %collective-permute-start.3 = (f32[40,128]{1,0:T(8,128)S(1)}, f32[40,128]{1,0:T(8,128)S(1)}, u32[]{:S(2)}, u32[]{:S(2)}) collective-permute-start(f32[40,128]{1,0:T(8,128)S(1)} %add.10), channel_id=1, source_target_pairs={{0,16},{16,0},{1,17},{17,1},{2,18},{18,2},{3,19},{19,3},{4,20},{20... | collective-permute-start | bytes 61448 | tf_op jit(solution)/shard_map/ppermute | solution.py:362
  119.6 29.6 %collective-permute-start.4 = (f32[704,512]{1,0:T(8,128)S(1)}, f32[704,512]{1,0:T(8,128)S(1)}, u32[]{:S(2)}, u32[]{:S(2)}) collective-permute-start(f32[704,512]{1,0:T(8,128)S(1)} %get-tuple-element.27.far_ref), channel_id=1, source_target_pairs={{0,2},{2,0},{1,3},{3,1},{4,6},{6,4},{5,7},{7,5},{8,10},{10,8},{9,1... | collective-permute-start | bytes 4325384 | tf_op jit(solution)/shard_map/ppermute | solution.py:362
  133.0 1.6 %collective-permute-start.5 = (f32[640,128]{1,0:T(8,128)S(1)}, f32[640,128]{1,0:T(8,128)S(1)}, u32[]{:S(2)}, u32[]{:S(2)}) collective-permute-start(f32[640,128]{1,0:T(8,128)S(1)} %bitcast.14), channel_id=1, source_target_pairs={{0,1},{1,0},{2,3},{3,2},{4,5},{5,4},{6,7},{7,6},{8,9},{9,8},{10,11... | collective-permute-start | bytes 983048 | tf_op jit(solution)/shard_map/ppermute | solution.py:362
  149.0 2.0 %collective-permute-start.7 = (f32[1024,128]{1,0:T(8,128)S(1)}, f32[1024,128]{1,0:T(8,128)S(1)}, u32[]{:S(2)}, u32[]{:S(2)}) collective-permute-start(f32[1024,128]{1,0:T(8,128)S(1)} %get-tuple-element.32), channel_id=1, source_target_pairs={{0,1},{1,0},{2,3},{3,2},{4,5},{5,4},{6,7},{7,6},{8,9},{9,8},{10,11... | collective-permute-start | bytes 1572872 | tf_op jit(solution)/shard_map/ppermute | solution.py:362
  150.2 2.5 %collective-permute-start.6 = (f32[1024,128]{1,0:T(8,128)S(1)}, f32[1024,128]{1,0:T(8,128)S(1)}, u32[]{:S(2)}, u32[]{:S(2)}) collective-permute-start(f32[1024,128]{1,0:T(8,128)S(1)} %get-tuple-element.29), channel_id=1, source_target_pairs={{0,1},{1,0},{2,3},{3,2},{4,5},{5,4},{6,7},{7,6},{8,9},{9,8},{10,11... | collective-permute-start | bytes 1572872 | tf_op jit(solution)/shard_map/ppermute | solution.py:362

commit v4 on v3

--- a/solution.py
+++ b/solution.py
@@ -21,6 +21,7 @@
 F32 = jnp.float32
 BF16 = jnp.bfloat16
 VMEM = 30 * 1024 * 1024
+VMEM_SPREAD = 60 * 1024 * 1024
 VMEM_SMALL = 24 * 1024 * 1024
 
 STENCIL = (135.0, -13.5, 1.0)
@@ -70,34 +71,54 @@
     return dot(a[0], b[0]) + (dot(a[0], b[1]) + dot(a[1], b[0]))
 
 
-def spread_kernel(v_ref, pot_ref, out_ref):
-    step = pl.program_id(0)
-
-    @pl.when(step < 4)
-    def _():
-        a = v_ref[0].T.reshape(16, 8, PLANE)
-        b = v_ref[1].T.reshape(16, 8, PLANE)
+def spread_kernel(v_hbm, pot_hbm, out_hbm, v_ref, pot_ref, out_ref, in_sems, out_sems):
+    loads = [
+        pltpu.make_async_copy(v_hbm.at[x], v_ref.at[x], in_sems.at[x]) for x in range(SLAB)
+    ]
+    loads.append(pltpu.make_async_copy(pot_hbm, pot_ref, in_sems.at[SLAB]))
+    for load in loads:
+        load.start()
+
+    def store(t):
+        rows = pl.ds(8 * t, 8)
+        return pltpu.make_async_copy(
+            out_ref.at[:, :, rows], out_hbm.at[:, :, rows], out_sems.at[t]
+        )
+
+    for t in range(4):
+        loads[2 * t].wait()
+        loads[2 * t + 1].wait()
+        a = v_ref[2 * t].T.reshape(16, 8, PLANE)
+        b = v_ref[2 * t + 1].T.reshape(16, 8, PLANE)
         low = low_rows(a.shape)
-        out_ref[:, 0] = jnp.where(low, a, swap_halves(b))
-        out_ref[:, 1] = jnp.where(low, swap_halves(a), b)
-
-    @pl.when(step == 4)
-    def _():
-        pot = jnp.concatenate([pot_ref[:, y, :] for y in range(NY)], axis=1)
-        out_ref[...] = jnp.broadcast_to(pot, out_ref.shape)
+        rows = pl.ds(8 * t, 8)
+        out_ref[:, 0, rows, :] = jnp.where(low, a, swap_halves(b))
+        out_ref[:, 1, rows, :] = jnp.where(low, swap_halves(a), b)
+        store(t).start()
+        if t == 0:
+            loads[SLAB].wait()
+            pot = jnp.concatenate([pot_ref[:, y, :] for y in range(NY)], axis=1)
+            out_ref[:, :, 32:40, :] = jnp.broadcast_to(pot, (16, 2, SLAB, PLANE))
+            store(4).start()
+    for t in range(5):
+        store(t).wait()
 
 
 def spread(field, potential):
+    shape = (16, 2, 40, PLANE)
     out = pl.pallas_call(
         spread_kernel,
-        grid=(5,),
-        in_specs=[
-            pl.BlockSpec((2, PLANE, 128), lambda i: (jnp.minimum(i, 3), 0, 0)),
-            pl.BlockSpec((SLAB, NY, NZ), lambda i: (0, 0, 0)),
+        in_specs=[pl.BlockSpec(memory_space=pl.ANY)] * 2,
+        out_specs=pl.BlockSpec(memory_space=pl.ANY),
+        out_shape=jax.ShapeDtypeStruct(shape, F32),
+        scratch_shapes=[
+            pltpu.VMEM((SLAB, PLANE, 128), F32),
+            pltpu.VMEM((SLAB, NY, NZ), F32),
+            pltpu.VMEM(shape, F32),
+            pltpu.SemaphoreType.DMA((SLAB + 1,)),
+            pltpu.SemaphoreType.DMA((5,)),
         ],
-        out_specs=pl.BlockSpec((16, 2, 8, PLANE), lambda i: (0, 0, i, 0)),
-        out_shape=jax.ShapeDtypeStruct((16, 2, 40, PLANE), F32),
-        compiler_params=pltpu.CompilerParams(vmem_limit_bytes=VMEM),
+        compiler_params=pltpu.CompilerParams(vmem_limit_bytes=VMEM_SPREAD),
         name="spread",
     )(field, potential)
     return out.reshape(32 * 40, PLANE)
@@ -192,10 +213,10 @@
 
 
 BLOCKS = tuple((i, j) for i in range(4) for j in range(i, 4))
-PART = 320
-
-
-def gram_kernel(place_ref, in_ref, near_ref, far_ref, mine_ref, other_ref, cells_ref, sums_ref):
+PART = 352
+
+
+def turn_kernel(in_ref, near_ref, far_ref, left_ref, cells_ref):
     for q in range(4):
         a = in_ref[:, 0, q]
         b = in_ref[:, 1, q]
@@ -207,8 +228,26 @@
     by_cell = by_orbital.T
     near_ref[...] = by_cell[:PART]
     far_ref[...] = by_cell[PART:]
-    left, right = by_orbital.astype(BF16), split(by_cell)
-    square, cross = dot(left, right[0]), dot(left, right[1])
+    left_ref[...] = by_orbital.astype(BF16)
+
+
+def turn(cells):
+    return pl.pallas_call(
+        turn_kernel,
+        out_shape=(
+            jax.ShapeDtypeStruct((PART, NORB), F32),
+            jax.ShapeDtypeStruct((2 * PLANE - PART, NORB), F32),
+            jax.ShapeDtypeStruct((NORB, 2 * PLANE), BF16),
+        ),
+        scratch_shapes=[pltpu.VMEM((NORB, 2 * PLANE), F32)],
+        compiler_params=pltpu.CompilerParams(vmem_limit_bytes=VMEM_SMALL),
+        name="turn",
+    )(cells.reshape(16, 2, 4, 8, PLANE))
+
+
+def gram_kernel(place_ref, near_ref, far_ref, left_ref, mine_ref, other_ref, sums_ref):
+    right = split(jnp.concatenate([near_ref[...], far_ref[...]], axis=0))
+    square, cross = dot(left_ref[...], right[0]), dot(left_ref[...], right[1])
 
     def block(a, i, j):
         return a[128 * i : 128 * (i + 1), 128 * j : 128 * (j + 1)]
@@ -227,27 +266,32 @@
 ANYWHERE = pl.BlockSpec(memory_space=pl.ANY)
 
 
-def gram(place, cells):
+def gram(place, near, far, left):
     return pl.pallas_call(
         gram_kernel,
-        out_shape=(
-            jax.ShapeDtypeStruct((PART, NORB), F32),
-            jax.ShapeDtypeStruct((2 * PLANE - PART, NORB), F32),
-            jax.ShapeDtypeStruct((640, 128), F32),
-            jax.ShapeDtypeStruct((640, 128), F32),
-        ),
-        in_specs=[SCALARS, VECTORS],
-        scratch_shapes=[pltpu.VMEM((NORB, 2 * PLANE), F32), pltpu.VMEM((2, 640, 128), F32)],
-        compiler_params=pltpu.CompilerParams(vmem_limit_bytes=VMEM),
+        in_specs=[SCALARS, VECTORS, VECTORS, VECTORS],
+        out_shape=(jax.ShapeDtypeStruct((640, 128), F32),) * 2,
+        scratch_shapes=[pltpu.VMEM((2, 640, 128), F32)],
+        compiler_params=pltpu.CompilerParams(vmem_limit_bytes=VMEM_SMALL),
         name="gram",
-    )(place, cells.reshape(16, 2, 4, 8, PLANE))
+    )(place, near, far, left)
+
+
+def mirrored(a):
+    row = lax.broadcasted_iota(jnp.int32, a.shape, 0)
+    col = lax.broadcasted_iota(jnp.int32, a.shape, 1)
+    return jnp.where(row <= col, a, a.T)
 
 
 def product(a, b):
     top = dot3([p[:256] for p in a], b)
     low_block = dot_wide([p[256:] for p in a], [p[:, 256:] for p in b])
     return jnp.concatenate(
-        [top, jnp.concatenate([top[:, 256:].T, low_block], axis=1)], axis=0
+        [
+            jnp.concatenate([mirrored(top[:, :256]), top[:, 256:]], axis=1),
+            jnp.concatenate([top[:, 256:].T, mirrored(low_block)], axis=1),
+        ],
+        axis=0,
     )
 
 
@@ -279,8 +323,9 @@
     for pair in range(NS_ITERS // 2):
         parts = split(m)
         m2 = squared(parts)
-        tail = product(split(m2), split(0.0625 * m2 - 0.5625 * m))
-        factor = (jnp.where(diagonal, 2.25, 0.0) - 2.4375 * m) + (1.6875 * m2 + tail)
+        base = 0.25 * m2 - 1.125 * m + jnp.where(diagonal, 27.0 / 32.0, 0.0)
+        rest = jnp.where(diagonal, 1575.0 / 1024.0, 0.0) - (69.0 / 128.0) * m
+        factor = squared(split(base)) + rest
         factors = split(factor)
         if inverse is None:
             chip = jnp.where(zl == 0, factor[:, :256], factor[:, 256:])
@@ -368,14 +413,17 @@
     sent = spread(orbitals.reshape(SLAB, PLANE, 128), potential)
     sent, place = lax.optimization_barrier((sent, place))
     filtered = chebyshev(exchange(sent, SPACE), ring)
-    near, far, mine, other = gram(place, exchange(filtered, EVERY))
+    near, far, left = turn(exchange(filtered, EVERY))
+    mine, other = gram(place, near, far, left)
 
     other_near = swap(near, "zl")
     share = exchange(mine + swap(other, "c"), ("x", "y"))
     share = jnp.sum(share.reshape(16, -1, 128), axis=0)
     share, other_near = lax.optimization_barrier((share, other_near))
-    share = share + swap(share, "zl")
-    share = share + swap(share, "zh")
+    ring_z = [
+        lax.ppermute(share, ("zh", "zl"), [(i, (i + k) % 4) for i in range(4)]) for k in (2, 1, 3)
+    ]
+    share = (share + ring_z[0]) + (ring_z[1] + ring_z[2])
     share, far = lax.optimization_barrier((share, far))
     other_far = swap(far, "zl")
     total = exchange(jnp.tile(share, (16, 1)), ("x", "y"))

time: 156 us -> 153 us (0.981)
  waiting for transfers between devices: 11.4 us -> 7.2 us
  local copies, waits for them, and re-layouts: 2.46 us -> 0.03 us
  starting transfers between devices: 5.33 us -> 7.34 us
    ppermute x8 -> x6, waiting for transfers between devices: 11.4 us -> 3.68 us  [swap(): return lax.ppermute(a, axis, [(0, 1), (1, 0)])]
    ppermute x0 -> x3, starting transfers between devices: none -> 3.79 us  [body(): lax.ppermute(share, ('zh', 'zl'), [(i, (i + k) % 4) for i in range(4)])]
    ppermute x0 -> x3, waiting for transfers between devices: none -> 3.52 us  [body(): lax.ppermute(share, ('zh', 'zl'), [(i, (i + k) % 4) for i in range(4)])]
    pallas_call x2 -> x3, Pallas kernels: 3.41 us -> 5.85 us  [the longest x1 3.23 us: spread(): pl.pallas_call(spread_kernel, in_specs=[pl.BlockSpec(memory_space=pl.ANY)...]
    unnamed x6 -> x2, local copies, waits for them, and re-layouts: 2.44 us -> 0.01 us
    ppermute x8 -> x6, starting transfers between devices: 5.33 us -> 3.54 us  [swap(): return lax.ppermute(a, axis, [(0, 1), (1, 0)])]
  transfers between devices with their start and end apart: 8 -> 9, of which waited for: 6 -> 6; matrix products, arithmetic and copies ran while one was open for 0% -> 0% of each run, Pallas kernels for 11% -> 12%
where the time goes in v4:
time: 153 us; the launch traced here: 151 us
  blocking collectives  106 us (69%)
  Pallas kernels  30.9 us (20%)
  starting transfers between devices  7.34 us (5%)
  waiting for transfers between devices  7.2 us (5%)
    all_to_all x4, blocking collectives, exchange(): return lax.all_to_all(a, axes, 0, 0, tiled=True)  106 us
    pallas_call x1, Pallas kernels, inverse_root(): pl.pallas_call(root_kernel, in_specs=[SCALARS, VECTORS, VECTORS], out_sha...  12 us
    pallas_call x1, Pallas kernels, chebyshev(): pl.pallas_call(filter_kernel, out_shape=jax.ShapeDtypeStruct((ROWS, PLANE...  7.95 us
    ppermute x3, starting transfers between devices, body(): lax.ppermute(share, ('zh', 'zl'), [(i, (i + k) % 4) for i in range(4)])  3.79 us
    ppermute x6, waiting for transfers between devices, swap(): return lax.ppermute(a, axis, [(0, 1), (1, 0)])  3.68 us
    ppermute x6, starting transfers between devices, swap(): return lax.ppermute(a, axis, [(0, 1), (1, 0)])  3.54 us
    ppermute x3, waiting for transfers between devices, body(): lax.ppermute(share, ('zh', 'zl'), [(i, (i + k) % 4) for i in range(4)])  3.52 us
    pallas_call x1, Pallas kernels, spread(): pl.pallas_call(spread_kernel, in_specs=[pl.BlockSpec(memory_space=pl.ANY)...  3.23 us
  transfers between devices with their start and end apart: 9, of which 6 were waited for; matrix products, arithmetic and copies ran while one was open for 0% of the time, Pallas kernels for 12%

profile of v4, /device:TPU:0, one launch (start us, length us, event | category | flops | bytes accessed | tf_op | source)
XLA Modules:
  0.0 151.5 jit_solution(6088037249020304642)
XLA Ops:
  0.0 0.1 pad_add_fusion.place_ref
  0.1 3.2 %spread.1 = f32[16,2,40,512]{3,2,1,0:T(8,128)} custom-call(f32[8,512,128]{2,1,0:T(8,128)} %bitcast.15, f32[8,16,32]{2,1,0:T(8,128)} %pot_hbm.1), custom_call_target="tpu_custom_call" | custom-call | tf_op jit(solution)/shard_map/spread/pallas_call | solution.py:109
  3.3 0.0 copy-start
  3.3 46.7 %all_to_all.35.in_ref = f32[32,40,512]{2,1,0:T(8,128)S(1)} all-to-all(f32[32,40,512]{2,1,0:T(8,128)} %bitcast.14), channel_id=1, replica_groups=mesh['x'=4,'zh'=2,'y'=4,'zl'=2,'c'=2] {'x','zh','y'}, dimensions={0} | all-to-all | bytes 5242880 | tf_op jit(solution)/shard_map/all_to_all | solution.py:403
  50.0 0.0 copy-done
  50.0 7.9 %chebyshev.1 = f32[1024,512]{1,0:T(8,128)S(1)} custom-call(f32[32,40,512]{2,1,0:T(8,128)S(1)} %all_to_all.35.in_ref, bf16[1024,512]{1,0:T(8,128)(2,1)S(1)} %copy-done), custom_call_target="tpu_custom_call" | custom-call | tf_op jit(solution)/shard_map/chebyshev/pallas_call | solution.py:200
  58.0 34.0 %all_to_all.36 = f32[128,8,512]{2,1,0:T(8,128)S(1)} all-to-all(f32[128,8,512]{2,1,0:T(8,128)S(1)} %bitcast.11), channel_id=1, replica_groups=mesh['x'=4,'zh'=2,'y'=4,'zl'=2,'c'=2] {'x','zh','y','zl','c'}, dimensions={0} | all-to-all | bytes 4194304 | tf_op jit(solution)/shard_map/all_to_all | solution.py:403
  92.0 0.6 turn.1
  92.7 0.9 collective-permute-start.1
  93.5 2.0 %gram.1 = (f32[640,128]{1,0:T(8,128)S(1)}, f32[640,128]{1,0:T(8,128)S(1)}) custom-call(s32[2]{0:T(128)S(1)} %pad_add_fusion.place_ref, f32[352,512]{1,0:T(8,128)S(1)} %get-tuple-element.22.near_ref, f32[672,512]{1,0:T(8,128)S(1)} %get-tuple-element.29.far_ref, bf16[512,1024]{1,0:T(8,128)(2,1)S(1)} %get-tuple-element.24.left_ref), custom_call_target="tpu_custom_call" | custom-call | tf_op jit(solution)/shard_map/gram/pallas_call | solution.py:270
  95.5 0.1 collective-permute-start
  95.6 1.6 %collective-permute-done = f32[640,128]{1,0:T(8,128)S(1)} collective-permute-done((f32[640,128]{1,0:T(8,128)S(1)}, f32[640,128]{1,0:T(8,128)S(1)}, u32[]{:S(2)}, u32[]{:S(2)}) %collective-permute-start) | collective-permute-done | bytes 327712 | tf_op jit(solution)/shard_map/ppermute | solution.py:407
  97.3 12.5 %all_to_all.37 = f32[16,40,128]{2,1,0:T(8,128)S(1)} all-to-all(f32[16,40,128]{2,1,0:T(8,128)S(1)} %bitcast.16), channel_id=1, replica_groups=mesh['x'=4,'zh'=2,'y'=4,'zl'=2,'c'=2] {'x','y'}, dimensions={0} | all-to-all | bytes 655360 | tf_op jit(solution)/shard_map/all_to_all | solution.py:403
  109.8 0.1 collective-permute-done.1.near_ref
  110.0 0.9 collective-permute-start.4
  110.9 1.1 collective-permute-start.3
  112.0 1.8 %collective-permute-start.2 = (f32[40,128]{1,0:T(8,128)S(1)}, f32[40,128]{1,0:T(8,128)S(1)}, u32[]{:S(2)}, u32[]{:S(2)}) collective-permute-start(f32[40,128]{1,0:T(8,128)S(1)} %reduce_sum.9), channel_id=1, source_target_pairs={{0,16},{2,18},{16,0},{18,2},{1,17},{3,19},{17,1},{19,3},{4,20},{6,... | collective-permute-start | bytes 61448 | tf_op jit(solution)/shard_map/ppermute | solution.py:424
  113.7 0.0 collective-permute-done.4
  113.8 2.1 %collective-permute-done.3 = f32[40,128]{1,0:T(8,128)S(1)} collective-permute-done((f32[40,128]{1,0:T(8,128)S(1)}, f32[40,128]{1,0:T(8,128)S(1)}, u32[]{:S(2)}, u32[]{:S(2)}) %collective-permute-start.3) | collective-permute-done | bytes 20512 | tf_op jit(solution)/shard_map/ppermute | solution.py:424
  115.9 1.4 collective-permute-done.2
  117.3 1.9 %collective-permute-start.5 = (f32[672,512]{1,0:T(8,128)S(1)}, f32[672,512]{1,0:T(8,128)S(1)}, u32[]{:S(2)}, u32[]{:S(2)}) collective-permute-start(f32[672,512]{1,0:T(8,128)S(1)} %get-tuple-element.29.far_ref), channel_id=1, source_target_pairs={{0,2},{2,0},{1,3},{3,1},{4,6},{6,4},{5,7},{7,5},{8,10},{10,8},{9,1... | collective-permute-start | bytes 4128776 | tf_op jit(solution)/shard_map/ppermute | solution.py:407
  119.2 12.4 %all_to_all.38 = f32[16,40,128]{2,1,0:T(8,128)S(1)} all-to-all(f32[16,40,128]{2,1,0:T(8,128)S(1)} %tile.2), channel_id=1, replica_groups=mesh['x'=4,'zh'=2,'y'=4,'zl'=2,'c'=2] {'x','y'}, dimensions={0} | all-to-all | bytes 655360 | tf_op jit(solution)/shard_map/all_to_all | solution.py:403
  131.6 0.0 collective-permute-start.6
  131.6 1.6 %collective-permute-done.6.other_ref = f32[640,128]{1,0:T(8,128)S(1)} collective-permute-done((f32[640,128]{1,0:T(8,128)S(1)}, f32[640,128]{1,0:T(8,128)S(1)}, u32[]{:S(2)}, u32[]{:S(2)}) %collective-permute-start.6) | collective-permute-done | bytes 327712 | tf_op jit(solution)/shard_map/ppermute | solution.py:407
  133.2 12.0 %inverse_root.1.root_ref = bf16[2,512,256]{2,1,0:T(8,128)(2,1)S(1)} custom-call(s32[2]{0:T(128)S(1)} %pad_add_fusion.place_ref, f32[640,128]{1,0:T(8,128)S(1)} %bitcast.13, f32[640,128]{1,0:T(8,128)S(1)} %collective-permute-done.6.other_ref), custom_call_target="tpu_custom_call" | custom-call | tf_op jit(solution)/shard_map/inverse_root/pallas_call | solution.py:346
  145.2 1.0 whiten.3
  146.2 0.2 collective-permute-start.8
  146.5 0.0 collective-permute-done.5.far_ref
  146.5 1.0 whiten.2
  147.5 0.5 collective-permute-start.7
  147.9 0.3 collective-permute-done.8.refs_2_
  148.2 1.7 %put.2.refs_1_ = f32[2,2,1024,128]{3,2,1,0:T(8,128)} custom-call(s32[2]{0:T(128)S(1)} %pad_add_fusion.place_ref, f32[1024,128]{1,0:T(8,128)S(1)} %get-tuple-element.32.refs_0_, f32[1024,128]{1,0:T(8,128)S(1)} %get-tuple-element.33.refs_1_, f32[1024,128]{1,0:T(8,128)S(1)} %collective-permute-done.8.refs_2_), custom_call_target="tpu_custom_call" | custom-call | tf_op jit(solution)/shard_map/put/pallas_call | solution.py:390
  150.0 0.0 collective-permute-done.7.refs_0_
  150.0 1.4 put.3
  (4 shorter events, 0.1 us)
Async XLA Ops:
  3.3 46.7 %copy-start = (bf16[1024,512]{1,0:T(8,128)(2,1)S(1)}, bf16[1024,512]{1,0:T(8,128)(2,1)}, u32[]{:S(2)}) copy-start(bf16[1024,512]{1,0:T(8,128)(2,1)} %constant.10.clone.ring_ref) | copy-start | bytes 3145732
  92.7 17.3 %collective-permute-start.1 = (f32[352,512]{1,0:T(8,128)S(1)}, f32[352,512]{1,0:T(8,128)S(1)}, u32[]{:S(2)}, u32[]{:S(2)}) collective-permute-start(f32[352,512]{1,0:T(8,128)S(1)} %get-tuple-element.22.near_ref), channel_id=1, source_target_pairs={{0,2},{2,0},{1,3},{3,1},{4,6},{6,4},{5,7},{7,5},{8,10},{10,8},{9,1... | collective-permute-start | bytes 2162696 | tf_op jit(solution)/shard_map/ppermute | solution.py:407
  95.5 1.7 %collective-permute-start = (f32[640,128]{1,0:T(8,128)S(1)}, f32[640,128]{1,0:T(8,128)S(1)}, u32[]{:S(2)}, u32[]{:S(2)}) collective-permute-start(f32[640,128]{1,0:T(8,128)S(1)} %get-tuple-element.26), channel_id=1, source_target_pairs={{0,1},{1,0},{2,3},{3,2},{4,5},{5,4},{6,7},{7,6},{8,9},{9,8},{10,11... | collective-permute-start | bytes 983048 | tf_op jit(solution)/shard_map/ppermute | solution.py:407
  110.0 3.8 %collective-permute-start.4 = (f32[40,128]{1,0:T(8,128)S(1)}, f32[40,128]{1,0:T(8,128)S(1)}, u32[]{:S(2)}, u32[]{:S(2)}) collective-permute-start(f32[40,128]{1,0:T(8,128)S(1)} %reduce_sum.9), channel_id=1, source_target_pairs={{0,18},{2,0},{16,2},{18,16},{1,19},{3,1},{17,3},{19,17},{4,22},{6,... | collective-permute-start | bytes 61448 | tf_op jit(solution)/shard_map/ppermute | solution.py:424
  110.9 5.0 %collective-permute-start.3 = (f32[40,128]{1,0:T(8,128)S(1)}, f32[40,128]{1,0:T(8,128)S(1)}, u32[]{:S(2)}, u32[]{:S(2)}) collective-permute-start(f32[40,128]{1,0:T(8,128)S(1)} %reduce_sum.9), channel_id=1, source_target_pairs={{0,2},{2,16},{16,18},{18,0},{1,3},{3,17},{17,19},{19,1},{4,6},{6,2... | collective-permute-start | bytes 61448 | tf_op jit(solution)/shard_map/ppermute | solution.py:424
  112.0 5.3 %collective-permute-start.2 = (f32[40,128]{1,0:T(8,128)S(1)}, f32[40,128]{1,0:T(8,128)S(1)}, u32[]{:S(2)}, u32[]{:S(2)}) collective-permute-start(f32[40,128]{1,0:T(8,128)S(1)} %reduce_sum.9), channel_id=1, source_target_pairs={{0,16},{2,18},{16,0},{18,2},{1,17},{3,19},{17,1},{19,3},{4,20},{6,... | collective-permute-start | bytes 61448 | tf_op jit(solution)/shard_map/ppermute | solution.py:424
  117.3 29.2 %collective-permute-start.5 = (f32[672,512]{1,0:T(8,128)S(1)}, f32[672,512]{1,0:T(8,128)S(1)}, u32[]{:S(2)}, u32[]{:S(2)}) collective-permute-start(f32[672,512]{1,0:T(8,128)S(1)} %get-tuple-element.29.far_ref), channel_id=1, source_target_pairs={{0,2},{2,0},{1,3},{3,1},{4,6},{6,4},{5,7},{7,5},{8,10},{10,8},{9,1... | collective-permute-start | bytes 4128776 | tf_op jit(solution)/shard_map/ppermute | solution.py:407
  131.6 1.6 %collective-permute-start.6 = (f32[640,128]{1,0:T(8,128)S(1)}, f32[640,128]{1,0:T(8,128)S(1)}, u32[]{:S(2)}, u32[]{:S(2)}) collective-permute-start(f32[640,128]{1,0:T(8,128)S(1)} %bitcast.12), channel_id=1, source_target_pairs={{0,1},{1,0},{2,3},{3,2},{4,5},{5,4},{6,7},{7,6},{8,9},{9,8},{10,11... | collective-permute-start | bytes 983048 | tf_op jit(solution)/shard_map/ppermute | solution.py:407
  146.2 2.0 %collective-permute-start.8 = (f32[1024,128]{1,0:T(8,128)S(1)}, f32[1024,128]{1,0:T(8,128)S(1)}, u32[]{:S(2)}, u32[]{:S(2)}) collective-permute-start(f32[1024,128]{1,0:T(8,128)S(1)} %get-tuple-element.34), channel_id=1, source_target_pairs={{0,1},{1,0},{2,3},{3,2},{4,5},{5,4},{6,7},{7,6},{8,9},{9,8},{10,11... | collective-permute-start | bytes 1572872 | tf_op jit(solution)/shard_map/ppermute | solution.py:407
  147.5 2.5 %collective-permute-start.7 = (f32[1024,128]{1,0:T(8,128)S(1)}, f32[1024,128]{1,0:T(8,128)S(1)}, u32[]{:S(2)}, u32[]{:S(2)}) collective-permute-start(f32[1024,128]{1,0:T(8,128)S(1)} %get-tuple-element.31), channel_id=1, source_target_pairs={{0,1},{1,0},{2,3},{3,2},{4,5},{5,4},{6,7},{7,6},{8,9},{9,8},{10,11... | collective-permute-start | bytes 1572872 | tf_op jit(solution)/shard_map/ppermute | solution.py:407

commit v5 on v4

--- a/solution.py
+++ b/solution.py
@@ -71,41 +71,55 @@
     return dot(a[0], b[0]) + (dot(a[0], b[1]) + dot(a[1], b[0]))
 
 
+FIELD_ROWS = 128
+POT_ROWS = 16
+MESSAGE = FIELD_ROWS + POT_ROWS
+
+
 def spread_kernel(v_hbm, pot_hbm, out_hbm, v_ref, pot_ref, out_ref, in_sems, out_sems):
+    pot_load = pltpu.make_async_copy(pot_hbm, pot_ref, in_sems.at[SLAB])
+    pot_load.start()
     loads = [
         pltpu.make_async_copy(v_hbm.at[x], v_ref.at[x], in_sems.at[x]) for x in range(SLAB)
     ]
-    loads.append(pltpu.make_async_copy(pot_hbm, pot_ref, in_sems.at[SLAB]))
     for load in loads:
         load.start()
 
     def store(t):
-        rows = pl.ds(8 * t, 8)
+        rows = pl.ds(32 * t, 32 if t < 4 else POT_ROWS)
         return pltpu.make_async_copy(
             out_ref.at[:, :, rows], out_hbm.at[:, :, rows], out_sems.at[t]
         )
 
+    pot_load.wait()
+    pot = jnp.concatenate([pot_ref[:, y, :] for y in range(NY)], axis=1)
+    half = jnp.where(lax.axis_index("c") == 0, pot[:4], pot[4:])
+    for k in range(2):
+        tile = jnp.concatenate(
+            [half[:, 256 * k + 128 * u : 256 * k + 128 * (u + 1)] for u in range(2)], axis=0
+        )
+        rows = pl.ds(FIELD_ROWS + 8 * k, 8)
+        out_ref[:, :, rows, :] = jnp.broadcast_to(tile, (16, 2, 8, 128))
+    store(4).start()
     for t in range(4):
         loads[2 * t].wait()
         loads[2 * t + 1].wait()
         a = v_ref[2 * t].T.reshape(16, 8, PLANE)
         b = v_ref[2 * t + 1].T.reshape(16, 8, PLANE)
         low = low_rows(a.shape)
-        rows = pl.ds(8 * t, 8)
-        out_ref[:, 0, rows, :] = jnp.where(low, a, swap_halves(b))
-        out_ref[:, 1, rows, :] = jnp.where(low, swap_halves(a), b)
+        even = jnp.where(low, a, swap_halves(b))
+        odd = jnp.where(low, swap_halves(a), b)
+        for k in range(4):
+            rows, lanes = pl.ds(32 * t + 8 * k, 8), slice(128 * k, 128 * (k + 1))
+            out_ref[:, 0, rows, :] = even[:, :, lanes]
+            out_ref[:, 1, rows, :] = odd[:, :, lanes]
         store(t).start()
-        if t == 0:
-            loads[SLAB].wait()
-            pot = jnp.concatenate([pot_ref[:, y, :] for y in range(NY)], axis=1)
-            out_ref[:, :, 32:40, :] = jnp.broadcast_to(pot, (16, 2, SLAB, PLANE))
-            store(4).start()
     for t in range(5):
         store(t).wait()
 
 
 def spread(field, potential):
-    shape = (16, 2, 40, PLANE)
+    shape = (16, 2, MESSAGE, 128)
     out = pl.pallas_call(
         spread_kernel,
         in_specs=[pl.BlockSpec(memory_space=pl.ANY)] * 2,
@@ -121,7 +135,7 @@
         compiler_params=pltpu.CompilerParams(vmem_limit_bytes=VMEM_SPREAD),
         name="spread",
     )(field, potential)
-    return out.reshape(32 * 40, PLANE)
+    return out.reshape(32 * MESSAGE, 128)
 
 
 ROWS = 4 * NX
@@ -129,18 +143,85 @@
 CHUNK = 256
 
 
-def filter_kernel(in_ref, ring_ref, out_ref, one_ref, two_ref, diag_ref, sems):
+CHUNKS = ROWS // CHUNK
+PARTS = 32 // CHUNKS
+
+
+def neighbours(wide, ring):
+    near = dot(jnp.concatenate(split(wide[EDGE : EDGE + CHUNK]), axis=1), ring)
+    half = pltpu.roll(wide, 4, 0)
+
+    def at(a, shift):
+        return a[EDGE + shift : EDGE + shift + CHUNK]
+
+    along = (
+        STENCIL[0] * (at(half, 0) + at(half, 8))
+        + STENCIL[1] * (at(wide, 8) + at(wide, -8))
+        + (at(half, -8) + at(half, 16))
+    )
+    return near + along
+
+
+def gather_kernel(in_ref, ring_ref, field_ref, sum_ref):
+    def planes(s, first, count):
+        tiles = in_ref[s, 32 * first : 32 * (first + count), :].reshape(-1, count, 4, 8, 128)
+        return jnp.concatenate(
+            [tiles[:, :, k].reshape(-1, 128) for k in range(4)], axis=1
+        )
+
+    ring = ring_ref[...]
+    for i in range(CHUNKS):
+        before, after = (PARTS * i - 1) % 32, PARTS * (i + 1) % 32
+        middle = planes(slice(PARTS * i, PARTS * (i + 1)), 0, 4)
+        wide = jnp.concatenate(
+            [
+                planes(slice(before, before + 1), 2, 2),
+                middle,
+                planes(slice(after, after + 1), 0, 2),
+            ],
+            axis=0,
+        )
+        rows = pl.ds(CHUNK * i, CHUNK)
+        field_ref[rows, :] = middle
+        sum_ref[rows, :] = neighbours(wide, ring)
+
+
+def gather(messages, ring):
+    return pl.pallas_call(
+        gather_kernel,
+        out_shape=(jax.ShapeDtypeStruct((ROWS, PLANE), F32),) * 2,
+        compiler_params=pltpu.CompilerParams(vmem_limit_bytes=VMEM),
+        name="gather",
+    )(messages, ring)
+
+
+def filter_kernel(
+    place_ref, field_ref, sum_ref, mine_ref, other_ref, ring_ref,
+    out_ref, one_ref, two_ref, diag_ref, sems,
+):
+    c = place_ref[1]
+
     def fill(s, _):
         base = pl.multiple_of(s * 32, 32)
-        one_ref[pl.ds(EDGE + base, 32), :] = in_ref[s, 0:32, :]
-        pot = in_ref[s, 32:40, :]
-        low = low_rows((8, PLANE))
-        for t in range(4):
-            row = jnp.where(low, pot[2 * t : 2 * t + 1], pot[2 * t + 1 : 2 * t + 2])
-            diag_ref[pl.ds(base + 8 * t, 8), :] = 0.5 * row + 2.0 * DIAGONAL
+        mine, other = mine_ref[s], other_ref[s]
+        low = low_rows((8, 128))
+        for h in range(2):
+            pot = 0.5 * jnp.where(c == h, mine, other) + 2.0 * DIAGONAL
+            for t in range(2):
+                tiles = []
+                for k in range(4):
+                    at = 8 * (k // 2) + 4 * (k % 2) + 2 * t
+                    tiles.append(jnp.where(low, pot[at : at + 1], pot[at + 1 : at + 2]))
+                diag = jnp.concatenate(tiles, axis=1)
+                at = base + 16 * h + 8 * t
+                rows = pl.ds(at, 8)
+                diag_ref[rows, :] = diag
+                one_ref[pl.ds(EDGE + at, 8), :] = (
+                    UNIT * sum_ref[rows, :] + 0.5 * diag * field_ref[rows, :]
+                )
         return 0
 
-    lax.fori_loop(0, 32, fill, 0)
+    lax.fori_loop(0, 32, fill, 0, unroll=4)
     ring = ring_ref[...]
 
     def close(ref):
@@ -150,66 +231,58 @@
     def twice(cur_ref, base):
         wide = cur_ref[pl.ds(base, CHUNK + 2 * EDGE), :]
         cur = wide[EDGE : EDGE + CHUNK]
-        near = dot(jnp.concatenate(split(cur), axis=1), ring)
-        half = pltpu.roll(wide, 4, 0)
-
-        def at(a, shift):
-            return a[EDGE + shift : EDGE + shift + CHUNK]
-
-        along = (
-            STENCIL[0] * (at(half, 0) + at(half, 8))
-            + STENCIL[1] * (at(wide, 8) + at(wide, -8))
-            + (at(half, -8) + at(half, 16))
-        )
-        return (2.0 * UNIT) * (near + along) + diag_ref[pl.ds(base, CHUNK), :] * cur
-
-    def sweep(body):
-        for i in range(ROWS // CHUNK):
-            body(i * CHUNK)
-
-    def copy(ref, base):
+        return (2.0 * UNIT) * neighbours(wide, ring) + diag_ref[pl.ds(base, CHUNK), :] * cur
+
+    def copy(base):
         return pltpu.make_async_copy(
-            ref.at[pl.ds(EDGE + base, CHUNK)],
+            two_ref.at[pl.ds(EDGE + base, CHUNK)],
             out_ref.at[pl.ds(base, CHUNK)],
             sems.at[base // CHUNK],
         )
 
+    def sweep(body):
+        for i in range(CHUNKS):
+            body(i * CHUNK)
+
+    def second(base):
+        two_ref[pl.ds(EDGE + base, CHUNK), :] = (
+            twice(one_ref, base) - field_ref[pl.ds(base, CHUNK), :]
+        )
+
+    def third(base):
+        rows = pl.ds(EDGE + base, CHUNK)
+        one_ref[rows, :] = twice(two_ref, base) - one_ref[rows, :]
+
+    def fourth(base):
+        rows = pl.ds(EDGE + base, CHUNK)
+        two_ref[rows, :] = twice(one_ref, base) - two_ref[rows, :]
+        copy(base).start()
+
     close(one_ref)
-
-    def first(base):
-        two_ref[pl.ds(EDGE + base, CHUNK), :] = 0.5 * twice(one_ref, base)
-
-    sweep(first)
-    previous, current = one_ref, two_ref
-    for degree_step in range(2, DEGREE + 1):
-        close(current)
-        last = degree_step == DEGREE
-
-        def following(base, previous=previous, current=current, last=last):
-            rows = pl.ds(EDGE + base, CHUNK)
-            previous[rows, :] = twice(current, base) - previous[rows, :]
-            if last:
-                copy(previous, base).start()
-
-        sweep(following)
-        previous, current = current, previous
-    sweep(lambda base: copy(current, base).wait())
-
-
-def chebyshev(spread_cells, ring):
+    for body, ref in ((second, two_ref), (third, one_ref)):
+        sweep(body)
+        close(ref)
+    sweep(fourth)
+    sweep(lambda base: copy(base).wait())
+
+
+def chebyshev(place, field, partial_sum, mine, other, ring):
+    smem = pl.BlockSpec(memory_space=pltpu.SMEM)
+    vmem = pl.BlockSpec(memory_space=pltpu.VMEM)
     return pl.pallas_call(
         filter_kernel,
+        in_specs=[smem] + [vmem] * 5,
         out_shape=jax.ShapeDtypeStruct((ROWS, PLANE), F32),
         scratch_shapes=[
             pltpu.VMEM((ROWS + 2 * EDGE, PLANE), F32),
             pltpu.VMEM((ROWS + 2 * EDGE, PLANE), F32),
             pltpu.VMEM((ROWS, PLANE), F32),
-            pltpu.SemaphoreType.DMA((ROWS // CHUNK,)),
+            pltpu.SemaphoreType.DMA((CHUNKS,)),
         ],
         out_specs=pl.BlockSpec(memory_space=pltpu.HBM),
         compiler_params=pltpu.CompilerParams(vmem_limit_bytes=VMEM),
         name="chebyshev",
-    )(spread_cells.reshape(32, 40, PLANE), ring)
+    )(place, field, partial_sum, mine, other, ring)
 
 
 BLOCKS = tuple((i, j) for i in range(4) for j in range(i, 4))
@@ -352,47 +425,58 @@
     )(place, mine, other)
 
 
-def whiten_kernel(near_ref, far_ref, root_ref, ours_ref, theirs_ref):
+def whiten_kernel(*refs):
+    chunks, root_ref, ours_ref, theirs_ref = refs[:-3], refs[-3], refs[-2], refs[-1]
     root = (root_ref[0], root_ref[1])
-    for ref, rows in ((near_ref, pl.ds(0, PART)), (far_ref, pl.ds(PART, 2 * PLANE - PART))):
+    start = 0
+    for ref in chunks:
         white = dot_wide(split(ref[...]), root)
+        rows = pl.ds(start, ref.shape[0])
         ours_ref[rows, :] = white[:, :128]
         theirs_ref[rows, :] = white[:, 128:]
-
-
-def whiten(near, far, root):
+        start += ref.shape[0]
+
+
+def whiten(chunks, root):
+    rows = sum(chunk.shape[0] for chunk in chunks)
     return pl.pallas_call(
         whiten_kernel,
-        out_shape=(jax.ShapeDtypeStruct((2 * PLANE, 128), F32),) * 2,
+        out_shape=(jax.ShapeDtypeStruct((rows, 128), F32),) * 2,
         compiler_params=pltpu.CompilerParams(vmem_limit_bytes=VMEM_SMALL),
         name="whiten",
-    )(near, far, root)
+    )(*chunks, root)
 
 
 WHOLE = jax.ShapeDtypeStruct((2, 2, 2 * PLANE, 128), F32)
 
 
-def place_kernel(slots, place_ref, *refs):
-    parts, whole_ref, sems = refs[: len(slots)], refs[-2], refs[-1]
+def place_kernel(jobs, place_ref, *refs):
+    whole_ref, sems = refs[-2], refs[-1]
     copies = []
-    for k, (zl_flip, c_flip) in enumerate(slots):
-        zl = 1 - place_ref[0] if zl_flip else place_ref[0]
-        c = 1 - place_ref[1] if c_flip else place_ref[1]
-        copies.append(pltpu.make_async_copy(parts[k], whole_ref.at[zl, c], sems.at[k]))
+    for k, (part, source, rows, other_chip, other_core, at) in enumerate(jobs):
+        zl = 1 - place_ref[0] if other_chip else place_ref[0]
+        c = 1 - place_ref[1] if other_core else place_ref[1]
+        copies.append(
+            pltpu.make_async_copy(
+                refs[part].at[pl.ds(source, rows)],
+                whole_ref.at[zl, c, pl.ds(at, rows)],
+                sems.at[k],
+            )
+        )
     for copy in copies:
         copy.start()
     for copy in copies:
         copy.wait()
 
 
-def put(place, slots, parts, whole=None):
+def put(place, jobs, parts, whole=None):
     aliased = () if whole is None else (whole,)
     return pl.pallas_call(
-        functools.partial(place_kernel, slots),
+        functools.partial(place_kernel, jobs),
         in_specs=[SCALARS] + [ANYWHERE] * (len(parts) + len(aliased)),
         out_specs=ANYWHERE,
         out_shape=WHOLE,
-        scratch_shapes=[pltpu.SemaphoreType.DMA((len(parts),))],
+        scratch_shapes=[pltpu.SemaphoreType.DMA((len(jobs),))],
         input_output_aliases={1 + len(parts): 0} if aliased else {},
         compiler_params=pltpu.CompilerParams(vmem_limit_bytes=VMEM_SMALL),
         name="put",
@@ -412,7 +496,11 @@
     ring = jnp.asarray(np.tile(plane_stencil(), (2, 1)), BF16)
     sent = spread(orbitals.reshape(SLAB, PLANE, 128), potential)
     sent, place = lax.optimization_barrier((sent, place))
-    filtered = chebyshev(exchange(sent, SPACE), ring)
+    messages = exchange(sent, SPACE).reshape(32, MESSAGE, 128)
+    half = messages[:, FIELD_ROWS:]
+    other_half = swap(half, "c")
+    field, partial_sum = gather(messages, ring)
+    filtered = chebyshev(place, field, partial_sum, half, other_half, ring)
     near, far, left = turn(exchange(filtered, EVERY))
     mine, other = gram(place, near, far, left)
 
@@ -429,13 +517,21 @@
     total = exchange(jnp.tile(share, (16, 1)), ("x", "y"))
     root = inverse_root(place, total, swap(total, "c"))
 
-    ours, theirs = whiten(near, far, root)
+    ours, theirs = whiten((near, far, other_near), root)
     first = swap(theirs, "c")
-    other_ours, other_theirs = whiten(other_near, other_far, root)
-    second = swap(other_theirs, "c")
-    slots = ((False, False), (True, False), (False, True))
-    whole = put(place, slots, (ours, other_ours, first))
-    whitened = put(place, ((True, True),), (second,), whole)
+    late_ours, late_theirs = whiten((other_far,), root)
+    second = swap(late_theirs, "c")
+    chunk, late = 2 * PLANE, 2 * PLANE - PART
+    jobs = tuple(
+        job
+        for part, other_core in ((0, False), (2, True))
+        for job in (
+            (part, 0, chunk, False, other_core, 0),
+            (part, chunk, PART, True, other_core, 0),
+        )
+    )
+    whole = put(place, jobs + ((1, 0, late, True, False, PART),), (ours, late_ours, first))
+    whitened = put(place, ((0, 0, late, True, True, PART),), (second,), whole)
     return whitened.reshape(orbitals.shape)
 
 

time: 153 us -> 149 us (0.974)
  blocking collectives: 106 us -> 103 us
    all_to_all x4, blocking collectives: 106 us -> 103 us  [exchange(): return lax.all_to_all(a, axes, 0, 0, tiled=True)]
    ppermute x3, waiting for transfers between devices: 3.52 us -> 1.76 us  [body(): lax.ppermute(share, ('zh', 'zl'), [(i, (i + k) % 4) for i in range(4)])]
    ppermute x6 -> x7, starting transfers between devices: 3.54 us -> 2.57 us  [swap(): return lax.ppermute(a, axis, [(0, 1), (1, 0)])]
    ppermute x6 -> x7, waiting for transfers between devices: 3.68 us -> 4.61 us  [swap(): return lax.ppermute(a, axis, [(0, 1), (1, 0)])]
    pallas_call x5 -> x6, Pallas kernels: 13 us -> 13.5 us  [the longest x1 6.91 us: chebyshev(): pl.pallas_call(filter_kernel, in_specs=[smem] + [vmem] * 5, out_shape=jax...]
  transfers between devices with their start and end apart: 9 -> 10, of which waited for: 6 -> 7; matrix products, arithmetic and copies ran while one was open for 0% -> 0% of each run, Pallas kernels for 12% -> 13%
where the time goes in v5:
time: 149 us; the launch traced here: 148 us
  blocking collectives  103 us (69%)
  Pallas kernels  31 us (21%)
  starting transfers between devices  7.22 us (5%)
  waiting for transfers between devices  6.37 us (4%)
    all_to_all x4, blocking collectives, exchange(): return lax.all_to_all(a, axes, 0, 0, tiled=True)  103 us
    pallas_call x1, Pallas kernels, inverse_root(): pl.pallas_call(root_kernel, in_specs=[SCALARS, VECTORS, VECTORS], out_sha...  12 us
    pallas_call x1, Pallas kernels, chebyshev(): pl.pallas_call(filter_kernel, in_specs=[smem] + [vmem] * 5, out_shape=jax...  6.91 us
    ppermute x3, starting transfers between devices, body(): lax.ppermute(share, ('zh', 'zl'), [(i, (i + k) % 4) for i in range(4)])  4.66 us
    ppermute x7, waiting for transfers between devices, swap(): return lax.ppermute(a, axis, [(0, 1), (1, 0)])  4.61 us
    pallas_call x2, Pallas kernels, put(): pl.pallas_call(functools.partial(place_kernel, jobs), in_specs=[SCALARS]...  3.07 us
  transfers between devices with their start and end apart: 10, of which 7 were waited for; matrix products, arithmetic and copies ran while one was open for 0% of the time, Pallas kernels for 13%

profile of v5, /device:TPU:0, one launch (start us, length us, event | category | flops | bytes accessed | tf_op | source)
XLA Modules:
  0.0 148.1 jit_solution(16210695314998333283)
XLA Ops:
  0.0 0.1 pad_add_fusion.place_ref
  0.1 2.9 %spread.1 = f32[16,2,144,128]{3,2,1,0:T(8,128)} custom-call(f32[8,512,128]{2,1,0:T(8,128)} %bitcast.15, f32[8,16,32]{2,1,0:T(8,128)} %pot_hbm.1), custom_call_target="tpu_custom_call" | custom-call | tf_op jit(solution)/shard_map/spread/pallas_call | solution.py:123
  2.9 0.0 copy-start
  3.0 44.1 %all_to_all.35.in_ref = f32[32,144,128]{2,1,0:T(8,128)S(1)} all-to-all(f32[32,144,128]{2,1,0:T(8,128)} %bitcast.14), channel_id=1, replica_groups=mesh['x'=4,'zh'=2,'y'=4,'zl'=2,'c'=2] {'x','zh','y'}, dimensions={0} | all-to-all | bytes 4718592 | tf_op jit(solution)/shard_map/all_to_all | solution.py:487
  47.1 0.1 collective-permute-start
  47.2 0.0 copy-done
  47.2 1.5 %gather.1 = (f32[1024,512]{1,0:T(8,128)S(1)}, f32[1024,512]{1,0:T(8,128)S(1)}) custom-call(f32[32,144,128]{2,1,0:T(8,128)S(1)} %all_to_all.35.in_ref, bf16[1024,512]{1,0:T(8,128)(2,1)S(1)} %copy-done), custom_call_target="tpu_custom_call" | custom-call | tf_op jit(solution)/shard_map/gather/pallas_call | solution.py:190
  48.8 0.0 collective-permute-done.other_ref
  48.8 6.9 %chebyshev.1 = f32[1024,512]{1,0:T(8,128)S(1)} custom-call(s32[2]{0:T(128)S(1)} %pad_add_fusion.place_ref, f32[1024,512]{1,0:T(8,128)S(1)} %get-tuple-element.24.field_ref, f32[1024,512]{1,0:T(8,128)S(1)} %get-tuple-element.25.sum_ref, f32[32,16,128]{2,1,0:T(8,128)S(1)} %slice.4.mine_ref, f32[32,16,128]{2,1,0:T(8,128)S(1)} %collective-permute-done.other_ref, ...), custom_call_target="tpu_custom_call" | custom-call | tf_op jit(solution)/shard_map/chebyshev/pallas_call | solution.py:272
  55.7 34.1 %all_to_all.36 = f32[128,8,512]{2,1,0:T(8,128)S(1)} all-to-all(f32[128,8,512]{2,1,0:T(8,128)S(1)} %bitcast.11), channel_id=1, replica_groups=mesh['x'=4,'zh'=2,'y'=4,'zl'=2,'c'=2] {'x','zh','y','zl','c'}, dimensions={0} | all-to-all | bytes 4194304 | tf_op jit(solution)/shard_map/all_to_all | solution.py:487
  89.7 0.6 turn.1
  90.4 0.9 collective-permute-start.2
  91.3 2.0 %gram.1 = (f32[640,128]{1,0:T(8,128)S(1)}, f32[640,128]{1,0:T(8,128)S(1)}) custom-call(s32[2]{0:T(128)S(1)} %pad_add_fusion.place_ref, f32[352,512]{1,0:T(8,128)S(1)} %get-tuple-element.26.near_ref.refs_0_, f32[672,512]{1,0:T(8,128)S(1)} %get-tuple-element.32.far_ref.refs_1_, bf16[512,1024]{1,0:T(8,128)(2,1)S(1)} %get-tuple-element.28.left_ref), custom_call_target="tpu_custom_call" | custom-call | tf_op jit(solution)/shard_map/gram/pallas_call | solution.py:343
  93.2 0.1 collective-permute-start.1
  93.3 1.6 %collective-permute-done.1 = f32[640,128]{1,0:T(8,128)S(1)} collective-permute-done((f32[640,128]{1,0:T(8,128)S(1)}, f32[640,128]{1,0:T(8,128)S(1)}, u32[]{:S(2)}, u32[]{:S(2)}) %collective-permute-start.1) | collective-permute-done | bytes 327712 | tf_op jit(solution)/shard_map/ppermute | solution.py:491
  95.0 12.5 %all_to_all.37 = f32[16,40,128]{2,1,0:T(8,128)S(1)} all-to-all(f32[16,40,128]{2,1,0:T(8,128)S(1)} %bitcast.16), channel_id=1, replica_groups=mesh['x'=4,'zh'=2,'y'=4,'zl'=2,'c'=2] {'x','y'}, dimensions={0} | all-to-all | bytes 655360 | tf_op jit(solution)/shard_map/all_to_all | solution.py:487
  107.5 0.1 collective-permute-done.2.refs_2_
  107.7 1.4 collective-permute-start.3
  109.1 0.4 collective-permute-start.4
  109.5 2.8 %collective-permute-start.5 = (f32[40,128]{1,0:T(8,128)S(1)}, f32[40,128]{1,0:T(8,128)S(1)}, u32[]{:S(2)}, u32[]{:S(2)}) collective-permute-start(f32[40,128]{1,0:T(8,128)S(1)} %reduce_sum.9), channel_id=1, source_target_pairs={{0,18},{2,0},{16,2},{18,16},{1,19},{3,1},{17,3},{19,17},{4,22},{6,... | collective-permute-start | bytes 61448 | tf_op jit(solution)/shard_map/ppermute | solution.py:512
  112.3 0.6 collective-permute-done.3
  113.0 1.1 collective-permute-done.4
  114.1 0.0 collective-permute-done.5
  114.1 1.2 collective-permute-start.6
  115.4 12.3 %all_to_all.38 = f32[16,40,128]{2,1,0:T(8,128)S(1)} all-to-all(f32[16,40,128]{2,1,0:T(8,128)S(1)} %tile.2), channel_id=1, replica_groups=mesh['x'=4,'zh'=2,'y'=4,'zl'=2,'c'=2] {'x','y'}, dimensions={0} | all-to-all | bytes 655360 | tf_op jit(solution)/shard_map/all_to_all | solution.py:487
  127.7 0.0 collective-permute-start.7
  127.7 1.6 %collective-permute-done.7.other_ref = f32[640,128]{1,0:T(8,128)S(1)} collective-permute-done((f32[640,128]{1,0:T(8,128)S(1)}, f32[640,128]{1,0:T(8,128)S(1)}, u32[]{:S(2)}, u32[]{:S(2)}) %collective-permute-start.7) | collective-permute-done | bytes 327712 | tf_op jit(solution)/shard_map/ppermute | solution.py:491
  129.3 12.0 %inverse_root.1.refs_1_.refs_3_ = bf16[2,512,256]{2,1,0:T(8,128)(2,1)S(1)} custom-call(s32[2]{0:T(128)S(1)} %pad_add_fusion.place_ref, f32[640,128]{1,0:T(8,128)S(1)} %bitcast.13, f32[640,128]{1,0:T(8,128)S(1)} %collective-permute-done.7.other_ref), custom_call_target="tpu_custom_call" | custom-call | tf_op jit(solution)/shard_map/inverse_root/pallas_call | solution.py:419
  141.3 1.3 whiten.3
  142.6 0.2 collective-permute-start.9
  142.8 0.6 collective-permute-done.6.refs_0_
  143.5 0.7 whiten.2
  144.2 0.1 collective-permute-start.8
  144.3 0.6 collective-permute-done.9.refs_2_
  144.9 1.8 %put.2.refs_1_ = f32[2,2,1024,128]{3,2,1,0:T(8,128)} custom-call(s32[2]{0:T(128)S(1)} %pad_add_fusion.place_ref, f32[1376,128]{1,0:T(8,128)S(1)} %get-tuple-element.36.refs_0_, f32[672,128]{1,0:T(8,128)S(1)} %get-tuple-element.37.refs_1_, f32[1376,128]{1,0:T(8,128)S(1)} %collective-permute-done.9.refs_2_), custom_call_target="tpu_custom_call" | custom-call | tf_op jit(solution)/shard_map/put/pallas_call | solution.py:474
  146.6 0.0 collective-permute-done.8.refs_0_
  146.7 1.3 put.3
  (5 shorter events, 0.1 us)
Async XLA Ops:
  2.9 44.3 %copy-start = (bf16[1024,512]{1,0:T(8,128)(2,1)S(1)}, bf16[1024,512]{1,0:T(8,128)(2,1)}, u32[]{:S(2)}) copy-start(bf16[1024,512]{1,0:T(8,128)(2,1)} %constant.10.clone.ring_ref) | copy-start | bytes 3145732
  47.1 1.6 %collective-permute-start = (f32[32,16,128]{2,1,0:T(8,128)S(1)}, f32[32,16,128]{2,1,0:T(8,128)S(1)}, u32[]{:S(2)}, u32[]{:S(2)}) collective-permute-start(f32[32,16,128]{2,1,0:T(8,128)S(1)} %slice.4.mine_ref), channel_id=1, source_target_pairs={{0,1},{1,0},{2,3},{3,2},{4,5},{5,4},{6,7},{7,6},{8,9},{9,8},{10,11... | collective-permute-start | bytes 786440 | tf_op jit(solution)/shard_map/ppermute | solution.py:491
  90.4 17.3 %collective-permute-start.2 = (f32[352,512]{1,0:T(8,128)S(1)}, f32[352,512]{1,0:T(8,128)S(1)}, u32[]{:S(2)}, u32[]{:S(2)}) collective-permute-start(f32[352,512]{1,0:T(8,128)S(1)} %get-tuple-element.26.near_ref.refs_0_), channel_id=1, source_target_pairs={{0,2},{2,0},{1,3},{3,1},{4,6},{6,4},{5,7},{7,5},{8,10},{10,8},{9,1... | collective-permute-start | bytes 2162696 | tf_op jit(solution)/shard_map/ppermute | solution.py:491
  93.2 1.7 %collective-permute-start.1 = (f32[640,128]{1,0:T(8,128)S(1)}, f32[640,128]{1,0:T(8,128)S(1)}, u32[]{:S(2)}, u32[]{:S(2)}) collective-permute-start(f32[640,128]{1,0:T(8,128)S(1)} %get-tuple-element.30), channel_id=1, source_target_pairs={{0,1},{1,0},{2,3},{3,2},{4,5},{5,4},{6,7},{7,6},{8,9},{9,8},{10,11... | collective-permute-start | bytes 983048 | tf_op jit(solution)/shard_map/ppermute | solution.py:491
  107.7 5.3 %collective-permute-start.3 = (f32[40,128]{1,0:T(8,128)S(1)}, f32[40,128]{1,0:T(8,128)S(1)}, u32[]{:S(2)}, u32[]{:S(2)}) collective-permute-start(f32[40,128]{1,0:T(8,128)S(1)} %reduce_sum.9), channel_id=1, source_target_pairs={{0,16},{2,18},{16,0},{18,2},{1,17},{3,19},{17,1},{19,3},{4,20},{6,... | collective-permute-start | bytes 61448 | tf_op jit(solution)/shard_map/ppermute | solution.py:512
  109.1 5.0 %collective-permute-start.4 = (f32[40,128]{1,0:T(8,128)S(1)}, f32[40,128]{1,0:T(8,128)S(1)}, u32[]{:S(2)}, u32[]{:S(2)}) collective-permute-start(f32[40,128]{1,0:T(8,128)S(1)} %reduce_sum.9), channel_id=1, source_target_pairs={{0,2},{2,16},{16,18},{18,0},{1,3},{3,17},{17,19},{19,1},{4,6},{6,2... | collective-permute-start | bytes 61448 | tf_op jit(solution)/shard_map/ppermute | solution.py:512
  109.5 4.6 %collective-permute-start.5 = (f32[40,128]{1,0:T(8,128)S(1)}, f32[40,128]{1,0:T(8,128)S(1)}, u32[]{:S(2)}, u32[]{:S(2)}) collective-permute-start(f32[40,128]{1,0:T(8,128)S(1)} %reduce_sum.9), channel_id=1, source_target_pairs={{0,18},{2,0},{16,2},{18,16},{1,19},{3,1},{17,3},{19,17},{4,22},{6,... | collective-permute-start | bytes 61448 | tf_op jit(solution)/shard_map/ppermute | solution.py:512
  114.1 29.4 %collective-permute-start.6 = (f32[672,512]{1,0:T(8,128)S(1)}, f32[672,512]{1,0:T(8,128)S(1)}, u32[]{:S(2)}, u32[]{:S(2)}) collective-permute-start(f32[672,512]{1,0:T(8,128)S(1)} %get-tuple-element.32.far_ref.refs_1_), channel_id=1, source_target_pairs={{0,2},{2,0},{1,3},{3,1},{4,6},{6,4},{5,7},{7,5},{8,10},{10,8},{9,1... | collective-permute-start | bytes 4128776 | tf_op jit(solution)/shard_map/ppermute | solution.py:491
  127.7 1.6 %collective-permute-start.7 = (f32[640,128]{1,0:T(8,128)S(1)}, f32[640,128]{1,0:T(8,128)S(1)}, u32[]{:S(2)}, u32[]{:S(2)}) collective-permute-start(f32[640,128]{1,0:T(8,128)S(1)} %bitcast.12), channel_id=1, source_target_pairs={{0,1},{1,0},{2,3},{3,2},{4,5},{5,4},{6,7},{7,6},{8,9},{9,8},{10,11... | collective-permute-start | bytes 983048 | tf_op jit(solution)/shard_map/ppermute | solution.py:491
  142.6 2.2 %collective-permute-start.9 = (f32[1376,128]{1,0:T(8,128)S(1)}, f32[1376,128]{1,0:T(8,128)S(1)}, u32[]{:S(2)}, u32[]{:S(2)}) collective-permute-start(f32[1376,128]{1,0:T(8,128)S(1)} %get-tuple-element.38), channel_id=1, source_target_pairs={{0,1},{1,0},{2,3},{3,2},{4,5},{5,4},{6,7},{7,6},{8,9},{9,8},{10,11... | collective-permute-start | bytes 2113544 | tf_op jit(solution)/shard_map/ppermute | solution.py:491
  144.2 2.5 %collective-permute-start.8 = (f32[672,128]{1,0:T(8,128)S(1)}, f32[672,128]{1,0:T(8,128)S(1)}, u32[]{:S(2)}, u32[]{:S(2)}) collective-permute-start(f32[672,128]{1,0:T(8,128)S(1)} %get-tuple-element.34), channel_id=1, source_target_pairs={{0,1},{1,0},{2,3},{3,2},{4,5},{5,4},{6,7},{7,6},{8,9},{9,8},{10,11... | collective-permute-start | bytes 1032200 | tf_op jit(solution)/shard_map/ppermute | solution.py:491

commit v6 on v5

--- a/solution.py
+++ b/solution.py
@@ -140,26 +140,32 @@
 
 ROWS = 4 * NX
 EDGE = 16
-CHUNK = 256
+CHUNK = 512
 
 
 CHUNKS = ROWS // CHUNK
 PARTS = 32 // CHUNKS
 
 
-def neighbours(wide, ring):
-    near = dot(jnp.concatenate(split(wide[EDGE : EDGE + CHUNK]), axis=1), ring)
+SUB = 128
+
+
+def beside(wide, count):
     half = pltpu.roll(wide, 4, 0)
 
     def at(a, shift):
-        return a[EDGE + shift : EDGE + shift + CHUNK]
-
-    along = (
+        return a[EDGE + shift : EDGE + shift + count]
+
+    return (
         STENCIL[0] * (at(half, 0) + at(half, 8))
         + STENCIL[1] * (at(wide, 8) + at(wide, -8))
         + (at(half, -8) + at(half, 16))
     )
-    return near + along
+
+
+def neighbours(wide, ring):
+    near = dot(jnp.concatenate(split(wide[EDGE : EDGE + CHUNK]), axis=1), ring)
+    return near + beside(wide, CHUNK)
 
 
 def gather_kernel(in_ref, ring_ref, field_ref, sum_ref):
@@ -221,17 +227,30 @@
                 )
         return 0
 
-    lax.fori_loop(0, 32, fill, 0, unroll=4)
+    lax.fori_loop(0, 32, fill, 0, unroll=True)
     ring = ring_ref[...]
 
     def close(ref):
         ref[0:EDGE, :] = ref[ROWS : ROWS + EDGE, :]
         ref[ROWS + EDGE :, :] = ref[EDGE : 2 * EDGE, :]
 
-    def twice(cur_ref, base):
-        wide = cur_ref[pl.ds(base, CHUNK + 2 * EDGE), :]
-        cur = wide[EDGE : EDGE + CHUNK]
-        return (2.0 * UNIT) * neighbours(wide, ring) + diag_ref[pl.ds(base, CHUNK), :] * cur
+    def sweep(cur_ref, emit, finish=None):
+        def product(i):
+            cur = cur_ref[pl.ds(EDGE + CHUNK * i, CHUNK), :]
+            return dot(jnp.concatenate(split(cur), axis=1), ring)
+
+        ahead = product(0)
+        for i in range(CHUNKS):
+            near, ahead = ahead, product(i + 1) if i + 1 < CHUNKS else None
+            for r in range(0, CHUNK, SUB):
+                for k in range(0, PLANE, 128):
+                    lanes, rows = slice(k, k + 128), pl.ds(CHUNK * i + r, SUB)
+                    wide = cur_ref[pl.ds(CHUNK * i + r, SUB + 2 * EDGE), lanes]
+                    total = near[r : r + SUB, lanes] + beside(wide, SUB)
+                    own = diag_ref[rows, lanes] * wide[EDGE : EDGE + SUB]
+                    emit(rows, lanes, (2.0 * UNIT) * total + own)
+            if finish is not None:
+                finish(CHUNK * i)
 
     def copy(base):
         return pltpu.make_async_copy(
@@ -240,30 +259,28 @@
             sems.at[base // CHUNK],
         )
 
-    def sweep(body):
-        for i in range(CHUNKS):
-            body(i * CHUNK)
-
-    def second(base):
-        two_ref[pl.ds(EDGE + base, CHUNK), :] = (
-            twice(one_ref, base) - field_ref[pl.ds(base, CHUNK), :]
-        )
-
-    def third(base):
-        rows = pl.ds(EDGE + base, CHUNK)
-        one_ref[rows, :] = twice(two_ref, base) - one_ref[rows, :]
-
-    def fourth(base):
-        rows = pl.ds(EDGE + base, CHUNK)
-        two_ref[rows, :] = twice(one_ref, base) - two_ref[rows, :]
-        copy(base).start()
+    def padded(rows):
+        return pl.ds(EDGE + rows.start, rows.size)
+
+    def second(rows, lanes, value):
+        two_ref[padded(rows), lanes] = value - field_ref[rows, lanes]
+
+    def third(rows, lanes, value):
+        rows = padded(rows)
+        one_ref[rows, lanes] = value - one_ref[rows, lanes]
+
+    def fourth(rows, lanes, value):
+        rows = padded(rows)
+        two_ref[rows, lanes] = value - two_ref[rows, lanes]
 
     close(one_ref)
-    for body, ref in ((second, two_ref), (third, one_ref)):
-        sweep(body)
-        close(ref)
-    sweep(fourth)
-    sweep(lambda base: copy(base).wait())
+    sweep(one_ref, second)
+    close(two_ref)
+    sweep(two_ref, third)
+    close(one_ref)
+    sweep(one_ref, fourth, lambda base: copy(base).start())
+    for i in range(CHUNKS):
+        copy(CHUNK * i).wait()
 
 
 def chebyshev(place, field, partial_sum, mine, other, ring):

time: 149 us -> 149 us (level)
  no operation moved by 1% of the time
where the time goes in v6:
time: 149 us; the launch traced here: 147 us
  blocking collectives  103 us (69%)
  Pallas kernels  30.4 us (20%)
  starting transfers between devices  7.24 us (5%)
  waiting for transfers between devices  6.35 us (4%)
    all_to_all x4, blocking collectives, exchange(): return lax.all_to_all(a, axes, 0, 0, tiled=True)  103 us
    pallas_call x1, Pallas kernels, inverse_root(): pl.pallas_call(root_kernel, in_specs=[SCALARS, VECTORS, VECTORS], out_sha...  12 us
    pallas_call x1, Pallas kernels, chebyshev(): pl.pallas_call(filter_kernel, in_specs=[smem] + [vmem] * 5, out_shape=jax...  6.17 us
    ppermute x3, starting transfers between devices, body(): lax.ppermute(share, ('zh', 'zl'), [(i, (i + k) % 4) for i in range(4)])  4.66 us
    ppermute x7, waiting for transfers between devices, swap(): return lax.ppermute(a, axis, [(0, 1), (1, 0)])  4.6 us
    pallas_call x2, Pallas kernels, put(): pl.pallas_call(functools.partial(place_kernel, jobs), in_specs=[SCALARS]...  3.07 us
  transfers between devices with their start and end apart: 10, of which 7 were waited for; matrix products, arithmetic and copies ran while one was open for 0% of the time, Pallas kernels for 13%

profile of v6, /device:TPU:0, one launch (start us, length us, event | category | flops | bytes accessed | tf_op | source)
XLA Modules:
  0.0 147.5 jit_solution(8249267769747725477)
XLA Ops:
  0.0 0.1 pad_add_fusion.place_ref
  0.1 2.9 %spread.1 = f32[16,2,144,128]{3,2,1,0:T(8,128)} custom-call(f32[8,512,128]{2,1,0:T(8,128)} %bitcast.15, f32[8,16,32]{2,1,0:T(8,128)} %pot_hbm.1), custom_call_target="tpu_custom_call" | custom-call | tf_op jit(solution)/shard_map/spread/pallas_call | solution.py:123
  2.9 0.0 copy-start
  3.0 44.1 %all_to_all.35.in_ref = f32[32,144,128]{2,1,0:T(8,128)S(1)} all-to-all(f32[32,144,128]{2,1,0:T(8,128)} %bitcast.14), channel_id=1, replica_groups=mesh['x'=4,'zh'=2,'y'=4,'zl'=2,'c'=2] {'x','zh','y'}, dimensions={0} | all-to-all | bytes 4718592 | tf_op jit(solution)/shard_map/all_to_all | solution.py:504
  47.1 0.1 collective-permute-start
  47.2 0.0 copy-done
  47.2 1.6 %gather.1 = (f32[1024,512]{1,0:T(8,128)S(1)}, f32[1024,512]{1,0:T(8,128)S(1)}) custom-call(f32[32,144,128]{2,1,0:T(8,128)S(1)} %all_to_all.35.in_ref, bf16[1024,512]{1,0:T(8,128)(2,1)S(1)} %copy-done), custom_call_target="tpu_custom_call" | custom-call | tf_op jit(solution)/shard_map/gather/pallas_call | solution.py:196
  48.9 0.0 collective-permute-done.other_ref
  48.9 6.2 %chebyshev.1 = f32[1024,512]{1,0:T(8,128)S(1)} custom-call(s32[2]{0:T(128)S(1)} %pad_add_fusion.place_ref, f32[1024,512]{1,0:T(8,128)S(1)} %get-tuple-element.24.field_ref, f32[1024,512]{1,0:T(8,128)S(1)} %get-tuple-element.25.sum_ref, f32[32,16,128]{2,1,0:T(8,128)S(1)} %slice.4.mine_ref, f32[32,16,128]{2,1,0:T(8,128)S(1)} %collective-permute-done.other_ref, ...), custom_call_target="tpu_custom_call" | custom-call | tf_op jit(solution)/shard_map/chebyshev/pallas_call | solution.py:289
  55.0 34.1 %all_to_all.36 = f32[128,8,512]{2,1,0:T(8,128)S(1)} all-to-all(f32[128,8,512]{2,1,0:T(8,128)S(1)} %bitcast.11), channel_id=1, replica_groups=mesh['x'=4,'zh'=2,'y'=4,'zl'=2,'c'=2] {'x','zh','y','zl','c'}, dimensions={0} | all-to-all | bytes 4194304 | tf_op jit(solution)/shard_map/all_to_all | solution.py:504
  89.1 0.6 turn.1
  89.8 0.9 collective-permute-start.2
  90.6 2.0 %gram.1 = (f32[640,128]{1,0:T(8,128)S(1)}, f32[640,128]{1,0:T(8,128)S(1)}) custom-call(s32[2]{0:T(128)S(1)} %pad_add_fusion.place_ref, f32[352,512]{1,0:T(8,128)S(1)} %get-tuple-element.26.near_ref.refs_0_, f32[672,512]{1,0:T(8,128)S(1)} %get-tuple-element.32.far_ref.refs_1_, bf16[512,1024]{1,0:T(8,128)(2,1)S(1)} %get-tuple-element.28.left_ref), custom_call_target="tpu_custom_call" | custom-call | tf_op jit(solution)/shard_map/gram/pallas_call | solution.py:360
  92.6 0.1 collective-permute-start.1
  92.7 1.6 %collective-permute-done.1 = f32[640,128]{1,0:T(8,128)S(1)} collective-permute-done((f32[640,128]{1,0:T(8,128)S(1)}, f32[640,128]{1,0:T(8,128)S(1)}, u32[]{:S(2)}, u32[]{:S(2)}) %collective-permute-start.1) | collective-permute-done | bytes 327712 | tf_op jit(solution)/shard_map/ppermute | solution.py:508
  94.4 12.5 %all_to_all.37 = f32[16,40,128]{2,1,0:T(8,128)S(1)} all-to-all(f32[16,40,128]{2,1,0:T(8,128)S(1)} %bitcast.16), channel_id=1, replica_groups=mesh['x'=4,'zh'=2,'y'=4,'zl'=2,'c'=2] {'x','y'}, dimensions={0} | all-to-all | bytes 655360 | tf_op jit(solution)/shard_map/all_to_all | solution.py:504
  106.9 0.1 collective-permute-done.2.refs_2_
  107.1 1.4 collective-permute-start.3
  108.5 0.4 collective-permute-start.4
  108.9 2.8 %collective-permute-start.5 = (f32[40,128]{1,0:T(8,128)S(1)}, f32[40,128]{1,0:T(8,128)S(1)}, u32[]{:S(2)}, u32[]{:S(2)}) collective-permute-start(f32[40,128]{1,0:T(8,128)S(1)} %reduce_sum.9), channel_id=1, source_target_pairs={{0,18},{2,0},{16,2},{18,16},{1,19},{3,1},{17,3},{19,17},{4,22},{6,... | collective-permute-start | bytes 61448 | tf_op jit(solution)/shard_map/ppermute | solution.py:529
  111.7 0.6 collective-permute-done.3
  112.3 1.1 collective-permute-done.4
  113.5 0.0 collective-permute-done.5
  113.5 1.2 collective-permute-start.6
  114.8 12.3 %all_to_all.38 = f32[16,40,128]{2,1,0:T(8,128)S(1)} all-to-all(f32[16,40,128]{2,1,0:T(8,128)S(1)} %tile.2), channel_id=1, replica_groups=mesh['x'=4,'zh'=2,'y'=4,'zl'=2,'c'=2] {'x','y'}, dimensions={0} | all-to-all | bytes 655360 | tf_op jit(solution)/shard_map/all_to_all | solution.py:504
  127.0 0.0 collective-permute-start.7
  127.1 1.6 %collective-permute-done.7.other_ref = f32[640,128]{1,0:T(8,128)S(1)} collective-permute-done((f32[640,128]{1,0:T(8,128)S(1)}, f32[640,128]{1,0:T(8,128)S(1)}, u32[]{:S(2)}, u32[]{:S(2)}) %collective-permute-start.7) | collective-permute-done | bytes 327712 | tf_op jit(solution)/shard_map/ppermute | solution.py:508
  128.7 12.0 %inverse_root.1.refs_1_.refs_3_ = bf16[2,512,256]{2,1,0:T(8,128)(2,1)S(1)} custom-call(s32[2]{0:T(128)S(1)} %pad_add_fusion.place_ref, f32[640,128]{1,0:T(8,128)S(1)} %bitcast.13, f32[640,128]{1,0:T(8,128)S(1)} %collective-permute-done.7.other_ref), custom_call_target="tpu_custom_call" | custom-call | tf_op jit(solution)/shard_map/inverse_root/pallas_call | solution.py:436
  140.7 1.3 whiten.3
  142.0 0.2 collective-permute-start.9
  142.2 0.6 collective-permute-done.6.refs_0_
  142.8 0.7 whiten.2
  143.6 0.1 collective-permute-start.8
  143.7 0.6 collective-permute-done.9.refs_2_
  144.2 1.8 %put.2.refs_1_ = f32[2,2,1024,128]{3,2,1,0:T(8,128)} custom-call(s32[2]{0:T(128)S(1)} %pad_add_fusion.place_ref, f32[1376,128]{1,0:T(8,128)S(1)} %get-tuple-element.36.refs_0_, f32[672,128]{1,0:T(8,128)S(1)} %get-tuple-element.37.refs_1_, f32[1376,128]{1,0:T(8,128)S(1)} %collective-permute-done.9.refs_2_), custom_call_target="tpu_custom_call" | custom-call | tf_op jit(solution)/shard_map/put/pallas_call | solution.py:491
  146.0 0.0 collective-permute-done.8.refs_0_
  146.0 1.3 put.3
  (5 shorter events, 0.1 us)
Async XLA Ops:
  2.9 44.3 %copy-start = (bf16[1024,512]{1,0:T(8,128)(2,1)S(1)}, bf16[1024,512]{1,0:T(8,128)(2,1)}, u32[]{:S(2)}) copy-start(bf16[1024,512]{1,0:T(8,128)(2,1)} %constant.10.clone.ring_ref) | copy-start | bytes 3145732
  47.1 1.7 %collective-permute-start = (f32[32,16,128]{2,1,0:T(8,128)S(1)}, f32[32,16,128]{2,1,0:T(8,128)S(1)}, u32[]{:S(2)}, u32[]{:S(2)}) collective-permute-start(f32[32,16,128]{2,1,0:T(8,128)S(1)} %slice.4.mine_ref), channel_id=1, source_target_pairs={{0,1},{1,0},{2,3},{3,2},{4,5},{5,4},{6,7},{7,6},{8,9},{9,8},{10,11... | collective-permute-start | bytes 786440 | tf_op jit(solution)/shard_map/ppermute | solution.py:508
  89.8 17.3 %collective-permute-start.2 = (f32[352,512]{1,0:T(8,128)S(1)}, f32[352,512]{1,0:T(8,128)S(1)}, u32[]{:S(2)}, u32[]{:S(2)}) collective-permute-start(f32[352,512]{1,0:T(8,128)S(1)} %get-tuple-element.26.near_ref.refs_0_), channel_id=1, source_target_pairs={{0,2},{2,0},{1,3},{3,1},{4,6},{6,4},{5,7},{7,5},{8,10},{10,8},{9,1... | collective-permute-start | bytes 2162696 | tf_op jit(solution)/shard_map/ppermute | solution.py:508
  92.6 1.7 %collective-permute-start.1 = (f32[640,128]{1,0:T(8,128)S(1)}, f32[640,128]{1,0:T(8,128)S(1)}, u32[]{:S(2)}, u32[]{:S(2)}) collective-permute-start(f32[640,128]{1,0:T(8,128)S(1)} %get-tuple-element.30), channel_id=1, source_target_pairs={{0,1},{1,0},{2,3},{3,2},{4,5},{5,4},{6,7},{7,6},{8,9},{9,8},{10,11... | collective-permute-start | bytes 983048 | tf_op jit(solution)/shard_map/ppermute | solution.py:508
  107.1 5.3 %collective-permute-start.3 = (f32[40,128]{1,0:T(8,128)S(1)}, f32[40,128]{1,0:T(8,128)S(1)}, u32[]{:S(2)}, u32[]{:S(2)}) collective-permute-start(f32[40,128]{1,0:T(8,128)S(1)} %reduce_sum.9), channel_id=1, source_target_pairs={{0,16},{2,18},{16,0},{18,2},{1,17},{3,19},{17,1},{19,3},{4,20},{6,... | collective-permute-start | bytes 61448 | tf_op jit(solution)/shard_map/ppermute | solution.py:529
  108.5 5.0 %collective-permute-start.4 = (f32[40,128]{1,0:T(8,128)S(1)}, f32[40,128]{1,0:T(8,128)S(1)}, u32[]{:S(2)}, u32[]{:S(2)}) collective-permute-start(f32[40,128]{1,0:T(8,128)S(1)} %reduce_sum.9), channel_id=1, source_target_pairs={{0,2},{2,16},{16,18},{18,0},{1,3},{3,17},{17,19},{19,1},{4,6},{6,2... | collective-permute-start | bytes 61448 | tf_op jit(solution)/shard_map/ppermute | solution.py:529
  108.9 4.6 %collective-permute-start.5 = (f32[40,128]{1,0:T(8,128)S(1)}, f32[40,128]{1,0:T(8,128)S(1)}, u32[]{:S(2)}, u32[]{:S(2)}) collective-permute-start(f32[40,128]{1,0:T(8,128)S(1)} %reduce_sum.9), channel_id=1, source_target_pairs={{0,18},{2,0},{16,2},{18,16},{1,19},{3,1},{17,3},{19,17},{4,22},{6,... | collective-permute-start | bytes 61448 | tf_op jit(solution)/shard_map/ppermute | solution.py:529
  113.5 29.4 %collective-permute-start.6 = (f32[672,512]{1,0:T(8,128)S(1)}, f32[672,512]{1,0:T(8,128)S(1)}, u32[]{:S(2)}, u32[]{:S(2)}) collective-permute-start(f32[672,512]{1,0:T(8,128)S(1)} %get-tuple-element.32.far_ref.refs_1_), channel_id=1, source_target_pairs={{0,2},{2,0},{1,3},{3,1},{4,6},{6,4},{5,7},{7,5},{8,10},{10,8},{9,1... | collective-permute-start | bytes 4128776 | tf_op jit(solution)/shard_map/ppermute | solution.py:508
  127.0 1.6 %collective-permute-start.7 = (f32[640,128]{1,0:T(8,128)S(1)}, f32[640,128]{1,0:T(8,128)S(1)}, u32[]{:S(2)}, u32[]{:S(2)}) collective-permute-start(f32[640,128]{1,0:T(8,128)S(1)} %bitcast.12), channel_id=1, source_target_pairs={{0,1},{1,0},{2,3},{3,2},{4,5},{5,4},{6,7},{7,6},{8,9},{9,8},{10,11... | collective-permute-start | bytes 983048 | tf_op jit(solution)/shard_map/ppermute | solution.py:508
  142.0 2.2 %collective-permute-start.9 = (f32[1376,128]{1,0:T(8,128)S(1)}, f32[1376,128]{1,0:T(8,128)S(1)}, u32[]{:S(2)}, u32[]{:S(2)}) collective-permute-start(f32[1376,128]{1,0:T(8,128)S(1)} %get-tuple-element.38), channel_id=1, source_target_pairs={{0,1},{1,0},{2,3},{3,2},{4,5},{5,4},{6,7},{7,6},{8,9},{9,8},{10,11... | collective-permute-start | bytes 2113544 | tf_op jit(solution)/shard_map/ppermute | solution.py:508
  143.6 2.5 %collective-permute-start.8 = (f32[672,128]{1,0:T(8,128)S(1)}, f32[672,128]{1,0:T(8,128)S(1)}, u32[]{:S(2)}, u32[]{:S(2)}) collective-permute-start(f32[672,128]{1,0:T(8,128)S(1)} %get-tuple-element.34), channel_id=1, source_target_pairs={{0,1},{1,0},{2,3},{3,2},{4,5},{5,4},{6,7},{7,6},{8,9},{9,8},{10,11... | collective-permute-start | bytes 1032200 | tf_op jit(solution)/shard_map/ppermute | solution.py:508

commit v7 on v6

--- a/solution.py
+++ b/solution.py
@@ -163,9 +163,12 @@
     )
 
 
-def neighbours(wide, ring):
-    near = dot(jnp.concatenate(split(wide[EDGE : EDGE + CHUNK]), axis=1), ring)
-    return near + beside(wide, CHUNK)
+def neighbours(wide, ring, count):
+    near = dot(jnp.concatenate(split(wide[EDGE : EDGE + count]), axis=1), ring)
+    return near + beside(wide, count)
+
+
+FIRST = 256
 
 
 def gather_kernel(in_ref, ring_ref, field_ref, sum_ref):
@@ -176,9 +179,9 @@
         )
 
     ring = ring_ref[...]
-    for i in range(CHUNKS):
-        before, after = (PARTS * i - 1) % 32, PARTS * (i + 1) % 32
-        middle = planes(slice(PARTS * i, PARTS * (i + 1)), 0, 4)
+    for i in range((ROWS // FIRST)):
+        before, after = ((FIRST // 32) * i - 1) % 32, (FIRST // 32) * (i + 1) % 32
+        middle = planes(slice((FIRST // 32) * i, (FIRST // 32) * (i + 1)), 0, 4)
         wide = jnp.concatenate(
             [
                 planes(slice(before, before + 1), 2, 2),
@@ -187,9 +190,9 @@
             ],
             axis=0,
         )
-        rows = pl.ds(CHUNK * i, CHUNK)
+        rows = pl.ds(FIRST * i, FIRST)
         field_ref[rows, :] = middle
-        sum_ref[rows, :] = neighbours(wide, ring)
+        sum_ref[rows, :] = neighbours(wide, ring, FIRST)
 
 
 def gather(messages, ring):
@@ -442,8 +445,7 @@
     )(place, mine, other)
 
 
-def whiten_kernel(*refs):
-    chunks, root_ref, ours_ref, theirs_ref = refs[:-3], refs[-3], refs[-2], refs[-1]
+def whiten_rows(chunks, root_ref, ours_ref, theirs_ref, finish=None):
     root = (root_ref[0], root_ref[1])
     start = 0
     for ref in chunks:
@@ -452,6 +454,33 @@
         ours_ref[rows, :] = white[:, :128]
         theirs_ref[rows, :] = white[:, 128:]
         start += ref.shape[0]
+        if finish is not None and start == 2 * PLANE:
+            finish()
+
+
+def whiten_kernel(*refs):
+    whiten_rows(refs[:-3], *refs[-3:])
+
+
+def early_kernel(place_ref, near_ref, far_ref, other_ref, root_ref, ours_ref, theirs_ref, whole_ref, sem):
+    copy = pltpu.make_async_copy(
+        ours_ref.at[pl.ds(0, 2 * PLANE)], whole_ref.at[place_ref[0], place_ref[1]], sem
+    )
+    whiten_rows((near_ref, far_ref, other_ref), root_ref, ours_ref, theirs_ref, copy.start)
+    copy.wait()
+
+
+def whiten_early(place, chunks, root):
+    rows = sum(chunk.shape[0] for chunk in chunks)
+    return pl.pallas_call(
+        early_kernel,
+        in_specs=[SCALARS] + [VECTORS] * 4,
+        out_specs=(VECTORS, VECTORS, ANYWHERE),
+        out_shape=(jax.ShapeDtypeStruct((rows, 128), F32),) * 2 + (WHOLE,),
+        scratch_shapes=[pltpu.SemaphoreType.DMA],
+        compiler_params=pltpu.CompilerParams(vmem_limit_bytes=VMEM_SMALL),
+        name="whiten_early",
+    )(place, *chunks, root)
 
 
 def whiten(chunks, root):
@@ -534,20 +563,18 @@
     total = exchange(jnp.tile(share, (16, 1)), ("x", "y"))
     root = inverse_root(place, total, swap(total, "c"))
 
-    ours, theirs = whiten((near, far, other_near), root)
+    ours, theirs, whole = whiten_early(place, (near, far, other_near), root)
     first = swap(theirs, "c")
     late_ours, late_theirs = whiten((other_far,), root)
     second = swap(late_theirs, "c")
     chunk, late = 2 * PLANE, 2 * PLANE - PART
-    jobs = tuple(
-        job
-        for part, other_core in ((0, False), (2, True))
-        for job in (
-            (part, 0, chunk, False, other_core, 0),
-            (part, chunk, PART, True, other_core, 0),
-        )
-    )
-    whole = put(place, jobs + ((1, 0, late, True, False, PART),), (ours, late_ours, first))
+    jobs = (
+        (0, chunk, PART, True, False, 0),
+        (1, 0, late, True, False, PART),
+        (2, 0, chunk, False, True, 0),
+        (2, chunk, PART, True, True, 0),
+    )
+    whole = put(place, jobs, (ours, late_ours, first), whole)
     whitened = put(place, ((0, 0, late, True, True, PART),), (second,), whole)
     return whitened.reshape(orbitals.shape)
 

time: 149 us -> 150 us (level)
    pallas_call x0 -> x1, Pallas kernels: none -> 2.62 us  [whiten_early(): pl.pallas_call(early_kernel, in_specs=[SCALARS] + [VECTORS] * 4, out_spec...]
  transfers between devices with their start and end apart: 10 -> 10, of which waited for: 7 -> 6; matrix products, arithmetic and copies ran while one was open for 0% -> 0% of each run, Pallas kernels for 13% -> 14%
where the time goes in v7:
time: 150 us; the launch traced here: 149 us
  blocking collectives  103 us (69%)
  Pallas kernels  31.4 us (21%)
  starting transfers between devices  7.6 us (5%)
  waiting for transfers between devices  6 us (4%)
    all_to_all x4, blocking collectives, exchange(): return lax.all_to_all(a, axes, 0, 0, tiled=True)  103 us
    pallas_call x1, Pallas kernels, inverse_root(): pl.pallas_call(root_kernel, in_specs=[SCALARS, VECTORS, VECTORS], out_sha...  12 us
    pallas_call x1, Pallas kernels, chebyshev(): pl.pallas_call(filter_kernel, in_specs=[smem] + [vmem] * 5, out_shape=jax...  6.2 us
    ppermute x3, starting transfers between devices, body(): lax.ppermute(share, ('zh', 'zl'), [(i, (i + k) % 4) for i in range(4)])  4.66 us
    ppermute x7, waiting for transfers between devices, swap(): return lax.ppermute(a, axis, [(0, 1), (1, 0)])  4.24 us
  transfers between devices with their start and end apart: 10, of which 6 were waited for; matrix products, arithmetic and copies ran while one was open for 0% of the time, Pallas kernels for 14%

profile of v7, /device:TPU:0, one launch (start us, length us, event | category | flops | bytes accessed | tf_op | source)
XLA Modules:
  0.0 148.5 jit_solution(14903370423396325770)
XLA Ops:
  0.0 0.1 pad_add_fusion.place_ref
  0.1 2.9 %spread.1 = f32[16,2,144,128]{3,2,1,0:T(8,128)} custom-call(f32[8,512,128]{2,1,0:T(8,128)} %bitcast.15, f32[8,16,32]{2,1,0:T(8,128)} %pot_hbm.1), custom_call_target="tpu_custom_call" | custom-call | tf_op jit(solution)/shard_map/spread/pallas_call | solution.py:123
  2.9 0.0 copy-start
  3.0 44.1 %all_to_all.35.in_ref = f32[32,144,128]{2,1,0:T(8,128)S(1)} all-to-all(f32[32,144,128]{2,1,0:T(8,128)} %bitcast.14), channel_id=1, replica_groups=mesh['x'=4,'zh'=2,'y'=4,'zl'=2,'c'=2] {'x','zh','y'}, dimensions={0} | all-to-all | bytes 4718592 | tf_op jit(solution)/shard_map/all_to_all | solution.py:533
  47.1 0.1 collective-permute-start
  47.2 0.0 copy-done
  47.2 1.5 %gather.1 = (f32[1024,512]{1,0:T(8,128)S(1)}, f32[1024,512]{1,0:T(8,128)S(1)}) custom-call(f32[32,144,128]{2,1,0:T(8,128)S(1)} %all_to_all.35.in_ref, bf16[1024,512]{1,0:T(8,128)(2,1)S(1)} %copy-done), custom_call_target="tpu_custom_call" | custom-call | tf_op jit(solution)/shard_map/gather/pallas_call | solution.py:199
  48.8 0.0 collective-permute-done.other_ref
  48.8 6.2 %chebyshev.1 = f32[1024,512]{1,0:T(8,128)S(1)} custom-call(s32[2]{0:T(128)S(1)} %pad_add_fusion.place_ref, f32[1024,512]{1,0:T(8,128)S(1)} %get-tuple-element.25.field_ref, f32[1024,512]{1,0:T(8,128)S(1)} %get-tuple-element.26.sum_ref, f32[32,16,128]{2,1,0:T(8,128)S(1)} %slice.4.mine_ref, f32[32,16,128]{2,1,0:T(8,128)S(1)} %collective-permute-done.other_ref, ...), custom_call_target="tpu_custom_call" | custom-call | tf_op jit(solution)/shard_map/chebyshev/pallas_call | solution.py:292
  55.0 34.0 %all_to_all.36 = f32[128,8,512]{2,1,0:T(8,128)S(1)} all-to-all(f32[128,8,512]{2,1,0:T(8,128)S(1)} %bitcast.11), channel_id=1, replica_groups=mesh['x'=4,'zh'=2,'y'=4,'zl'=2,'c'=2] {'x','zh','y','zl','c'}, dimensions={0} | all-to-all | bytes 4194304 | tf_op jit(solution)/shard_map/all_to_all | solution.py:533
  89.0 0.6 turn.1
  89.7 0.9 collective-permute-start.2
  90.5 2.0 %gram.1 = (f32[640,128]{1,0:T(8,128)S(1)}, f32[640,128]{1,0:T(8,128)S(1)}) custom-call(s32[2]{0:T(128)S(1)} %pad_add_fusion.place_ref, f32[352,512]{1,0:T(8,128)S(1)} %get-tuple-element.27.near_ref, f32[672,512]{1,0:T(8,128)S(1)} %get-tuple-element.33.far_ref, bf16[512,1024]{1,0:T(8,128)(2,1)S(1)} %get-tuple-element.29.left_ref), custom_call_target="tpu_custom_call" | custom-call | tf_op jit(solution)/shard_map/gram/pallas_call | solution.py:363
  92.5 0.1 collective-permute-start.1
  92.6 1.6 %collective-permute-done.1 = f32[640,128]{1,0:T(8,128)S(1)} collective-permute-done((f32[640,128]{1,0:T(8,128)S(1)}, f32[640,128]{1,0:T(8,128)S(1)}, u32[]{:S(2)}, u32[]{:S(2)}) %collective-permute-start.1) | collective-permute-done | bytes 327712 | tf_op jit(solution)/shard_map/ppermute | solution.py:537
  94.3 12.5 %all_to_all.37 = f32[16,40,128]{2,1,0:T(8,128)S(1)} all-to-all(f32[16,40,128]{2,1,0:T(8,128)S(1)} %bitcast.16), channel_id=1, replica_groups=mesh['x'=4,'zh'=2,'y'=4,'zl'=2,'c'=2] {'x','y'}, dimensions={0} | all-to-all | bytes 655360 | tf_op jit(solution)/shard_map/all_to_all | solution.py:533
  106.8 0.1 collective-permute-done.2.other_ref
  106.9 1.4 collective-permute-start.3
  108.4 0.4 collective-permute-start.4
  108.8 2.8 %collective-permute-start.5 = (f32[40,128]{1,0:T(8,128)S(1)}, f32[40,128]{1,0:T(8,128)S(1)}, u32[]{:S(2)}, u32[]{:S(2)}) collective-permute-start(f32[40,128]{1,0:T(8,128)S(1)} %reduce_sum.9), channel_id=1, source_target_pairs={{0,18},{2,0},{16,2},{18,16},{1,19},{3,1},{17,3},{19,17},{4,22},{6,... | collective-permute-start | bytes 61448 | tf_op jit(solution)/shard_map/ppermute | solution.py:558
  111.6 0.6 collective-permute-done.3
  112.2 1.1 collective-permute-done.4
  113.4 0.0 collective-permute-done.5
  113.4 1.2 collective-permute-start.6
  114.6 12.3 %all_to_all.38 = f32[16,40,128]{2,1,0:T(8,128)S(1)} all-to-all(f32[16,40,128]{2,1,0:T(8,128)S(1)} %tile.2), channel_id=1, replica_groups=mesh['x'=4,'zh'=2,'y'=4,'zl'=2,'c'=2] {'x','y'}, dimensions={0} | all-to-all | bytes 655360 | tf_op jit(solution)/shard_map/all_to_all | solution.py:533
  126.9 0.0 collective-permute-start.7
  126.9 1.6 %collective-permute-done.7.other_ref = f32[640,128]{1,0:T(8,128)S(1)} collective-permute-done((f32[640,128]{1,0:T(8,128)S(1)}, f32[640,128]{1,0:T(8,128)S(1)}, u32[]{:S(2)}, u32[]{:S(2)}) %collective-permute-start.7) | collective-permute-done | bytes 327712 | tf_op jit(solution)/shard_map/ppermute | solution.py:537
  128.6 12.0 %inverse_root.1.refs_1_.root_ref = bf16[2,512,256]{2,1,0:T(8,128)(2,1)S(1)} custom-call(s32[2]{0:T(128)S(1)} %pad_add_fusion.place_ref, f32[640,128]{1,0:T(8,128)S(1)} %bitcast.13, f32[640,128]{1,0:T(8,128)S(1)} %collective-permute-done.7.other_ref), custom_call_target="tpu_custom_call" | custom-call | tf_op jit(solution)/shard_map/inverse_root/pallas_call | solution.py:439
  140.6 2.6 %whiten_early.1 = (f32[1376,128]{1,0:T(8,128)S(1)}, f32[1376,128]{1,0:T(8,128)S(1)}, f32[2,2,1024,128]{3,2,1,0:T(8,128)}) custom-call(s32[2]{0:T(128)S(1)} %pad_add_fusion.place_ref, f32[352,512]{1,0:T(8,128)S(1)} %get-tuple-element.27.near_ref, f32[672,512]{1,0:T(8,128)S(1)} %get-tuple-element.33.far_ref, f32[352,512]{1,0:T(8,128)S(1)} %collective-permute-done.2.other_ref, ...), custom_call_target="tpu_custom_call" | custom-call | tf_op jit(solution)/shard_map/whiten_early/pallas_call | solution.py:475
  143.2 0.2 collective-permute-start.9
  143.4 0.0 collective-permute-done.6.refs_0_
  143.4 0.7 whiten.1
  144.1 0.5 collective-permute-start.8
  144.6 0.9 collective-permute-done.9.refs_2_
  145.4 1.6 %put.2.refs_1_ = f32[2,2,1024,128]{3,2,1,0:T(8,128)} custom-call(s32[2]{0:T(128)S(1)} %pad_add_fusion.place_ref, f32[1376,128]{1,0:T(8,128)S(1)} %get-tuple-element.37.refs_0_, f32[672,128]{1,0:T(8,128)S(1)} %get-tuple-element.38.refs_1_, f32[1376,128]{1,0:T(8,128)S(1)} %collective-permute-done.9.refs_2_, ...), custom_call_target="tpu_custom_call", output_to_operand_aliasing={{}: (4, {})} | custom-call | tf_op jit(solution)/shard_map/put/pallas_call | solution.py:520
  147.0 0.0 collective-permute-done.8.refs_0_
  147.1 1.3 put.3
  (5 shorter events, 0.1 us)
Async XLA Ops:
  2.9 44.3 %copy-start = (bf16[1024,512]{1,0:T(8,128)(2,1)S(1)}, bf16[1024,512]{1,0:T(8,128)(2,1)}, u32[]{:S(2)}) copy-start(bf16[1024,512]{1,0:T(8,128)(2,1)} %constant.10.clone.ring_ref) | copy-start | bytes 3145732
  47.1 1.6 %collective-permute-start = (f32[32,16,128]{2,1,0:T(8,128)S(1)}, f32[32,16,128]{2,1,0:T(8,128)S(1)}, u32[]{:S(2)}, u32[]{:S(2)}) collective-permute-start(f32[32,16,128]{2,1,0:T(8,128)S(1)} %slice.4.mine_ref), channel_id=1, source_target_pairs={{0,1},{1,0},{2,3},{3,2},{4,5},{5,4},{6,7},{7,6},{8,9},{9,8},{10,11... | collective-permute-start | bytes 786440 | tf_op jit(solution)/shard_map/ppermute | solution.py:537
  89.7 17.3 %collective-permute-start.2 = (f32[352,512]{1,0:T(8,128)S(1)}, f32[352,512]{1,0:T(8,128)S(1)}, u32[]{:S(2)}, u32[]{:S(2)}) collective-permute-start(f32[352,512]{1,0:T(8,128)S(1)} %get-tuple-element.27.near_ref), channel_id=1, source_target_pairs={{0,2},{2,0},{1,3},{3,1},{4,6},{6,4},{5,7},{7,5},{8,10},{10,8},{9,1... | collective-permute-start | bytes 2162696 | tf_op jit(solution)/shard_map/ppermute | solution.py:537
  92.5 1.7 %collective-permute-start.1 = (f32[640,128]{1,0:T(8,128)S(1)}, f32[640,128]{1,0:T(8,128)S(1)}, u32[]{:S(2)}, u32[]{:S(2)}) collective-permute-start(f32[640,128]{1,0:T(8,128)S(1)} %get-tuple-element.31), channel_id=1, source_target_pairs={{0,1},{1,0},{2,3},{3,2},{4,5},{5,4},{6,7},{7,6},{8,9},{9,8},{10,11... | collective-permute-start | bytes 983048 | tf_op jit(solution)/shard_map/ppermute | solution.py:537
  106.9 5.3 %collective-permute-start.3 = (f32[40,128]{1,0:T(8,128)S(1)}, f32[40,128]{1,0:T(8,128)S(1)}, u32[]{:S(2)}, u32[]{:S(2)}) collective-permute-start(f32[40,128]{1,0:T(8,128)S(1)} %reduce_sum.9), channel_id=1, source_target_pairs={{0,16},{2,18},{16,0},{18,2},{1,17},{3,19},{17,1},{19,3},{4,20},{6,... | collective-permute-start | bytes 61448 | tf_op jit(solution)/shard_map/ppermute | solution.py:558
  108.4 5.0 %collective-permute-start.4 = (f32[40,128]{1,0:T(8,128)S(1)}, f32[40,128]{1,0:T(8,128)S(1)}, u32[]{:S(2)}, u32[]{:S(2)}) collective-permute-start(f32[40,128]{1,0:T(8,128)S(1)} %reduce_sum.9), channel_id=1, source_target_pairs={{0,2},{2,16},{16,18},{18,0},{1,3},{3,17},{17,19},{19,1},{4,6},{6,2... | collective-permute-start | bytes 61448 | tf_op jit(solution)/shard_map/ppermute | solution.py:558
  108.8 4.6 %collective-permute-start.5 = (f32[40,128]{1,0:T(8,128)S(1)}, f32[40,128]{1,0:T(8,128)S(1)}, u32[]{:S(2)}, u32[]{:S(2)}) collective-permute-start(f32[40,128]{1,0:T(8,128)S(1)} %reduce_sum.9), channel_id=1, source_target_pairs={{0,18},{2,0},{16,2},{18,16},{1,19},{3,1},{17,3},{19,17},{4,22},{6,... | collective-permute-start | bytes 61448 | tf_op jit(solution)/shard_map/ppermute | solution.py:558
  113.4 30.0 %collective-permute-start.6 = (f32[672,512]{1,0:T(8,128)S(1)}, f32[672,512]{1,0:T(8,128)S(1)}, u32[]{:S(2)}, u32[]{:S(2)}) collective-permute-start(f32[672,512]{1,0:T(8,128)S(1)} %get-tuple-element.33.far_ref), channel_id=1, source_target_pairs={{0,2},{2,0},{1,3},{3,1},{4,6},{6,4},{5,7},{7,5},{8,10},{10,8},{9,1... | collective-permute-start | bytes 4128776 | tf_op jit(solution)/shard_map/ppermute | solution.py:537
  126.9 1.6 %collective-permute-start.7 = (f32[640,128]{1,0:T(8,128)S(1)}, f32[640,128]{1,0:T(8,128)S(1)}, u32[]{:S(2)}, u32[]{:S(2)}) collective-permute-start(f32[640,128]{1,0:T(8,128)S(1)} %bitcast.12), channel_id=1, source_target_pairs={{0,1},{1,0},{2,3},{3,2},{4,5},{5,4},{6,7},{7,6},{8,9},{9,8},{10,11... | collective-permute-start | bytes 983048 | tf_op jit(solution)/shard_map/ppermute | solution.py:537
  143.2 2.2 %collective-permute-start.9 = (f32[1376,128]{1,0:T(8,128)S(1)}, f32[1376,128]{1,0:T(8,128)S(1)}, u32[]{:S(2)}, u32[]{:S(2)}) collective-permute-start(f32[1376,128]{1,0:T(8,128)S(1)} %get-tuple-element.39), channel_id=1, source_target_pairs={{0,1},{1,0},{2,3},{3,2},{4,5},{5,4},{6,7},{7,6},{8,9},{9,8},{10,11... | collective-permute-start | bytes 2113544 | tf_op jit(solution)/shard_map/ppermute | solution.py:537
  144.1 2.9 %collective-permute-start.8 = (f32[672,128]{1,0:T(8,128)S(1)}, f32[672,128]{1,0:T(8,128)S(1)}, u32[]{:S(2)}, u32[]{:S(2)}) collective-permute-start(f32[672,128]{1,0:T(8,128)S(1)} %get-tuple-element.35), channel_id=1, source_target_pairs={{0,1},{1,0},{2,3},{3,2},{4,5},{5,4},{6,7},{7,6},{8,9},{9,8},{10,11... | collective-permute-start | bytes 1032200 | tf_op jit(solution)/shard_map/ppermute | solution.py:537

commit v8 on v6

--- a/solution.py
+++ b/solution.py
@@ -85,10 +85,10 @@
     for load in loads:
         load.start()
 
-    def store(t):
+    def store(t, parity):
         rows = pl.ds(32 * t, 32 if t < 4 else POT_ROWS)
         return pltpu.make_async_copy(
-            out_ref.at[:, :, rows], out_hbm.at[:, :, rows], out_sems.at[t]
+            out_ref.at[:, parity, rows], out_hbm.at[:, parity, rows], out_sems.at[t, parity]
         )
 
     pot_load.wait()
@@ -100,22 +100,26 @@
         )
         rows = pl.ds(FIELD_ROWS + 8 * k, 8)
         out_ref[:, :, rows, :] = jnp.broadcast_to(tile, (16, 2, 8, 128))
-    store(4).start()
+    for parity in range(2):
+        store(4, parity).start()
     for t in range(4):
         loads[2 * t].wait()
         loads[2 * t + 1].wait()
         a = v_ref[2 * t].T.reshape(16, 8, PLANE)
         b = v_ref[2 * t + 1].T.reshape(16, 8, PLANE)
         low = low_rows(a.shape)
-        even = jnp.where(low, a, swap_halves(b))
-        odd = jnp.where(low, swap_halves(a), b)
-        for k in range(4):
-            rows, lanes = pl.ds(32 * t + 8 * k, 8), slice(128 * k, 128 * (k + 1))
-            out_ref[:, 0, rows, :] = even[:, :, lanes]
-            out_ref[:, 1, rows, :] = odd[:, :, lanes]
-        store(t).start()
+        for parity in range(2):
+            if parity == 0:
+                mixed = jnp.where(low, a, swap_halves(b))
+            else:
+                mixed = jnp.where(low, swap_halves(a), b)
+            for k in range(4):
+                rows = pl.ds(32 * t + 8 * k, 8)
+                out_ref[:, parity, rows, :] = mixed[:, :, 128 * k : 128 * (k + 1)]
+            store(t, parity).start()
     for t in range(5):
-        store(t).wait()
+        for parity in range(2):
+            store(t, parity).wait()
 
 
 def spread(field, potential):
@@ -130,7 +134,7 @@
             pltpu.VMEM((SLAB, NY, NZ), F32),
             pltpu.VMEM(shape, F32),
             pltpu.SemaphoreType.DMA((SLAB + 1,)),
-            pltpu.SemaphoreType.DMA((5,)),
+            pltpu.SemaphoreType.DMA((5, 2)),
         ],
         compiler_params=pltpu.CompilerParams(vmem_limit_bytes=VMEM_SPREAD),
         name="spread",
@@ -163,9 +167,12 @@
     )
 
 
-def neighbours(wide, ring):
-    near = dot(jnp.concatenate(split(wide[EDGE : EDGE + CHUNK]), axis=1), ring)
-    return near + beside(wide, CHUNK)
+def neighbours(wide, ring, count):
+    near = dot(jnp.concatenate(split(wide[EDGE : EDGE + count]), axis=1), ring)
+    return near + beside(wide, count)
+
+
+FIRST = 256
 
 
 def gather_kernel(in_ref, ring_ref, field_ref, sum_ref):
@@ -176,9 +183,9 @@
         )
 
     ring = ring_ref[...]
-    for i in range(CHUNKS):
-        before, after = (PARTS * i - 1) % 32, PARTS * (i + 1) % 32
-        middle = planes(slice(PARTS * i, PARTS * (i + 1)), 0, 4)
+    for i in range(ROWS // FIRST):
+        before, after = ((FIRST // 32) * i - 1) % 32, (FIRST // 32) * (i + 1) % 32
+        middle = planes(slice((FIRST // 32) * i, (FIRST // 32) * (i + 1)), 0, 4)
         wide = jnp.concatenate(
             [
                 planes(slice(before, before + 1), 2, 2),
@@ -187,9 +194,9 @@
             ],
             axis=0,
         )
-        rows = pl.ds(CHUNK * i, CHUNK)
+        rows = pl.ds(FIRST * i, FIRST)
         field_ref[rows, :] = middle
-        sum_ref[rows, :] = neighbours(wide, ring)
+        sum_ref[rows, :] = neighbours(wide, ring, FIRST)
 
 
 def gather(messages, ring):

time: 149 us -> 149 us (level)
  no operation moved by 1% of the time
where the time goes in v8:
time: 149 us; the launch traced here: 148 us
  blocking collectives  103 us (69%)
  Pallas kernels  30.4 us (20%)
  starting transfers between devices  7.22 us (5%)
  waiting for transfers between devices  6.37 us (4%)
    all_to_all x4, blocking collectives, exchange(): return lax.all_to_all(a, axes, 0, 0, tiled=True)  103 us
    pallas_call x1, Pallas kernels, inverse_root(): pl.pallas_call(root_kernel, in_specs=[SCALARS, VECTORS, VECTORS], out_sha...  12 us
    pallas_call x1, Pallas kernels, chebyshev(): pl.pallas_call(filter_kernel, in_specs=[smem] + [vmem] * 5, out_shape=jax...  6.17 us
    ppermute x3, starting transfers between devices, body(): lax.ppermute(share, ('zh', 'zl'), [(i, (i + k) % 4) for i in range(4)])  4.66 us
    ppermute x7, waiting for transfers between devices, swap(): return lax.ppermute(a, axis, [(0, 1), (1, 0)])  4.61 us
    pallas_call x2, Pallas kernels, put(): pl.pallas_call(functools.partial(place_kernel, jobs), in_specs=[SCALARS]...  3.07 us
    pallas_call x1, Pallas kernels, spread(): pl.pallas_call(spread_kernel, in_specs=[pl.BlockSpec(memory_space=pl.ANY)...  3 us
  transfers between devices with their start and end apart: 10, of which 7 were waited for; matrix products, arithmetic and copies ran while one was open for 0% of the time, Pallas kernels for 13%

profile of v8, /device:TPU:0, one launch (start us, length us, event | category | flops | bytes accessed | tf_op | source)
XLA Modules:
  0.0 147.5 jit_solution(926741394449724013)
XLA Ops:
  0.0 0.1 pad_add_fusion.place_ref
  0.1 3.0 %spread.1 = f32[16,2,144,128]{3,2,1,0:T(8,128)} custom-call(f32[8,512,128]{2,1,0:T(8,128)} %bitcast.15, f32[8,16,32]{2,1,0:T(8,128)} %pot_hbm.1), custom_call_target="tpu_custom_call" | custom-call | tf_op jit(solution)/shard_map/spread/pallas_call | solution.py:127
  3.1 0.0 copy-start
  3.1 44.1 %all_to_all.35.in_ref = f32[32,144,128]{2,1,0:T(8,128)S(1)} all-to-all(f32[32,144,128]{2,1,0:T(8,128)} %bitcast.14), channel_id=1, replica_groups=mesh['x'=4,'zh'=2,'y'=4,'zl'=2,'c'=2] {'x','zh','y'}, dimensions={0} | all-to-all | bytes 4718592 | tf_op jit(solution)/shard_map/all_to_all | solution.py:511
  47.3 0.1 collective-permute-start
  47.4 0.0 copy-done
  47.4 1.5 %gather.1 = (f32[1024,512]{1,0:T(8,128)S(1)}, f32[1024,512]{1,0:T(8,128)S(1)}) custom-call(f32[32,144,128]{2,1,0:T(8,128)S(1)} %all_to_all.35.in_ref, bf16[1024,512]{1,0:T(8,128)(2,1)S(1)} %copy-done), custom_call_target="tpu_custom_call" | custom-call | tf_op jit(solution)/shard_map/gather/pallas_call | solution.py:203
  48.9 0.0 collective-permute-done.other_ref
  48.9 6.2 %chebyshev.1 = f32[1024,512]{1,0:T(8,128)S(1)} custom-call(s32[2]{0:T(128)S(1)} %pad_add_fusion.place_ref, f32[1024,512]{1,0:T(8,128)S(1)} %get-tuple-element.24.field_ref, f32[1024,512]{1,0:T(8,128)S(1)} %get-tuple-element.25.sum_ref, f32[32,16,128]{2,1,0:T(8,128)S(1)} %slice.4.mine_ref, f32[32,16,128]{2,1,0:T(8,128)S(1)} %collective-permute-done.other_ref, ...), custom_call_target="tpu_custom_call" | custom-call | tf_op jit(solution)/shard_map/chebyshev/pallas_call | solution.py:296
  55.1 34.1 %all_to_all.36 = f32[128,8,512]{2,1,0:T(8,128)S(1)} all-to-all(f32[128,8,512]{2,1,0:T(8,128)S(1)} %bitcast.11), channel_id=1, replica_groups=mesh['x'=4,'zh'=2,'y'=4,'zl'=2,'c'=2] {'x','zh','y','zl','c'}, dimensions={0} | all-to-all | bytes 4194304 | tf_op jit(solution)/shard_map/all_to_all | solution.py:511
  89.2 0.6 turn.1
  89.8 0.9 collective-permute-start.2
  90.7 2.0 %gram.1 = (f32[640,128]{1,0:T(8,128)S(1)}, f32[640,128]{1,0:T(8,128)S(1)}) custom-call(s32[2]{0:T(128)S(1)} %pad_add_fusion.place_ref, f32[352,512]{1,0:T(8,128)S(1)} %get-tuple-element.26.near_ref.refs_0_, f32[672,512]{1,0:T(8,128)S(1)} %get-tuple-element.32.far_ref.refs_1_, bf16[512,1024]{1,0:T(8,128)(2,1)S(1)} %get-tuple-element.28.left_ref), custom_call_target="tpu_custom_call" | custom-call | tf_op jit(solution)/shard_map/gram/pallas_call | solution.py:367
  92.7 0.1 collective-permute-start.1
  92.8 1.6 %collective-permute-done.1 = f32[640,128]{1,0:T(8,128)S(1)} collective-permute-done((f32[640,128]{1,0:T(8,128)S(1)}, f32[640,128]{1,0:T(8,128)S(1)}, u32[]{:S(2)}, u32[]{:S(2)}) %collective-permute-start.1) | collective-permute-done | bytes 327712 | tf_op jit(solution)/shard_map/ppermute | solution.py:515
  94.4 12.5 %all_to_all.37 = f32[16,40,128]{2,1,0:T(8,128)S(1)} all-to-all(f32[16,40,128]{2,1,0:T(8,128)S(1)} %bitcast.16), channel_id=1, replica_groups=mesh['x'=4,'zh'=2,'y'=4,'zl'=2,'c'=2] {'x','y'}, dimensions={0} | all-to-all | bytes 655360 | tf_op jit(solution)/shard_map/all_to_all | solution.py:511
  107.0 0.1 collective-permute-done.2.refs_2_
  107.1 1.4 collective-permute-start.3
  108.5 0.4 collective-permute-start.4
  108.9 2.8 %collective-permute-start.5 = (f32[40,128]{1,0:T(8,128)S(1)}, f32[40,128]{1,0:T(8,128)S(1)}, u32[]{:S(2)}, u32[]{:S(2)}) collective-permute-start(f32[40,128]{1,0:T(8,128)S(1)} %reduce_sum.9), channel_id=1, source_target_pairs={{0,18},{2,0},{16,2},{18,16},{1,19},{3,1},{17,3},{19,17},{4,22},{6,... | collective-permute-start | bytes 61448 | tf_op jit(solution)/shard_map/ppermute | solution.py:536
  111.8 0.6 collective-permute-done.3
  112.4 1.1 collective-permute-done.4
  113.5 0.0 collective-permute-done.5
  113.5 1.2 collective-permute-start.6
  114.8 12.3 %all_to_all.38 = f32[16,40,128]{2,1,0:T(8,128)S(1)} all-to-all(f32[16,40,128]{2,1,0:T(8,128)S(1)} %tile.2), channel_id=1, replica_groups=mesh['x'=4,'zh'=2,'y'=4,'zl'=2,'c'=2] {'x','y'}, dimensions={0} | all-to-all | bytes 655360 | tf_op jit(solution)/shard_map/all_to_all | solution.py:511
  127.1 0.0 collective-permute-start.7
  127.1 1.6 %collective-permute-done.7.other_ref = f32[640,128]{1,0:T(8,128)S(1)} collective-permute-done((f32[640,128]{1,0:T(8,128)S(1)}, f32[640,128]{1,0:T(8,128)S(1)}, u32[]{:S(2)}, u32[]{:S(2)}) %collective-permute-start.7) | collective-permute-done | bytes 327712 | tf_op jit(solution)/shard_map/ppermute | solution.py:515
  128.7 12.0 %inverse_root.1.refs_1_.refs_3_ = bf16[2,512,256]{2,1,0:T(8,128)(2,1)S(1)} custom-call(s32[2]{0:T(128)S(1)} %pad_add_fusion.place_ref, f32[640,128]{1,0:T(8,128)S(1)} %bitcast.13, f32[640,128]{1,0:T(8,128)S(1)} %collective-permute-done.7.other_ref), custom_call_target="tpu_custom_call" | custom-call | tf_op jit(solution)/shard_map/inverse_root/pallas_call | solution.py:443
  140.7 1.3 whiten.3
  142.0 0.2 collective-permute-start.9
  142.2 0.6 collective-permute-done.6.refs_0_
  142.9 0.7 whiten.2
  143.6 0.1 collective-permute-start.8
  143.7 0.6 collective-permute-done.9.refs_2_
  144.3 1.8 %put.2.refs_1_ = f32[2,2,1024,128]{3,2,1,0:T(8,128)} custom-call(s32[2]{0:T(128)S(1)} %pad_add_fusion.place_ref, f32[1376,128]{1,0:T(8,128)S(1)} %get-tuple-element.36.refs_0_, f32[672,128]{1,0:T(8,128)S(1)} %get-tuple-element.37.refs_1_, f32[1376,128]{1,0:T(8,128)S(1)} %collective-permute-done.9.refs_2_), custom_call_target="tpu_custom_call" | custom-call | tf_op jit(solution)/shard_map/put/pallas_call | solution.py:498
  146.1 0.0 collective-permute-done.8.refs_0_
  146.1 1.3 put.3
  (5 shorter events, 0.1 us)
Async XLA Ops:
  3.1 44.3 %copy-start = (bf16[1024,512]{1,0:T(8,128)(2,1)S(1)}, bf16[1024,512]{1,0:T(8,128)(2,1)}, u32[]{:S(2)}) copy-start(bf16[1024,512]{1,0:T(8,128)(2,1)} %constant.10.clone.ring_ref) | copy-start | bytes 3145732
  47.3 1.6 %collective-permute-start = (f32[32,16,128]{2,1,0:T(8,128)S(1)}, f32[32,16,128]{2,1,0:T(8,128)S(1)}, u32[]{:S(2)}, u32[]{:S(2)}) collective-permute-start(f32[32,16,128]{2,1,0:T(8,128)S(1)} %slice.4.mine_ref), channel_id=1, source_target_pairs={{0,1},{1,0},{2,3},{3,2},{4,5},{5,4},{6,7},{7,6},{8,9},{9,8},{10,11... | collective-permute-start | bytes 786440 | tf_op jit(solution)/shard_map/ppermute | solution.py:515
  89.8 17.3 %collective-permute-start.2 = (f32[352,512]{1,0:T(8,128)S(1)}, f32[352,512]{1,0:T(8,128)S(1)}, u32[]{:S(2)}, u32[]{:S(2)}) collective-permute-start(f32[352,512]{1,0:T(8,128)S(1)} %get-tuple-element.26.near_ref.refs_0_), channel_id=1, source_target_pairs={{0,2},{2,0},{1,3},{3,1},{4,6},{6,4},{5,7},{7,5},{8,10},{10,8},{9,1... | collective-permute-start | bytes 2162696 | tf_op jit(solution)/shard_map/ppermute | solution.py:515
  92.7 1.7 %collective-permute-start.1 = (f32[640,128]{1,0:T(8,128)S(1)}, f32[640,128]{1,0:T(8,128)S(1)}, u32[]{:S(2)}, u32[]{:S(2)}) collective-permute-start(f32[640,128]{1,0:T(8,128)S(1)} %get-tuple-element.30), channel_id=1, source_target_pairs={{0,1},{1,0},{2,3},{3,2},{4,5},{5,4},{6,7},{7,6},{8,9},{9,8},{10,11... | collective-permute-start | bytes 983048 | tf_op jit(solution)/shard_map/ppermute | solution.py:515
  107.1 5.3 %collective-permute-start.3 = (f32[40,128]{1,0:T(8,128)S(1)}, f32[40,128]{1,0:T(8,128)S(1)}, u32[]{:S(2)}, u32[]{:S(2)}) collective-permute-start(f32[40,128]{1,0:T(8,128)S(1)} %reduce_sum.9), channel_id=1, source_target_pairs={{0,16},{2,18},{16,0},{18,2},{1,17},{3,19},{17,1},{19,3},{4,20},{6,... | collective-permute-start | bytes 61448 | tf_op jit(solution)/shard_map/ppermute | solution.py:536
  108.5 5.0 %collective-permute-start.4 = (f32[40,128]{1,0:T(8,128)S(1)}, f32[40,128]{1,0:T(8,128)S(1)}, u32[]{:S(2)}, u32[]{:S(2)}) collective-permute-start(f32[40,128]{1,0:T(8,128)S(1)} %reduce_sum.9), channel_id=1, source_target_pairs={{0,2},{2,16},{16,18},{18,0},{1,3},{3,17},{17,19},{19,1},{4,6},{6,2... | collective-permute-start | bytes 61448 | tf_op jit(solution)/shard_map/ppermute | solution.py:536
  108.9 4.6 %collective-permute-start.5 = (f32[40,128]{1,0:T(8,128)S(1)}, f32[40,128]{1,0:T(8,128)S(1)}, u32[]{:S(2)}, u32[]{:S(2)}) collective-permute-start(f32[40,128]{1,0:T(8,128)S(1)} %reduce_sum.9), channel_id=1, source_target_pairs={{0,18},{2,0},{16,2},{18,16},{1,19},{3,1},{17,3},{19,17},{4,22},{6,... | collective-permute-start | bytes 61448 | tf_op jit(solution)/shard_map/ppermute | solution.py:536
  113.5 29.4 %collective-permute-start.6 = (f32[672,512]{1,0:T(8,128)S(1)}, f32[672,512]{1,0:T(8,128)S(1)}, u32[]{:S(2)}, u32[]{:S(2)}) collective-permute-start(f32[672,512]{1,0:T(8,128)S(1)} %get-tuple-element.32.far_ref.refs_1_), channel_id=1, source_target_pairs={{0,2},{2,0},{1,3},{3,1},{4,6},{6,4},{5,7},{7,5},{8,10},{10,8},{9,1... | collective-permute-start | bytes 4128776 | tf_op jit(solution)/shard_map/ppermute | solution.py:515
  127.1 1.6 %collective-permute-start.7 = (f32[640,128]{1,0:T(8,128)S(1)}, f32[640,128]{1,0:T(8,128)S(1)}, u32[]{:S(2)}, u32[]{:S(2)}) collective-permute-start(f32[640,128]{1,0:T(8,128)S(1)} %bitcast.12), channel_id=1, source_target_pairs={{0,1},{1,0},{2,3},{3,2},{4,5},{5,4},{6,7},{7,6},{8,9},{9,8},{10,11... | collective-permute-start | bytes 983048 | tf_op jit(solution)/shard_map/ppermute | solution.py:515
  142.0 2.2 %collective-permute-start.9 = (f32[1376,128]{1,0:T(8,128)S(1)}, f32[1376,128]{1,0:T(8,128)S(1)}, u32[]{:S(2)}, u32[]{:S(2)}) collective-permute-start(f32[1376,128]{1,0:T(8,128)S(1)} %get-tuple-element.38), channel_id=1, source_target_pairs={{0,1},{1,0},{2,3},{3,2},{4,5},{5,4},{6,7},{7,6},{8,9},{9,8},{10,11... | collective-permute-start | bytes 2113544 | tf_op jit(solution)/shard_map/ppermute | solution.py:515
  143.6 2.5 %collective-permute-start.8 = (f32[672,128]{1,0:T(8,128)S(1)}, f32[672,128]{1,0:T(8,128)S(1)}, u32[]{:S(2)}, u32[]{:S(2)}) collective-permute-start(f32[672,128]{1,0:T(8,128)S(1)} %get-tuple-element.34), channel_id=1, source_target_pairs={{0,1},{1,0},{2,3},{3,2},{4,5},{5,4},{6,7},{7,6},{8,9},{9,8},{10,11... | collective-permute-start | bytes 1032200 | tf_op jit(solution)/shard_map/ppermute | solution.py:515

commit v9 on v6

--- a/solution.py
+++ b/solution.py
@@ -163,9 +163,12 @@
     )
 
 
-def neighbours(wide, ring):
-    near = dot(jnp.concatenate(split(wide[EDGE : EDGE + CHUNK]), axis=1), ring)
-    return near + beside(wide, CHUNK)
+def neighbours(wide, ring, count):
+    near = dot(jnp.concatenate(split(wide[EDGE : EDGE + count]), axis=1), ring)
+    return near + beside(wide, count)
+
+
+FIRST = 256
 
 
 def gather_kernel(in_ref, ring_ref, field_ref, sum_ref):
@@ -176,9 +179,9 @@
         )
 
     ring = ring_ref[...]
-    for i in range(CHUNKS):
-        before, after = (PARTS * i - 1) % 32, PARTS * (i + 1) % 32
-        middle = planes(slice(PARTS * i, PARTS * (i + 1)), 0, 4)
+    for i in range(ROWS // FIRST):
+        before, after = ((FIRST // 32) * i - 1) % 32, (FIRST // 32) * (i + 1) % 32
+        middle = planes(slice((FIRST // 32) * i, (FIRST // 32) * (i + 1)), 0, 4)
         wide = jnp.concatenate(
             [
                 planes(slice(before, before + 1), 2, 2),
@@ -187,9 +190,9 @@
             ],
             axis=0,
         )
-        rows = pl.ds(CHUNK * i, CHUNK)
+        rows = pl.ds(FIRST * i, FIRST)
         field_ref[rows, :] = middle
-        sum_ref[rows, :] = neighbours(wide, ring)
+        sum_ref[rows, :] = neighbours(wide, ring, FIRST)
 
 
 def gather(messages, ring):

time: 149 us -> 149 us (level)
  no operation moved by 1% of the time
where the time goes in v9:
time: 149 us; the launch traced here: 147 us
  blocking collectives  103 us (69%)
  Pallas kernels  30.3 us (20%)
  starting transfers between devices  7.22 us (5%)
  waiting for transfers between devices  6.37 us (4%)
    all_to_all x4, blocking collectives, exchange(): return lax.all_to_all(a, axes, 0, 0, tiled=True)  103 us
    pallas_call x1, Pallas kernels, inverse_root(): pl.pallas_call(root_kernel, in_specs=[SCALARS, VECTORS, VECTORS], out_sha...  12 us
    pallas_call x1, Pallas kernels, chebyshev(): pl.pallas_call(filter_kernel, in_specs=[smem] + [vmem] * 5, out_shape=jax...  6.2 us
    ppermute x3, starting transfers between devices, body(): lax.ppermute(share, ('zh', 'zl'), [(i, (i + k) % 4) for i in range(4)])  4.66 us
    ppermute x7, waiting for transfers between devices, swap(): return lax.ppermute(a, axis, [(0, 1), (1, 0)])  4.61 us
    pallas_call x2, Pallas kernels, put(): pl.pallas_call(functools.partial(place_kernel, jobs), in_specs=[SCALARS]...  3.07 us
  transfers between devices with their start and end apart: 10, of which 7 were waited for; matrix products, arithmetic and copies ran while one was open for 0% of the time, Pallas kernels for 13%

profile of v9, /device:TPU:0, one launch (start us, length us, event | category | flops | bytes accessed | tf_op | source)
XLA Modules:
  0.0 147.4 jit_solution(14826144145350282526)
XLA Ops:
  0.0 0.1 pad_add_fusion.place_ref
  0.1 2.9 %spread.1 = f32[16,2,144,128]{3,2,1,0:T(8,128)} custom-call(f32[8,512,128]{2,1,0:T(8,128)} %bitcast.15, f32[8,16,32]{2,1,0:T(8,128)} %pot_hbm.1), custom_call_target="tpu_custom_call" | custom-call | tf_op jit(solution)/shard_map/spread/pallas_call | solution.py:123
  2.9 0.0 copy-start
  3.0 44.1 %all_to_all.35.in_ref = f32[32,144,128]{2,1,0:T(8,128)S(1)} all-to-all(f32[32,144,128]{2,1,0:T(8,128)} %bitcast.14), channel_id=1, replica_groups=mesh['x'=4,'zh'=2,'y'=4,'zl'=2,'c'=2] {'x','zh','y'}, dimensions={0} | all-to-all | bytes 4718592 | tf_op jit(solution)/shard_map/all_to_all | solution.py:507
  47.1 0.1 collective-permute-start
  47.2 0.0 copy-done
  47.2 1.5 %gather.1 = (f32[1024,512]{1,0:T(8,128)S(1)}, f32[1024,512]{1,0:T(8,128)S(1)}) custom-call(f32[32,144,128]{2,1,0:T(8,128)S(1)} %all_to_all.35.in_ref, bf16[1024,512]{1,0:T(8,128)(2,1)S(1)} %copy-done), custom_call_target="tpu_custom_call" | custom-call | tf_op jit(solution)/shard_map/gather/pallas_call | solution.py:199
  48.8 0.0 collective-permute-done.other_ref
  48.8 6.2 %chebyshev.1 = f32[1024,512]{1,0:T(8,128)S(1)} custom-call(s32[2]{0:T(128)S(1)} %pad_add_fusion.place_ref, f32[1024,512]{1,0:T(8,128)S(1)} %get-tuple-element.24.field_ref, f32[1024,512]{1,0:T(8,128)S(1)} %get-tuple-element.25.sum_ref, f32[32,16,128]{2,1,0:T(8,128)S(1)} %slice.4.mine_ref, f32[32,16,128]{2,1,0:T(8,128)S(1)} %collective-permute-done.other_ref, ...), custom_call_target="tpu_custom_call" | custom-call | tf_op jit(solution)/shard_map/chebyshev/pallas_call | solution.py:292
  55.0 34.0 %all_to_all.36 = f32[128,8,512]{2,1,0:T(8,128)S(1)} all-to-all(f32[128,8,512]{2,1,0:T(8,128)S(1)} %bitcast.11), channel_id=1, replica_groups=mesh['x'=4,'zh'=2,'y'=4,'zl'=2,'c'=2] {'x','zh','y','zl','c'}, dimensions={0} | all-to-all | bytes 4194304 | tf_op jit(solution)/shard_map/all_to_all | solution.py:507
  89.0 0.6 turn.1
  89.7 0.9 collective-permute-start.2
  90.5 2.0 %gram.1 = (f32[640,128]{1,0:T(8,128)S(1)}, f32[640,128]{1,0:T(8,128)S(1)}) custom-call(s32[2]{0:T(128)S(1)} %pad_add_fusion.place_ref, f32[352,512]{1,0:T(8,128)S(1)} %get-tuple-element.26.near_ref.refs_0_, f32[672,512]{1,0:T(8,128)S(1)} %get-tuple-element.32.far_ref.refs_1_, bf16[512,1024]{1,0:T(8,128)(2,1)S(1)} %get-tuple-element.28.left_ref), custom_call_target="tpu_custom_call" | custom-call | tf_op jit(solution)/shard_map/gram/pallas_call | solution.py:363
  92.5 0.1 collective-permute-start.1
  92.6 1.6 %collective-permute-done.1 = f32[640,128]{1,0:T(8,128)S(1)} collective-permute-done((f32[640,128]{1,0:T(8,128)S(1)}, f32[640,128]{1,0:T(8,128)S(1)}, u32[]{:S(2)}, u32[]{:S(2)}) %collective-permute-start.1) | collective-permute-done | bytes 327712 | tf_op jit(solution)/shard_map/ppermute | solution.py:511
  94.3 12.5 %all_to_all.37 = f32[16,40,128]{2,1,0:T(8,128)S(1)} all-to-all(f32[16,40,128]{2,1,0:T(8,128)S(1)} %bitcast.16), channel_id=1, replica_groups=mesh['x'=4,'zh'=2,'y'=4,'zl'=2,'c'=2] {'x','y'}, dimensions={0} | all-to-all | bytes 655360 | tf_op jit(solution)/shard_map/all_to_all | solution.py:507
  106.8 0.1 collective-permute-done.2.refs_2_
  106.9 1.4 collective-permute-start.3
  108.4 0.4 collective-permute-start.4
  108.8 2.8 %collective-permute-start.5 = (f32[40,128]{1,0:T(8,128)S(1)}, f32[40,128]{1,0:T(8,128)S(1)}, u32[]{:S(2)}, u32[]{:S(2)}) collective-permute-start(f32[40,128]{1,0:T(8,128)S(1)} %reduce_sum.9), channel_id=1, source_target_pairs={{0,18},{2,0},{16,2},{18,16},{1,19},{3,1},{17,3},{19,17},{4,22},{6,... | collective-permute-start | bytes 61448 | tf_op jit(solution)/shard_map/ppermute | solution.py:532
  111.6 0.6 collective-permute-done.3
  112.2 1.1 collective-permute-done.4
  113.4 0.0 collective-permute-done.5
  113.4 1.2 collective-permute-start.6
  114.6 12.3 %all_to_all.38 = f32[16,40,128]{2,1,0:T(8,128)S(1)} all-to-all(f32[16,40,128]{2,1,0:T(8,128)S(1)} %tile.2), channel_id=1, replica_groups=mesh['x'=4,'zh'=2,'y'=4,'zl'=2,'c'=2] {'x','y'}, dimensions={0} | all-to-all | bytes 655360 | tf_op jit(solution)/shard_map/all_to_all | solution.py:507
  126.9 0.0 collective-permute-start.7
  126.9 1.6 %collective-permute-done.7.other_ref = f32[640,128]{1,0:T(8,128)S(1)} collective-permute-done((f32[640,128]{1,0:T(8,128)S(1)}, f32[640,128]{1,0:T(8,128)S(1)}, u32[]{:S(2)}, u32[]{:S(2)}) %collective-permute-start.7) | collective-permute-done | bytes 327712 | tf_op jit(solution)/shard_map/ppermute | solution.py:511
  128.6 12.0 %inverse_root.1.refs_1_.refs_3_ = bf16[2,512,256]{2,1,0:T(8,128)(2,1)S(1)} custom-call(s32[2]{0:T(128)S(1)} %pad_add_fusion.place_ref, f32[640,128]{1,0:T(8,128)S(1)} %bitcast.13, f32[640,128]{1,0:T(8,128)S(1)} %collective-permute-done.7.other_ref), custom_call_target="tpu_custom_call" | custom-call | tf_op jit(solution)/shard_map/inverse_root/pallas_call | solution.py:439
  140.6 1.3 whiten.3
  141.9 0.2 collective-permute-start.9
  142.1 0.6 collective-permute-done.6.refs_0_
  142.7 0.7 whiten.2
  143.5 0.1 collective-permute-start.8
  143.5 0.6 collective-permute-done.9.refs_2_
  144.1 1.8 %put.2.refs_1_ = f32[2,2,1024,128]{3,2,1,0:T(8,128)} custom-call(s32[2]{0:T(128)S(1)} %pad_add_fusion.place_ref, f32[1376,128]{1,0:T(8,128)S(1)} %get-tuple-element.36.refs_0_, f32[672,128]{1,0:T(8,128)S(1)} %get-tuple-element.37.refs_1_, f32[1376,128]{1,0:T(8,128)S(1)} %collective-permute-done.9.refs_2_), custom_call_target="tpu_custom_call" | custom-call | tf_op jit(solution)/shard_map/put/pallas_call | solution.py:494
  145.9 0.0 collective-permute-done.8.refs_0_
  145.9 1.3 put.3
  (5 shorter events, 0.1 us)
Async XLA Ops:
  2.9 44.3 %copy-start = (bf16[1024,512]{1,0:T(8,128)(2,1)S(1)}, bf16[1024,512]{1,0:T(8,128)(2,1)}, u32[]{:S(2)}) copy-start(bf16[1024,512]{1,0:T(8,128)(2,1)} %constant.10.clone.ring_ref) | copy-start | bytes 3145732
  47.1 1.6 %collective-permute-start = (f32[32,16,128]{2,1,0:T(8,128)S(1)}, f32[32,16,128]{2,1,0:T(8,128)S(1)}, u32[]{:S(2)}, u32[]{:S(2)}) collective-permute-start(f32[32,16,128]{2,1,0:T(8,128)S(1)} %slice.4.mine_ref), channel_id=1, source_target_pairs={{0,1},{1,0},{2,3},{3,2},{4,5},{5,4},{6,7},{7,6},{8,9},{9,8},{10,11... | collective-permute-start | bytes 786440 | tf_op jit(solution)/shard_map/ppermute | solution.py:511
  89.7 17.3 %collective-permute-start.2 = (f32[352,512]{1,0:T(8,128)S(1)}, f32[352,512]{1,0:T(8,128)S(1)}, u32[]{:S(2)}, u32[]{:S(2)}) collective-permute-start(f32[352,512]{1,0:T(8,128)S(1)} %get-tuple-element.26.near_ref.refs_0_), channel_id=1, source_target_pairs={{0,2},{2,0},{1,3},{3,1},{4,6},{6,4},{5,7},{7,5},{8,10},{10,8},{9,1... | collective-permute-start | bytes 2162696 | tf_op jit(solution)/shard_map/ppermute | solution.py:511
  92.5 1.7 %collective-permute-start.1 = (f32[640,128]{1,0:T(8,128)S(1)}, f32[640,128]{1,0:T(8,128)S(1)}, u32[]{:S(2)}, u32[]{:S(2)}) collective-permute-start(f32[640,128]{1,0:T(8,128)S(1)} %get-tuple-element.30), channel_id=1, source_target_pairs={{0,1},{1,0},{2,3},{3,2},{4,5},{5,4},{6,7},{7,6},{8,9},{9,8},{10,11... | collective-permute-start | bytes 983048 | tf_op jit(solution)/shard_map/ppermute | solution.py:511
  106.9 5.3 %collective-permute-start.3 = (f32[40,128]{1,0:T(8,128)S(1)}, f32[40,128]{1,0:T(8,128)S(1)}, u32[]{:S(2)}, u32[]{:S(2)}) collective-permute-start(f32[40,128]{1,0:T(8,128)S(1)} %reduce_sum.9), channel_id=1, source_target_pairs={{0,16},{2,18},{16,0},{18,2},{1,17},{3,19},{17,1},{19,3},{4,20},{6,... | collective-permute-start | bytes 61448 | tf_op jit(solution)/shard_map/ppermute | solution.py:532
  108.4 5.0 %collective-permute-start.4 = (f32[40,128]{1,0:T(8,128)S(1)}, f32[40,128]{1,0:T(8,128)S(1)}, u32[]{:S(2)}, u32[]{:S(2)}) collective-permute-start(f32[40,128]{1,0:T(8,128)S(1)} %reduce_sum.9), channel_id=1, source_target_pairs={{0,2},{2,16},{16,18},{18,0},{1,3},{3,17},{17,19},{19,1},{4,6},{6,2... | collective-permute-start | bytes 61448 | tf_op jit(solution)/shard_map/ppermute | solution.py:532
  108.8 4.6 %collective-permute-start.5 = (f32[40,128]{1,0:T(8,128)S(1)}, f32[40,128]{1,0:T(8,128)S(1)}, u32[]{:S(2)}, u32[]{:S(2)}) collective-permute-start(f32[40,128]{1,0:T(8,128)S(1)} %reduce_sum.9), channel_id=1, source_target_pairs={{0,18},{2,0},{16,2},{18,16},{1,19},{3,1},{17,3},{19,17},{4,22},{6,... | collective-permute-start | bytes 61448 | tf_op jit(solution)/shard_map/ppermute | solution.py:532
  113.4 29.4 %collective-permute-start.6 = (f32[672,512]{1,0:T(8,128)S(1)}, f32[672,512]{1,0:T(8,128)S(1)}, u32[]{:S(2)}, u32[]{:S(2)}) collective-permute-start(f32[672,512]{1,0:T(8,128)S(1)} %get-tuple-element.32.far_ref.refs_1_), channel_id=1, source_target_pairs={{0,2},{2,0},{1,3},{3,1},{4,6},{6,4},{5,7},{7,5},{8,10},{10,8},{9,1... | collective-permute-start | bytes 4128776 | tf_op jit(solution)/shard_map/ppermute | solution.py:511
  126.9 1.6 %collective-permute-start.7 = (f32[640,128]{1,0:T(8,128)S(1)}, f32[640,128]{1,0:T(8,128)S(1)}, u32[]{:S(2)}, u32[]{:S(2)}) collective-permute-start(f32[640,128]{1,0:T(8,128)S(1)} %bitcast.12), channel_id=1, source_target_pairs={{0,1},{1,0},{2,3},{3,2},{4,5},{5,4},{6,7},{7,6},{8,9},{9,8},{10,11... | collective-permute-start | bytes 983048 | tf_op jit(solution)/shard_map/ppermute | solution.py:511
  141.9 2.2 %collective-permute-start.9 = (f32[1376,128]{1,0:T(8,128)S(1)}, f32[1376,128]{1,0:T(8,128)S(1)}, u32[]{:S(2)}, u32[]{:S(2)}) collective-permute-start(f32[1376,128]{1,0:T(8,128)S(1)} %get-tuple-element.38), channel_id=1, source_target_pairs={{0,1},{1,0},{2,3},{3,2},{4,5},{5,4},{6,7},{7,6},{8,9},{9,8},{10,11... | collective-permute-start | bytes 2113544 | tf_op jit(solution)/shard_map/ppermute | solution.py:511
  143.5 2.5 %collective-permute-start.8 = (f32[672,128]{1,0:T(8,128)S(1)}, f32[672,128]{1,0:T(8,128)S(1)}, u32[]{:S(2)}, u32[]{:S(2)}) collective-permute-start(f32[672,128]{1,0:T(8,128)S(1)} %get-tuple-element.34), channel_id=1, source_target_pairs={{0,1},{1,0},{2,3},{3,2},{4,5},{5,4},{6,7},{7,6},{8,9},{9,8},{10,11... | collective-permute-start | bytes 1032200 | tf_op jit(solution)/shard_map/ppermute | solution.py:511
